TPU v7x, 32 devices: a whole 2x2x4 slice. The times are simulated.
32 devices in a mesh: grp: 2 (over y), node: 16 (over z, x, core).
Axes of the slice: x: 2, y: 2, z: 4, core: 2. Of those that a mesh axis runs over, the one named last changes fastest.
Arguments:
- tokens: bfloat16 [128, 7168], P(('grp', 'node')), parts along dimension 0, may hold values from -6 to 6
- routes: int32 [128, 2], P(('grp', 'node')), parts along dimension 0, may hold values from 0 to 3, all different within a row; in each aligned block of 4 rows (0 to 3, 4 to 7, ...) at most 4 rows name the same one
- gates: float32 [128, 2], P(('grp', 'node')), parts along dimension 0, may hold values from 0.05 to 1
- norm_gain: bfloat16 [7168], replicated, may hold values from 0.5 to 1.5
- w_gate: bfloat16 [16, 7168, 256], P('node'), may hold values from -0.0625 to 0.0625
- w_up: bfloat16 [16, 7168, 256], P('node'), may hold values from -0.0625 to 0.0625
- w_down: bfloat16 [16, 256, 7168], P('node'), may hold values from -0.1875 to 0.1875
- queries: bfloat16 [32, 128, 576], P(('grp', 'node')), parts along dimension 0, may hold values from -60 to 60
- cache: bfloat16 [32, 1280, 576], P(('grp', 'node')), parts along dimension 0, may hold values from -6 to 6
- lengths: int32 [32], P(('grp', 'node')), parts along dimension 0, may hold values from 1 to 1280, as said below
Outputs:
- moe_out: bfloat16 [128, 7168], P(('grp', 'node')), parts along dimension 0
- attention_out: bfloat16 [32, 65536], P(('grp', 'node')), parts along dimension 0
There are 2 independent parts, one for each index of `grp`. A program takes and returns all parts, laid end to end along the dimension named above; an argument that names none is the same for every part. Nothing has to cross between parts.
Inputs may be any that keep to these rules, and one draw needn't show every extreme that they name: `routes`: each token names 2 different replicas; within the rows of one device no replica is named by more than 4 tokens. `lengths`: some request has all 1280 positions filled.
All inputs are finite; a program needn't handle non-finite values.
Results may differ from a plain program's by a relative error of at most 0.0077.
Values may be sent and summed in bfloat16 or wider, within the bound.
No kernel may reach another device: no remote copies, remote signals or barrier semaphores. Data moves between devices by JAX's collectives and lax.ppermute only.
A program may use at most 128 MiB of HBM per device.

v0:
```python
import jax
import jax.numpy as jnp
from jax import lax
from jax.sharding import PartitionSpec as P

SPLIT = 4
VALUE_DIM = 512


norm_eps = 1e-06
route_scale = 2.5
softmax_scale = 192.0 ** (-0.5)


def per_device(tokens, routes, gates, norm_gain, w_gate, w_up, w_down, queries, cache, lengths):
    row_count = tokens.shape[0]
    pick_count = routes.shape[1]
    width = tokens.shape[1]
    node_count = lax.axis_size("node")
    slot_count = node_count // SPLIT
    capacity = max(2, 2 * row_count * pick_count // slot_count)
    hidden_in = tokens.astype(jnp.float32)
    inverse = lax.rsqrt(jnp.mean(hidden_in * hidden_in, axis=-1, keepdims=True) + norm_eps)
    normed = (hidden_in * inverse * norm_gain.astype(jnp.float32)).astype(jnp.bfloat16)
    mixing = route_scale * gates / jnp.sum(gates, axis=-1, keepdims=True)
    picks_flat = routes.reshape(-1)
    total_picks = row_count * pick_count
    pick_rows = jnp.arange(total_picks, dtype=jnp.int32) // pick_count
    one_hot = (picks_flat[:, None] == jnp.arange(slot_count, dtype=jnp.int32)[None, :]).astype(
        jnp.int32
    )
    rank_in = jnp.sum((jnp.cumsum(one_hot, axis=0) - 1) * one_hot, axis=1)
    placed = picks_flat * capacity + rank_in
    matches = placed[None, :] == jnp.arange(slot_count * capacity, dtype=jnp.int32)[:, None]
    filled = jnp.any(matches, axis=1)
    source_row = jnp.sum(jnp.where(matches, pick_rows[None, :], 0), axis=1)
    slot_rows = jnp.where(filled[:, None], normed[source_row], jnp.zeros((), jnp.bfloat16))
    slot_rows = slot_rows.reshape(slot_count, capacity, width).reshape(
        slot_count, 1, capacity, width
    )
    outgoing = jnp.broadcast_to(slot_rows, (slot_count, SPLIT, capacity, width)).reshape(
        node_count, capacity, width
    )
    arrived = lax.all_to_all(outgoing, "node", split_axis=0, concat_axis=0, tiled=True)
    arrived_shape = arrived.shape
    flat_rows = arrived.reshape(-1, width)
    gate_part = jnp.dot(flat_rows, w_gate[0], preferred_element_type=jnp.float32)
    up_part = jnp.dot(flat_rows, w_up[0], preferred_element_type=jnp.float32)
    hidden = (jax.nn.silu(gate_part) * up_part).astype(jnp.bfloat16)
    result = jnp.dot(hidden, w_down[0], preferred_element_type=jnp.float32).astype(jnp.bfloat16)
    send_result = result.reshape(arrived_shape)
    returned = lax.all_to_all(send_result, "node", split_axis=0, concat_axis=0, tiled=True)
    grouped = returned.reshape(slot_count, SPLIT, capacity, width)
    pieces = grouped[picks_flat, :, rank_in]
    summed = jnp.sum(pieces.astype(jnp.float32), axis=1)
    expert_sum = lax.optimization_barrier(summed.astype(jnp.bfloat16)).astype(jnp.float32)
    expert_sum = expert_sum.reshape(row_count, pick_count, width)
    moe_out = jnp.sum(expert_sum * mixing[:, :, None], axis=1).astype(jnp.bfloat16)
    cache_len = cache.shape[1]
    scores = (
        jnp.einsum("rhc,rjc->rhj", queries, cache, preferred_element_type=jnp.float32)
        * softmax_scale
    )
    valid = jnp.arange(cache_len, dtype=jnp.int32)[None, None, :] < lengths[:, None, None]
    scores = jnp.where(valid, scores, -jnp.inf)
    probs = jax.nn.softmax(scores, axis=-1).astype(jnp.bfloat16)
    attended = jnp.einsum(
        "rhj,rjv->rhv", probs, cache[:, :, :VALUE_DIM], preferred_element_type=jnp.float32
    )
    attention_out = attended.astype(jnp.bfloat16).reshape(queries.shape[0], -1)
    return (moe_out, attention_out)


def solution(mesh):
    in_specs = (
        P(("grp", "node"), None),
        P(("grp", "node"), None),
        P(("grp", "node"), None),
        P(),
        P("node", None, None),
        P("node", None, None),
        P("node", None, None),
        P(("grp", "node"), None, None),
        P(("grp", "node"), None, None),
        P(("grp", "node")),
    )
    out_specs = (P(("grp", "node"), None), P(("grp", "node"), None))
    return jax.shard_map(
        per_device, mesh=mesh, in_specs=in_specs, out_specs=out_specs, check_vma=False
    )
```

profile of v0, /device:TPU:0, one launch (start us, length us, event | category | flops | bytes accessed | tf_op | source)
XLA Modules:
  0.0 73.8 jit_solution(11095684832583081438)
XLA Ops:
  0.6 0.0 copy-start
  0.6 0.8 %copy.25 = s32[4,2]{1,0:T(4,128)S(1)} copy(s32[4,2]{0,1:T(2,128)} %param.11) | data formatting | bytes 64 | tf_op args[1]
  1.4 0.1 reshape.171
  1.5 0.2 reduce_window_sum.11
  1.8 0.1 fusion.37
  1.8 0.1 select_reduce_fusion
  1.9 0.7 convert_element_type.34
  2.7 1.0 %fusion.28 = f32[4]{0:T(128)S(1)} fusion(bf16[4,7168]{1,0:T(4,128)(2,1)} %param.10), kind=kLoop, calls=%fused_computation.28 | loop fusion | flops 86012 | bytes 57360 | tf_op jit(solution)/shard_map/reduce_sum | solution.py:23
  3.7 0.9 %fusion.30 = bf16[4,7168]{1,0:T(4,128)(2,1)S(1)} fusion(bf16[4,7168]{1,0:T(4,128)(2,1)} %param.10, f32[7168]{0:T(1024)S(1)} %convert_element_type.34, f32[4]{0:T(128)S(1)} %add_rsqrt_fusion), kind=kLoop, calls=%fused_computation.30 | loop fusion | flops 114688 | bytes 143376 | tf_op jit(solution)/shard_map/convert_element_type | solution.py:24
  4.6 0.7 gather_fusion
  5.3 0.1 gather.9
  5.4 0.1 broadcast_in_dim.36
  5.5 0.2 broadcast_select_fusion
  5.6 0.2 broadcast_in_dim.64
  5.9 29.7 %all_to_all.10 = bf16[16,4,7168]{2,1,0:T(4,128)(2,1)S(1)} all-to-all(bf16[16,4,7168]{2,1,0:T(4,128)(2,1)S(1)} %bitcast.53), channel_id=1, replica_groups=mesh['grp'=2,'node'=16] {'node'}, dimensions={0} | all-to-all | bytes 1835008 | tf_op jit(solution)/shard_map/all_to_all | solution.py:44
  35.6 0.2 reshape.173
  35.8 2.8 %fusion.3 = f32[64,256]{1,0:T(8,128)S(1)} fusion(bf16[64,7168]{1,0:T(8,128)(2,1)S(1)} %reshape.173, bf16[1,7168,256]{2,1,0:T(8,128)(2,1)} %param.14), kind=kOutput, calls=%fused_computation.6 | convolution fusion | flops 234881024 | bytes 4653056 | tf_op jit(solution)/shard_map/dot_general | solution.py:47
  38.6 5.5 %convolution_convert_fusion = bf16[64,7168]{1,0:T(8,128)(2,1)S(1)} fusion(bf16[1,256,7168]{2,1,0:T(8,128)(2,1)} %param.16, bf16[64,7168]{1,0:T(8,128)(2,1)S(1)} %reshape.173, bf16[1,7168,256]{2,1,0:T(8,128)(2,1)} %param.15, f32[64,256]{1,0:T(8,128)S(1)} %fusion.3), kind=kOutput, calls=%fused_computation.2 | convolution fusion | flops 470319104 | bytes 9240576 | tf_op jit(solution)/shard_map/dot_general | solution.py:50
  44.1 1.3 %reshape.174 = bf16[16,4,7168]{2,1,0:T(4,128)(2,1)} reshape(bf16[64,7168]{1,0:T(8,128)(2,1)S(1)} %convolution_convert_fusion) | data formatting | bytes 1835008 | tf_op jit(solution)/shard_map/reshape | solution.py:51
  45.3 4.5 %all-to-all-start.1 = ((bf16[16,4,7168]{2,1,0:T(4,128)(2,1)}), bf16[16,4,7168]{2,1,0:T(4,128)(2,1)S(1)}, u32[]{:S(2)}, u32[]{:S(2)}) async-start(bf16[16,4,7168]{2,1,0:T(4,128)(2,1)} %reshape.174), calls=%async_computation.1 | async-start | bytes 1835008 | tf_op jit(solution)/shard_map/all_to_all | solution.py:52
  49.8 0.1 reshape.176
  49.9 0.1 copy.28
  50.7 0.5 fusion.47
  51.2 0.3 fusion.24
  51.5 0.6 fusion.13
  52.1 0.9 %copy.31 = bf16[1,1,128,512]{3,1,2,0:T(2,128)(2,1)} copy(bf16[1,1,128,512]{3,2,1,0:T(8,128)(2,1)S(1)} %fusion.13) | data formatting | bytes 262144
  53.0 17.6 %all-to-all-done.1 = bf16[16,4,7168]{2,1,0:T(4,128)(2,1)S(1)} async-done(((bf16[16,4,7168]{2,1,0:T(4,128)(2,1)}), bf16[16,4,7168]{2,1,0:T(4,128)(2,1)S(1)}, u32[]{:S(2)}, u32[]{:S(2)}) %all-to-all-start.1) | async-done | bytes 917536 | tf_op jit(solution)/shard_map/all_to_all | solution.py:52
  70.6 0.5 copy.27
  71.1 0.9 %gather_fusion.1 = bf16[8,4,7168]{2,1,0:T(4,128)(2,1)S(1)} fusion(bf16[4,4,4,7168]{3,1,2,0:T(4,128)(2,1)S(1)} %copy.27, s32[8]{0:T(128)S(1)} %fusion.45), kind=kCustom, calls=%fused_computation.1 | custom fusion | bytes 917568 | tf_op jit(solution)/shard_map/gather | solution.py:54
  72.0 0.6 reduce_sum.75
  72.6 0.2 reshape.184
  72.8 1.0 %multiply_reduce_fusion = bf16[4,7168]{1,0:T(4,128)(2,1)} fusion(f32[4,2,7168]{2,1,0:T(2,128)S(1)} %reshape.184, f32[4,2]{1,0:T(4,128)S(1)} %copy.28), kind=kLoop, calls=%fused_computation.23 | loop fusion | flops 86016 | bytes 286752 | tf_op jit(solution)/shard_map/reduce_sum | solution.py:58
  (15 shorter events, 0.1 us)
Async XLA Ops:
  0.6 50.0 %copy-start = (bf16[1,128,576]{1,2,0:T(8,128)(2,1)S(1)}, bf16[1,128,576]{1,2,0:T(8,128)(2,1)}, u32[]{:S(2)}) copy-start(bf16[1,128,576]{1,2,0:T(8,128)(2,1)} %param.17) | copy-start | bytes 442372
  44.0 5.9 %copy-start.2 = (f32[4,2]{0,1:T(2,128)S(1)}, f32[4,2]{0,1:T(2,128)}, u32[]{:S(2)}) copy-start(f32[4,2]{0,1:T(2,128)} %param.12) | copy-start | bytes 100
  44.0 6.6 %copy-start.1 = (bf16[1,1280,576]{1,2,0:T(8,128)(2,1)S(1)}, bf16[1,1280,576]{1,2,0:T(8,128)(2,1)}, u32[]{:S(2)}) copy-start(bf16[1,1280,576]{1,2,0:T(8,128)(2,1)} %param.18) | copy-start | bytes 4423684
  45.3 25.3 %all-to-all-start.1 = ((bf16[16,4,7168]{2,1,0:T(4,128)(2,1)}), bf16[16,4,7168]{2,1,0:T(4,128)(2,1)S(1)}, u32[]{:S(2)}, u32[]{:S(2)}) async-start(bf16[16,4,7168]{2,1,0:T(4,128)(2,1)} %reshape.174), calls=%async_computation.1 | async-start | bytes 1835008 | tf_op jit(solution)/shard_map/all_to_all | solution.py:52
where the time goes:
time: 74.8 us; the launch traced here: 73.8 us
  blocking collectives  29.7 us (40%)
  waiting for transfers between devices  17.6 us (24%)
  matrix products  9.32 us (12%)
  local copies, waits for them, and re-layouts  6.13 us (8%)
  other arithmetic  5.08 us (7%)
  starting transfers between devices  4.48 us (6%)
  between operations  1.43 us (2%)
    all_to_all x1, blocking collectives, per_device(): lax.all_to_all(outgoing, 'node', split_axis=0, concat_axis=0, tiled=True)  29.7 us
    all_to_all x1, waiting for transfers between devices, per_device(): lax.all_to_all(send_result, 'node', split_axis=0, concat_axis=0, tiled=True)  17.6 us
    dot_general x1, matrix products, per_device(): jnp.dot(hidden, w_down[0], preferred_element_type=jnp.float32)  5.45 us
    all_to_all x1, starting transfers between devices, per_device(): lax.all_to_all(send_result, 'node', split_axis=0, concat_axis=0, tiled=True)  4.48 us
    dot_general x1, matrix products, per_device(): jnp.dot(flat_rows, w_gate[0], preferred_element_type=jnp.float32)  2.75 us
    unnamed x8, local copies, waits for them, and re-layouts  1.73 us
  transfers between devices with their start and end apart: 1, of which 1 were waited for; matrix products, arithmetic and copies ran while one was open for 3% of the time, Pallas kernels for 0%

commit v1 on v0

v1 whole, which is shorter than its diff:
```python
import jax
import jax.numpy as jnp
from jax import lax
from jax.sharding import PartitionSpec as P

SPLIT = 4
VALUE_DIM = 512
LANES = 128


norm_eps = 1e-06
route_scale = 2.5
softmax_scale = 192.0 ** (-0.5)


def exchange_steps(node_count):
    bits = [1 << bit for bit in range(node_count.bit_length() - 1)]
    far, near = bits[3:], bits[1:3]
    steps = [(mask, mask) for mask in reversed(far)]
    steps += [(even, odd) for even, odd in zip(near, reversed(near))]
    return steps + [(1, 1)]


def trade(value, masks, node_count):
    pairs = [(node, node ^ masks[node % 2]) for node in range(node_count)]
    return lax.ppermute(value, "node", pairs)


def attention(queries, cache, lengths):
    cache_len = cache.shape[1]
    scores = (
        jnp.einsum("rhc,rjc->rhj", queries, cache, preferred_element_type=jnp.float32)
        * softmax_scale
    )
    valid = jnp.arange(cache_len, dtype=jnp.int32)[None, None, :] < lengths[:, None, None]
    scores = jnp.where(valid, scores, -jnp.inf)
    probs = jax.nn.softmax(scores, axis=-1).astype(jnp.bfloat16)
    attended = jnp.einsum(
        "rhj,rjv->rhv", probs, cache[:, :, :VALUE_DIM], preferred_element_type=jnp.float32
    )
    return attended.astype(jnp.bfloat16).reshape(queries.shape[0], -1)


def per_device(tokens, routes, gates, norm_gain, w_gate, w_up, w_down, queries, cache, lengths):
    width = tokens.shape[1]
    picks = routes.shape[1]
    node_count = lax.axis_size("node")
    steps = exchange_steps(node_count)

    mixing = route_scale * gates / jnp.sum(gates, axis=-1, keepdims=True)
    high = lax.reduce_precision(mixing, 8, 7)
    notes = jnp.concatenate([routes.astype(jnp.float32), high, mixing - high], axis=1)
    notes = jnp.pad(notes, ((0, 0), (0, -(3 * picks) % LANES))).astype(jnp.bfloat16)
    rows = jnp.concatenate([tokens, notes], axis=1)
    for masks in steps:
        rows = jnp.concatenate([rows, trade(rows, masks, node_count)], axis=0)

    notes = rows[:, width : width + 3 * picks].astype(jnp.float32)
    replica = (lax.axis_index("node") // SPLIT).astype(jnp.float32)
    weight = notes[:, picks : 2 * picks] + notes[:, 2 * picks :]
    share = jnp.sum(jnp.where(notes[:, :picks] == replica, weight, 0.0), axis=1, keepdims=True)

    hidden_in = rows[:, :width].astype(jnp.float32)
    inverse = lax.rsqrt(jnp.mean(hidden_in * hidden_in, axis=-1, keepdims=True) + norm_eps)
    normed = (hidden_in * inverse * norm_gain.astype(jnp.float32)).astype(jnp.bfloat16)
    gate_part = jnp.dot(normed, w_gate[0], preferred_element_type=jnp.float32)
    up_part = jnp.dot(normed, w_up[0], preferred_element_type=jnp.float32)
    hidden = (jax.nn.silu(gate_part) * up_part * share).astype(jnp.bfloat16)
    total = jnp.dot(hidden, w_down[0], preferred_element_type=jnp.float32)

    for masks in reversed(steps):
        half = total.shape[0] // 2
        arrived = trade(total[half:].astype(jnp.bfloat16), masks, node_count)
        total = total[:half] + arrived.astype(jnp.float32)
    moe_out = total.astype(jnp.bfloat16)

    return (moe_out, attention(queries, cache, lengths))


def solution(mesh):
    in_specs = (
        P(("grp", "node"), None),
        P(("grp", "node"), None),
        P(("grp", "node"), None),
        P(),
        P("node", None, None),
        P("node", None, None),
        P("node", None, None),
        P(("grp", "node"), None, None),
        P(("grp", "node"), None, None),
        P(("grp", "node")),
    )
    out_specs = (P(("grp", "node"), None), P(("grp", "node"), None))
    return jax.shard_map(
        per_device, mesh=mesh, in_specs=in_specs, out_specs=out_specs, check_vma=False
    )
```

time: 74.8 us -> 55.2 us (0.74)
  blocking collectives: 29.7 us -> 0 us
  starting transfers between devices: 4.48 us -> 13.2 us
  local copies, waits for them, and re-layouts: 6.13 us -> 1.5 us
  waiting for transfers between devices: 17.6 us -> 21.1 us
  other arithmetic: 5.08 us -> 7.93 us
    all_to_all x1 -> x0, blocking collectives: 29.7 us -> none  [per_device(): lax.all_to_all(outgoing, 'node', split_axis=0, concat_axis=0, tiled=True)]
    ppermute x0 -> x8, waiting for transfers between devices: none -> 21.1 us  [trade(): return lax.ppermute(value, 'node', pairs)]
    all_to_all x1 -> x0, waiting for transfers between devices: 17.6 us -> none  [per_device(): lax.all_to_all(send_result, 'node', split_axis=0, concat_axis=0, tiled=True)]
    ppermute x0 -> x8, starting transfers between devices: none -> 13.2 us  [trade(): return lax.ppermute(value, 'node', pairs)]
    all_to_all x1 -> x0, starting transfers between devices: 4.48 us -> none  [per_device(): lax.all_to_all(send_result, 'node', split_axis=0, concat_axis=0, tiled=True)]
    concatenate x1 -> x5, other arithmetic: 0.01 us -> 3.57 us  [the longest x3 2.71 us: per_device(): rows = jnp.concatenate([rows, trade(rows, masks, node_count)], axis=0)]
    reshape x6 -> x0, local copies, waits for them, and re-layouts: 2.26 us -> none  [the longest x1 1.26 us: per_device(): send_result = result.reshape(arrived_shape)]
    gather x3 -> x0, local copies, waits for them, and re-layouts: 1.72 us -> none  [the longest x1 0.94 us: per_device(): pieces = grouped[picks_flat, :, rank_in]]
  transfers between devices with their start and end apart: 1 -> 8, of which waited for: 1 -> 8; matrix products, arithmetic and copies ran while one was open for 3% -> 5% of each run, Pallas kernels for 0% -> 0%
where the time goes in v1:
time: 55.2 us; the launch traced here: 54.7 us
  waiting for transfers between devices  21.1 us (38%)
  starting transfers between devices  13.2 us (24%)
  matrix products  9.45 us (17%)
  other arithmetic  7.93 us (14%)
  between operations  1.57 us (3%)
  local copies, waits for them, and re-layouts  1.5 us (3%)
    ppermute x8, waiting for transfers between devices, trade(): return lax.ppermute(value, 'node', pairs)  21.1 us
    ppermute x8, starting transfers between devices, trade(): return lax.ppermute(value, 'node', pairs)  13.2 us
    dot_general x1, matrix products, per_device(): total = jnp.dot(hidden, w_down[0], preferred_element_type=jnp.float32)  5.5 us
    dot_general x1, matrix products, per_device(): gate_part = jnp.dot(normed, w_gate[0], preferred_element_type=jnp.float32)  2.84 us
    concatenate x3, other arithmetic, per_device(): rows = jnp.concatenate([rows, trade(rows, masks, node_count)], axis=0)  2.71 us
    another operation x3, other arithmetic  1.38 us
  transfers between devices with their start and end apart: 8, of which 8 were waited for; matrix products, arithmetic and copies ran while one was open for 5% of the time, Pallas kernels for 0%

profile of v1, /device:TPU:0, one launch (start us, length us, event | category | flops | bytes accessed | tf_op | source)
XLA Modules:
  0.0 54.7 jit_solution(11636487722480530546)
XLA Ops:
  0.6 0.7 %reduce_sum.36 = f32[4]{0:T(128)S(1)} reduce(f32[4,2]{0,1:T(2,128)} %param.12, f32[]{:T(128)} %constant.28.clone.1), dimensions={1}, to_apply=%region_0.0 | reduce | flops 4 | bytes 52 | tf_op jit(solution)/shard_map/reduce_sum | solution.py:50
  1.4 0.7 %reduce-precision_convert_fusion = (bf16[4,2]{0,1:T(2,128)(2,1)S(1)}, f32[4,2]{0,1:T(2,128)S(1)}) fusion(f32[4]{0:T(128)S(1)} %reduce_sum.36, f32[4,2]{0,1:T(2,128)} %param.12), kind=kLoop, calls=%fused_computation.49 | loop fusion | flops 32 | bytes 96 | tf_op jit(solution)/shard_map/convert.7
  2.1 0.7 %convert_convert_fusion = bf16[4,2]{0,1:T(2,128)(2,1)S(1)} fusion(s32[4,2]{0,1:T(2,128)} %param.11), kind=kLoop, calls=%fused_computation.52 | loop fusion | flops 16 | bytes 48 | tf_op jit(solution)/shard_map/convert.6
  2.9 0.8 %pad_maximum_fusion.3 = bf16[4,7296]{1,0:T(4,128)(2,1)S(1)} fusion(bf16[4,128]{1,0:T(4,128)(2,1)S(1)} %pad.5.clone, bf16[4,7168]{1,0:T(4,128)(2,1)} %param.10), kind=kLoop, calls=%fused_computation.38 | loop fusion | flops 116736 | bytes 116736 | tf_op jit(solution)/shard_map/concatenate | solution.py:54
  3.7 4.1 %collective-permute-start = (bf16[4,7296]{1,0:T(4,128)(2,1)S(1)}, bf16[4,7296]{1,0:T(4,128)(2,1)S(1)}, u32[]{:S(2)}, u32[]{:S(2)}) collective-permute-start(bf16[4,7296]{1,0:T(4,128)(2,1)S(1)} %pad_maximum_fusion.3), channel_id=1, source_target_pairs={{0,8},{1,9},{2,10},{3,11},{4,12},{5,13},{6,14},{7,15},{8,0},{9,1},... | collective-permute-start | bytes 175112 | tf_op jit(solution)/shard_map/ppermute | solution.py:26
  7.8 2.8 %collective-permute-done = bf16[4,7296]{1,0:T(4,128)(2,1)S(1)} collective-permute-done((bf16[4,7296]{1,0:T(4,128)(2,1)S(1)}, bf16[4,7296]{1,0:T(4,128)(2,1)S(1)}, u32[]{:S(2)}, u32[]{:S(2)}) %collective-permute-start) | collective-permute-done | bytes 58400 | tf_op jit(solution)/shard_map/ppermute | solution.py:26
  10.6 0.9 %pad_maximum_fusion.2 = bf16[8,7296]{1,0:T(8,128)(2,1)S(1)} fusion(bf16[4,7296]{1,0:T(4,128)(2,1)S(1)} %collective-permute-done, bf16[4,128]{1,0:T(4,128)(2,1)S(1)} %pad.5.clone, bf16[4,7168]{1,0:T(4,128)(2,1)} %param.10), kind=kLoop, calls=%fused_computation.33 | loop fusion | flops 350208 | bytes 233472 | tf_op jit(solution)/shard_map/concatenate | solution.py:56
  11.5 2.4 %collective-permute-start.1 = (bf16[8,7296]{1,0:T(8,128)(2,1)S(1)}, bf16[8,7296]{1,0:T(8,128)(2,1)S(1)}, u32[]{:S(2)}, u32[]{:S(2)}) collective-permute-start(bf16[8,7296]{1,0:T(8,128)(2,1)S(1)} %pad_maximum_fusion.2), channel_id=1, source_target_pairs={{0,2},{1,5},{2,0},{3,7},{4,6},{5,1},{6,4},{7,3},{8,10},{9,13},{10,... | collective-permute-start | bytes 350216 | tf_op jit(solution)/shard_map/ppermute | solution.py:26
  13.9 2.8 %collective-permute-done.1 = bf16[8,7296]{1,0:T(8,128)(2,1)S(1)} collective-permute-done((bf16[8,7296]{1,0:T(8,128)(2,1)S(1)}, bf16[8,7296]{1,0:T(8,128)(2,1)S(1)}, u32[]{:S(2)}, u32[]{:S(2)}) %collective-permute-start.1) | collective-permute-done | bytes 116768 | tf_op jit(solution)/shard_map/ppermute | solution.py:26
  16.7 0.9 %pad_maximum_fusion.1 = bf16[16,7296]{1,0:T(8,128)(2,1)S(1)} fusion(bf16[8,7296]{1,0:T(8,128)(2,1)S(1)} %collective-permute-done.1, bf16[4,7296]{1,0:T(4,128)(2,1)S(1)} %collective-permute-done, bf16[4,128]{1,0:T(4,128)(2,1)S(1)} %pad.5.clone, bf16[4,7168]{1,0:T(4,128)(2,1)} %param.10), kind=kLoop, calls=%fused_computation.29 | loop fusion | flops 933888 | bytes 466944 | tf_op jit(solution)/shard_map/concatenate | solution.py:56
  17.6 1.0 %collective-permute-start.2 = (bf16[16,7296]{1,0:T(8,128)(2,1)S(1)}, bf16[16,7296]{1,0:T(8,128)(2,1)S(1)}, u32[]{:S(2)}, u32[]{:S(2)}) collective-permute-start(bf16[16,7296]{1,0:T(8,128)(2,1)S(1)} %pad_maximum_fusion.1), channel_id=1, source_target_pairs={{0,4},{1,3},{2,6},{3,1},{4,0},{5,7},{6,2},{7,5},{8,12},{9,11},{10,... | collective-permute-start | bytes 700424 | tf_op jit(solution)/shard_map/ppermute | solution.py:26
  18.7 5.1 %collective-permute-done.2 = bf16[16,7296]{1,0:T(8,128)(2,1)S(1)} collective-permute-done((bf16[16,7296]{1,0:T(8,128)(2,1)S(1)}, bf16[16,7296]{1,0:T(8,128)(2,1)S(1)}, u32[]{:S(2)}, u32[]{:S(2)}) %collective-permute-start.2) | collective-permute-done | bytes 233504 | tf_op jit(solution)/shard_map/ppermute | solution.py:26
  23.7 0.9 %pad_maximum_fusion = bf16[32,7296]{1,0:T(8,128)(2,1)S(1)} fusion(bf16[16,7296]{1,0:T(8,128)(2,1)S(1)} %collective-permute-done.2, bf16[8,7296]{1,0:T(8,128)(2,1)S(1)} %collective-permute-done.1, bf16[4,7296]{1,0:T(4,128)(2,1)S(1)} %collective-permute-done, bf16[4,128]{1,0:T(4,128)(2,1)S(1)} %pad.5.clone, bf16[4,7168]{1,0:T(4,128)(2,1)} %param.10), kind=kLoop, calls=%fused_computation.24 | loop fusion | flops 2334720 | bytes 933888 | tf_op jit(solution)/shard_map/concatenate | solution.py:56
  24.8 0.7 %convert_element_type.53 = f32[7168]{0:T(1024)S(1)} convert(bf16[7168]{0:T(1024)(128)(2,1)} %param.13) | non-fusion elementwise | flops 7168 | bytes 43008 | tf_op jit(solution)/shard_map/convert_element_type | solution.py:65
  25.5 1.1 %collective-permute-done.3 = bf16[32,7296]{1,0:T(8,128)(2,1)S(1)} collective-permute-done((bf16[32,7296]{1,0:T(8,128)(2,1)S(1)}, bf16[32,7296]{1,0:T(8,128)(2,1)S(1)}, u32[]{:S(2)}, u32[]{:S(2)}) %collective-permute-start.3) | collective-permute-done | bytes 466976 | tf_op jit(solution)/shard_map/ppermute | solution.py:26
  26.6 0.3 concatenate.27
  26.9 0.3 fusion.7
  27.4 2.8 %fusion.4 = f32[64,256]{1,0:T(8,128)S(1)} fusion(bf16[1,7168,256]{2,1,0:T(8,128)(2,1)} %param.14, f32[7168]{0:T(1024)S(1)} %convert_element_type.53, f32[64]{0:T(128)S(1)} %add_rsqrt_fusion, bf16[64,7296]{1,0:T(8,128)(2,1)S(1)} %concatenate.27), kind=kOutput, calls=%fused_computation.4 | convolution fusion | flops 236716032 | bytes 4682240 | tf_op jit(solution)/shard_map/dot_general | solution.py:66
  30.3 5.5 %fusion = f32[64,7168]{1,0:T(8,128)S(1)} fusion(bf16[1,256,7168]{2,1,0:T(8,128)(2,1)} %param.16, f32[64,256]{1,0:T(8,128)S(1)} %fusion.4, bf16[1,7168,256]{2,1,0:T(8,128)(2,1)} %param.15, f32[7168]{0:T(1024)S(1)} %convert_element_type.53, f32[64]{0:T(128)S(1)} %add_rsqrt_fusion, bf16[64,7296]{1,0:T(8,128)(2,1)S(1)} %concatenate.27, f32[64]{0:T(128)S(1)} %fusion.36), kind=kOutput, calls=%fused_computation | convolution fusion | flops 471711744 | bytes 10187776 | tf_op jit(solution)/shard_map/dot_general | solution.py:69
  35.8 0.2 collective-permute-start.4
  36.8 0.9 %collective-permute-done.4 = bf16[32,7168]{1,0:T(8,128)(2,1)S(1)} collective-permute-done((bf16[32,7168]{1,0:T(8,128)(2,1)S(1)}, bf16[32,7168]{1,0:T(8,128)(2,1)S(1)}, u32[]{:S(2)}, u32[]{:S(2)}) %collective-permute-start.4) | collective-permute-done | bytes 458784 | tf_op jit(solution)/shard_map/ppermute | solution.py:26
  37.8 1.0 %collective-permute-start.5 = (bf16[16,7168]{1,0:T(8,128)(2,1)S(1)}, bf16[16,7168]{1,0:T(8,128)(2,1)S(1)}, u32[]{:S(2)}, u32[]{:S(2)}) collective-permute-start(bf16[16,7168]{1,0:T(8,128)(2,1)S(1)} %slice.110), channel_id=1, source_target_pairs={{0,4},{1,3},{2,6},{3,1},{4,0},{5,7},{6,2},{7,5},{8,12},{9,11},{10,... | collective-permute-start | bytes 688136 | tf_op jit(solution)/shard_map/ppermute | solution.py:26
  38.9 0.5 fusion.41
  39.4 4.5 %collective-permute-done.5 = bf16[16,7168]{1,0:T(8,128)(2,1)S(1)} collective-permute-done((bf16[16,7168]{1,0:T(8,128)(2,1)S(1)}, bf16[16,7168]{1,0:T(8,128)(2,1)S(1)}, u32[]{:S(2)}, u32[]{:S(2)}) %collective-permute-start.5) | collective-permute-done | bytes 229408 | tf_op jit(solution)/shard_map/ppermute | solution.py:26
  44.0 2.1 %collective-permute-start.6 = (bf16[8,7168]{1,0:T(8,128)(2,1)S(1)}, bf16[8,7168]{1,0:T(8,128)(2,1)S(1)}, u32[]{:S(2)}, u32[]{:S(2)}) collective-permute-start(bf16[8,7168]{1,0:T(8,128)(2,1)S(1)} %slice.111), channel_id=1, source_target_pairs={{0,2},{1,5},{2,0},{3,7},{4,6},{5,1},{6,4},{7,3},{8,10},{9,13},{10,... | collective-permute-start | bytes 344072 | tf_op jit(solution)/shard_map/ppermute | solution.py:26
  46.1 0.2 fusion.20
  46.3 2.5 %collective-permute-done.6 = bf16[8,7168]{1,0:T(8,128)(2,1)S(1)} collective-permute-done((bf16[8,7168]{1,0:T(8,128)(2,1)S(1)}, bf16[8,7168]{1,0:T(8,128)(2,1)S(1)}, u32[]{:S(2)}, u32[]{:S(2)}) %collective-permute-start.6) | collective-permute-done | bytes 114720 | tf_op jit(solution)/shard_map/ppermute | solution.py:26
  48.9 2.2 %collective-permute-start.7 = (bf16[4,7168]{1,0:T(4,128)(2,1)S(1)}, bf16[4,7168]{1,0:T(4,128)(2,1)S(1)}, u32[]{:S(2)}, u32[]{:S(2)}) collective-permute-start(bf16[4,7168]{1,0:T(4,128)(2,1)S(1)} %slice.112), channel_id=1, source_target_pairs={{0,8},{1,9},{2,10},{3,11},{4,12},{5,13},{6,14},{7,15},{8,0},{9,1},... | collective-permute-start | bytes 172040 | tf_op jit(solution)/shard_map/ppermute | solution.py:26
  51.2 0.6 %fusion.17 = bf16[1,1,128,512]{3,2,1,0:T(8,128)(2,1)S(1)} fusion(bf16[1,1280,576]{1,2,0:T(8,128)(2,1)S(1)} %copy-done.1, f32[128,1280]{1,0:T(8,128)S(1)} %get-tuple-element.5, f32[128]{0:T(128)S(1)} %fusion.20, f32[128]{0:T(128)S(1)} %get-tuple-element.4), kind=kOutput, calls=%fused_computation.18 | convolution fusion | flops 168329216 | bytes 2098176 | tf_op jit(solution)/shard_map/rhj,rjv->rhv/dot_general | solution.py:38
  51.7 0.9 %copy.14 = bf16[1,1,128,512]{3,1,2,0:T(2,128)(2,1)} copy(bf16[1,1,128,512]{3,2,1,0:T(8,128)(2,1)S(1)} %fusion.17) | data formatting | bytes 262144
  52.6 1.4 %collective-permute-done.7 = bf16[4,7168]{1,0:T(4,128)(2,1)S(1)} collective-permute-done((bf16[4,7168]{1,0:T(4,128)(2,1)S(1)}, bf16[4,7168]{1,0:T(4,128)(2,1)S(1)}, u32[]{:S(2)}, u32[]{:S(2)}) %collective-permute-start.7) | collective-permute-done | bytes 57376 | tf_op jit(solution)/shard_map/ppermute | solution.py:26
  54.1 0.7 %fusion.26 = bf16[4,7168]{1,0:T(4,128)(2,1)} fusion(f32[8,7168]{1,0:T(8,128)S(1)} %slice_add_fusion.2, bf16[4,7168]{1,0:T(4,128)(2,1)S(1)} %collective-permute-done.7), kind=kLoop, calls=%fused_computation.36 | loop fusion | flops 86016 | bytes 229376 | tf_op jit(solution)/shard_map/convert_element_type | solution.py:75
  (20 shorter events, 0.7 us)
Async XLA Ops:
  0.6 38.2 %copy-start = (bf16[1,128,576]{1,2,0:T(8,128)(2,1)S(1)}, bf16[1,128,576]{1,2,0:T(8,128)(2,1)}, u32[]{:S(2)}) copy-start(bf16[1,128,576]{1,2,0:T(8,128)(2,1)} %param.17) | copy-start | bytes 442372
  3.7 6.9 %collective-permute-start = (bf16[4,7296]{1,0:T(4,128)(2,1)S(1)}, bf16[4,7296]{1,0:T(4,128)(2,1)S(1)}, u32[]{:S(2)}, u32[]{:S(2)}) collective-permute-start(bf16[4,7296]{1,0:T(4,128)(2,1)S(1)} %pad_maximum_fusion.3), channel_id=1, source_target_pairs={{0,8},{1,9},{2,10},{3,11},{4,12},{5,13},{6,14},{7,15},{8,0},{9,1},... | collective-permute-start | bytes 175112 | tf_op jit(solution)/shard_map/ppermute | solution.py:26
  11.5 5.2 %collective-permute-start.1 = (bf16[8,7296]{1,0:T(8,128)(2,1)S(1)}, bf16[8,7296]{1,0:T(8,128)(2,1)S(1)}, u32[]{:S(2)}, u32[]{:S(2)}) collective-permute-start(bf16[8,7296]{1,0:T(8,128)(2,1)S(1)} %pad_maximum_fusion.2), channel_id=1, source_target_pairs={{0,2},{1,5},{2,0},{3,7},{4,6},{5,1},{6,4},{7,3},{8,10},{9,13},{10,... | collective-permute-start | bytes 350216 | tf_op jit(solution)/shard_map/ppermute | solution.py:26
  17.6 6.1 %collective-permute-start.2 = (bf16[16,7296]{1,0:T(8,128)(2,1)S(1)}, bf16[16,7296]{1,0:T(8,128)(2,1)S(1)}, u32[]{:S(2)}, u32[]{:S(2)}) collective-permute-start(bf16[16,7296]{1,0:T(8,128)(2,1)S(1)} %pad_maximum_fusion.1), channel_id=1, source_target_pairs={{0,4},{1,3},{2,6},{3,1},{4,0},{5,7},{6,2},{7,5},{8,12},{9,11},{10,... | collective-permute-start | bytes 700424 | tf_op jit(solution)/shard_map/ppermute | solution.py:26
  24.7 1.9 %collective-permute-start.3 = (bf16[32,7296]{1,0:T(8,128)(2,1)S(1)}, bf16[32,7296]{1,0:T(8,128)(2,1)S(1)}, u32[]{:S(2)}, u32[]{:S(2)}) collective-permute-start(bf16[32,7296]{1,0:T(8,128)(2,1)S(1)} %pad_maximum_fusion), channel_id=1, source_target_pairs={{0,1},{1,0},{2,3},{3,2},{4,5},{5,4},{6,7},{7,6},{8,9},{9,8},{10,11... | collective-permute-start | bytes 1400840 | tf_op jit(solution)/shard_map/ppermute | solution.py:26
  35.8 3.1 %copy-start.1 = (bf16[1,1280,576]{1,2,0:T(8,128)(2,1)S(1)}, bf16[1,1280,576]{1,2,0:T(8,128)(2,1)}, u32[]{:S(2)}) copy-start(bf16[1,1280,576]{1,2,0:T(8,128)(2,1)} %param.18) | copy-start | bytes 4423684
  35.8 1.9 %collective-permute-start.4 = (bf16[32,7168]{1,0:T(8,128)(2,1)S(1)}, bf16[32,7168]{1,0:T(8,128)(2,1)S(1)}, u32[]{:S(2)}, u32[]{:S(2)}) collective-permute-start(bf16[32,7168]{1,0:T(8,128)(2,1)S(1)} %slice.109), channel_id=1, source_target_pairs={{0,1},{1,0},{2,3},{3,2},{4,5},{5,4},{6,7},{7,6},{8,9},{9,8},{10,11... | collective-permute-start | bytes 1376264 | tf_op jit(solution)/shard_map/ppermute | solution.py:26
  37.8 6.1 %collective-permute-start.5 = (bf16[16,7168]{1,0:T(8,128)(2,1)S(1)}, bf16[16,7168]{1,0:T(8,128)(2,1)S(1)}, u32[]{:S(2)}, u32[]{:S(2)}) collective-permute-start(bf16[16,7168]{1,0:T(8,128)(2,1)S(1)} %slice.110), channel_id=1, source_target_pairs={{0,4},{1,3},{2,6},{3,1},{4,0},{5,7},{6,2},{7,5},{8,12},{9,11},{10,... | collective-permute-start | bytes 688136 | tf_op jit(solution)/shard_map/ppermute | solution.py:26
  44.0 4.9 %collective-permute-start.6 = (bf16[8,7168]{1,0:T(8,128)(2,1)S(1)}, bf16[8,7168]{1,0:T(8,128)(2,1)S(1)}, u32[]{:S(2)}, u32[]{:S(2)}) collective-permute-start(bf16[8,7168]{1,0:T(8,128)(2,1)S(1)} %slice.111), channel_id=1, source_target_pairs={{0,2},{1,5},{2,0},{3,7},{4,6},{5,1},{6,4},{7,3},{8,10},{9,13},{10,... | collective-permute-start | bytes 344072 | tf_op jit(solution)/shard_map/ppermute | solution.py:26
  48.9 5.1 %collective-permute-start.7 = (bf16[4,7168]{1,0:T(4,128)(2,1)S(1)}, bf16[4,7168]{1,0:T(4,128)(2,1)S(1)}, u32[]{:S(2)}, u32[]{:S(2)}) collective-permute-start(bf16[4,7168]{1,0:T(4,128)(2,1)S(1)} %slice.112), channel_id=1, source_target_pairs={{0,8},{1,9},{2,10},{3,11},{4,12},{5,13},{6,14},{7,15},{8,0},{9,1},... | collective-permute-start | bytes 172040 | tf_op jit(solution)/shard_map/ppermute | solution.py:26

commit v2 on v1

v2 whole, which is shorter than its diff:
```python
import functools

import jax
import jax.numpy as jnp
from jax import lax
from jax.experimental import pallas as pl
from jax.experimental.pallas import tpu as pltpu
from jax.sharding import PartitionSpec as P

SPLIT = 4
CHUNK = 1024
VALUE_DIM = 512
LANES = 128
VMEM_LIMIT = 24 * 1024 * 1024


norm_eps = 1e-06
route_scale = 2.5
softmax_scale = 192.0 ** (-0.5)


def exchange_steps(node_count):
    nodes = range(node_count)
    far = [bit for bit in range(3, node_count.bit_length() - 1)]
    steps = [[node ^ (1 << bit) ^ (1 if bit == far[-1] else 0) for node in nodes] for bit in reversed(far)]
    for first, second in ((3, 5), (5, 3)):
        steps.append([node ^ (second if (node & 7).bit_count() % 2 else first) for node in nodes])
    return steps + [[node ^ 1 for node in nodes]]


def trade(value, partners):
    return lax.ppermute(value, "node", list(enumerate(partners)))


def in_hbm(array):
    return pltpu.with_memory_space_constraint(array, pltpu.HBM)


def pack_kernel(tokens_hbm, routes_hbm, gates_hbm, rows_ref, tokens_ref, routes_ref, gates_ref, sem):
    sources, targets = (routes_hbm, gates_hbm, tokens_hbm), (routes_ref, gates_ref, tokens_ref)
    copies = [
        pltpu.make_async_copy(source, target, sem.at[index])
        for index, (source, target) in enumerate(zip(sources, targets))
    ]
    for copy in copies:
        copy.start()
    count, width = tokens_ref.shape
    picks = routes_ref.shape[0]
    copies[0].wait()
    copies[1].wait()
    gates = gates_ref[...]
    mixing = route_scale * gates / jnp.sum(gates, axis=0, keepdims=True)
    high = mixing.astype(jnp.bfloat16).astype(jnp.float32)
    parts = [routes_ref[...].astype(jnp.float32), high, mixing - high]
    row = lax.broadcasted_iota(jnp.int32, (count, count), 0)
    diagonal = row == lax.broadcasted_iota(jnp.int32, (count, count), 1)
    lane = lax.broadcasted_iota(jnp.int32, (count, LANES), 1)
    notes = jnp.zeros((count, LANES), jnp.float32)
    for part, values in enumerate(parts):
        for pick in range(picks):
            spread = jnp.broadcast_to(values[pick : pick + 1], (count, count))
            column = jnp.sum(jnp.where(diagonal, spread, 0.0), axis=1, keepdims=True)
            notes = jnp.where(lane == part * picks + pick, column, notes)
    rows_ref[:, width:] = notes.astype(jnp.bfloat16)
    copies[2].wait()
    rows_ref[:, :width] = tokens_ref[...]


def pack(tokens, routes, gates):
    count, width = tokens.shape
    picks = routes.shape[1]
    hbm = pl.BlockSpec(memory_space=pltpu.HBM)
    return pl.pallas_call(
        pack_kernel,
        out_shape=jax.ShapeDtypeStruct((count, width + LANES), jnp.bfloat16),
        in_specs=[hbm, hbm, hbm],
        scratch_shapes=[
            pltpu.VMEM((count, width), jnp.bfloat16),
            pltpu.VMEM((picks, count), jnp.int32),
            pltpu.VMEM((picks, count), jnp.float32),
            pltpu.SemaphoreType.DMA((3,)),
        ],
        compiler_params=pltpu.CompilerParams(vmem_limit_bytes=VMEM_LIMIT),
        name="pack",
    )(*map(in_hbm, (tokens, routes.T, gates.T)))


def load_kernel(*refs):
    count = len(refs) // 2 - 1
    sources, targets, done_ref, sem = refs[1 : 1 + count], refs[1 + count : -2], refs[-2], refs[-1]
    copies = [
        pltpu.make_async_copy(source, target, sem.at[index])
        for index, (source, target) in enumerate(zip(sources, targets))
    ]
    for copy in copies:
        copy.start()
    for copy in copies:
        copy.wait()
    done_ref[...] = jnp.zeros(done_ref.shape, done_ref.dtype)


def load(after, arrays):
    anywhere = pl.BlockSpec(memory_space=pl.ANY)
    vmem = pl.BlockSpec(memory_space=pltpu.VMEM)
    hbm = pl.BlockSpec(memory_space=pltpu.HBM)
    return pl.pallas_call(
        load_kernel,
        out_shape=tuple(pltpu.VMEM(a.shape, a.dtype) for a in arrays)
        + (jax.ShapeDtypeStruct((8, LANES), jnp.float32),),
        in_specs=[anywhere] + [hbm] * len(arrays),
        out_specs=(vmem,) * (len(arrays) + 1),
        scratch_shapes=[pltpu.SemaphoreType.DMA((len(arrays),))],
        compiler_params=pltpu.CompilerParams(vmem_limit_bytes=VMEM_LIMIT),
        cost_estimate=pl.CostEstimate(
            flops=0, bytes_accessed=sum(a.size * a.dtype.itemsize for a in arrays), transcendentals=0
        ),
        name="load",
    )(after, *map(in_hbm, arrays))


def attention_kernel(after_ref, lengths_ref, queries_hbm, cache_hbm, attended_ref, queries_ref, cache_ref, sem):
    copies = [
        pltpu.make_async_copy(queries_hbm, queries_ref, sem.at[0]),
        pltpu.make_async_copy(cache_hbm, cache_ref, sem.at[1]),
    ]
    for copy in copies:
        copy.start()
    for copy in copies:
        copy.wait()
    queries = queries_ref[0].T
    cached = cache_ref[0]
    scores = jnp.dot(queries, cached, preferred_element_type=jnp.float32) * softmax_scale
    position = lax.broadcasted_iota(jnp.int32, scores.shape, 1)
    scores = jnp.where(position < lengths_ref[0], scores, -jnp.inf)
    powers = jnp.exp(scores - jnp.max(scores, axis=-1, keepdims=True))
    probs = (powers / jnp.sum(powers, axis=-1, keepdims=True)).astype(jnp.bfloat16)
    attended = lax.dot_general(
        probs,
        cached[:VALUE_DIM],
        (((1,), (1,)), ((), ())),
        preferred_element_type=jnp.float32,
    )
    attended_ref[0] = attended.astype(jnp.bfloat16)


def attention(after, lengths, queries, cache):
    heads = queries.shape[1]
    queries = jnp.swapaxes(queries, 1, 2)
    cache = jnp.swapaxes(cache, 1, 2)
    hbm = pl.BlockSpec(memory_space=pltpu.HBM)
    return pl.pallas_call(
        attention_kernel,
        out_shape=jax.ShapeDtypeStruct((1, heads, VALUE_DIM), jnp.bfloat16),
        in_specs=[pl.BlockSpec(memory_space=pl.ANY), pl.BlockSpec(memory_space=pltpu.SMEM), hbm, hbm],
        scratch_shapes=[
            pltpu.VMEM(queries.shape, queries.dtype),
            pltpu.VMEM(cache.shape, cache.dtype),
            pltpu.SemaphoreType.DMA((2,)),
        ],
        compiler_params=pltpu.CompilerParams(vmem_limit_bytes=VMEM_LIMIT),
        cost_estimate=pl.CostEstimate(flops=360_000_000, bytes_accessed=1_700_000, transcendentals=164_000),
        name="attention",
    )(after, lengths, *map(in_hbm, (queries, cache)))


def experts_kernel(picks, loaded_ref, own_ref, other_ref, gain_ref, gate_ref, up_ref, down_ref, sum_ref, send_ref):
    width = gate_ref.shape[1]
    half = own_ref.shape[0]
    count = 2 * half
    gate_part = jnp.zeros((count, gate_ref.shape[2]), jnp.float32)
    up_part = jnp.zeros((count, up_ref.shape[2]), jnp.float32)
    squares = jnp.zeros((count, LANES), jnp.float32)
    for start in range(0, width, CHUNK):
        chunk = pl.ds(start, min(CHUNK, width - start))
        rows = jnp.concatenate([own_ref[:, chunk], other_ref[:, chunk]], axis=0).astype(jnp.float32)
        scaled = []
        for lane in range(0, rows.shape[1], LANES):
            part = rows[:, lane : lane + LANES]
            squares = squares + part * part
            index = (start + lane) // LANES
            scaled.append((part * gain_ref[index : index + 1, :].astype(jnp.float32)).astype(jnp.bfloat16))
        scaled = jnp.concatenate(scaled, axis=1)
        gate_part += jnp.dot(scaled, gate_ref[0, chunk, :], preferred_element_type=jnp.float32)
        up_part += jnp.dot(scaled, up_ref[0, chunk, :], preferred_element_type=jnp.float32)
    inverse = lax.rsqrt(jnp.sum(squares, axis=-1, keepdims=True) / width + norm_eps)
    gate_part = gate_part * inverse
    up_part = up_part * inverse
    notes = jnp.concatenate([own_ref[:, width:], other_ref[:, width:]], axis=0).astype(jnp.float32)
    replica = (lax.axis_index("node") // SPLIT).astype(jnp.float32)
    share = jnp.zeros((count, 1), jnp.float32)
    for pick in range(picks):
        weight = notes[:, picks + pick : picks + pick + 1] + notes[:, 2 * picks + pick : 2 * picks + pick + 1]
        share = share + jnp.where(notes[:, pick : pick + 1] == replica, weight, 0.0)
    hidden = gate_part / (1.0 + jnp.exp(-gate_part)) * up_part * share
    hidden = hidden.astype(jnp.bfloat16)
    for start in range(0, width, CHUNK):
        chunk = pl.ds(start, min(CHUNK, width - start))
        part = jnp.dot(hidden, down_ref[0, :, chunk], preferred_element_type=jnp.float32)
        sum_ref[:, chunk] = part[:half]
        send_ref[:, chunk] = part[half:].astype(jnp.bfloat16)


def experts(loaded, own, other, picks, norm_gain, w_gate, w_up, w_down):
    half = own.shape[0]
    width = w_gate.shape[1]
    weights = [pltpu.with_memory_space_constraint(w, pltpu.VMEM) for w in (w_gate, w_up, w_down)]
    vmem = pl.BlockSpec(memory_space=pltpu.VMEM)
    return pl.pallas_call(
        functools.partial(experts_kernel, picks),
        out_shape=(
            jax.ShapeDtypeStruct((half, width), jnp.float32),
            jax.ShapeDtypeStruct((half, width), jnp.bfloat16),
        ),
        in_specs=[pl.BlockSpec(memory_space=pl.ANY)] + [vmem] * 6,
        out_specs=(vmem, vmem),
        compiler_params=pltpu.CompilerParams(vmem_limit_bytes=VMEM_LIMIT),
        name="experts",
    )(loaded, own, other, norm_gain.reshape(-1, LANES), *weights)


def per_device(tokens, routes, gates, norm_gain, w_gate, w_up, w_down, queries, cache, lengths):
    node_count = lax.axis_size("node")
    steps = exchange_steps(node_count)
    rows = pack(tokens, routes, gates)
    for partners in steps[:-2]:
        rows = jnp.concatenate([rows, trade(rows, partners)], axis=0)
    *weights, loaded = load(rows, (w_gate, w_up, w_down))
    arrived, loaded = lax.optimization_barrier((trade(rows, steps[-2]), loaded))
    rows = jnp.concatenate([rows, arrived], axis=0)
    other = trade(rows, steps[-1])

    total, send = experts(loaded, rows, other, routes.shape[1], norm_gain, *weights)
    total = total + trade(send, steps[-1]).astype(jnp.float32)
    attended = attention(total, lengths, queries, cache)
    for partners in reversed(steps[:-1]):
        half = total.shape[0] // 2
        arrived = trade(total[half:].astype(jnp.bfloat16), partners)
        if partners is steps[-2]:
            arrived, attended = lax.optimization_barrier((arrived, attended))
            attention_out = attended.reshape(1, -1)
        if partners is steps[-3]:
            arrived, attention_out = lax.optimization_barrier((arrived, attention_out))
        total = total[:half] + arrived.astype(jnp.float32)
    moe_out = total.astype(jnp.bfloat16)

    return (moe_out, attention_out)


def solution(mesh):
    in_specs = (
        P(("grp", "node"), None),
        P(("grp", "node"), None),
        P(("grp", "node"), None),
        P(),
        P("node", None, None),
        P("node", None, None),
        P("node", None, None),
        P(("grp", "node"), None, None),
        P(("grp", "node"), None, None),
        P(("grp", "node")),
    )
    out_specs = (P(("grp", "node"), None), P(("grp", "node"), None))
    return jax.shard_map(
        per_device, mesh=mesh, in_specs=in_specs, out_specs=out_specs, check_vma=False
    )
```

time: 55.2 us -> 41.8 us (0.76)
  the two profiles are of different devices: /device:TPU:0 before, /device:TPU:1 now
where the time goes in v2:
time: 41.8 us; the launch traced here: 41.6 us
  starting transfers between devices  15.1 us (36%)
  waiting for transfers between devices  13.2 us (32%)
  Pallas kernels  9.84 us (24%)
  between operations  1.37 us (3%)
  other arithmetic  1.07 us (3%)
  local copies, waits for them, and re-layouts  0.98 us (2%)
    ppermute x8, starting transfers between devices, trade(): return lax.ppermute(value, 'node', list(enumerate(partners)))  15.1 us
    ppermute x8, waiting for transfers between devices, trade(): return lax.ppermute(value, 'node', list(enumerate(partners)))  13.2 us
    pallas_call x1, Pallas kernels, load(): pl.pallas_call(load_kernel, out_shape=tuple((pltpu.VMEM(a.shape, a.dtype)...  4.23 us
    pallas_call x1, Pallas kernels, attention(): pl.pallas_call(attention_kernel, out_shape=jax.ShapeDtypeStruct((1, heads...  2.62 us
    pallas_call x1, Pallas kernels, experts(): pl.pallas_call(functools.partial(experts_kernel, picks), out_shape=(jax.S...  2.11 us
    unnamed x3, local copies, waits for them, and re-layouts  0.91 us
    pallas_call x1, Pallas kernels, pack(): pl.pallas_call(pack_kernel, out_shape=jax.ShapeDtypeStruct((count, width...  0.88 us
  transfers between devices with their start and end apart: 8, of which 8 were waited for; matrix products, arithmetic and copies ran while one was open for 2% of the time, Pallas kernels for 16%

profile of v2, /device:TPU:1, one launch (start us, length us, event | category | flops | bytes accessed | tf_op | source)
XLA Modules:
  0.0 41.6 jit_solution(9650539779856396709)
XLA Ops:
  0.6 0.9 %pack.1 = bf16[4,7296]{1,0:T(4,128)(2,1)S(1)} custom-call(bf16[4,7168]{1,0:T(4,128)(2,1)} %tokens_hbm.1, s32[2,4]{1,0:T(2,128)} %bitcast.12, f32[2,4]{1,0:T(2,128)} %bitcast.13), custom_call_target="tpu_custom_call" | custom-call | tf_op jit(solution)/shard_map/pack/pallas_call | solution.py:73
  1.5 3.8 %collective-permute-start = (bf16[4,7296]{1,0:T(4,128)(2,1)S(1)}, bf16[4,7296]{1,0:T(4,128)(2,1)S(1)}, u32[]{:S(2)}, u32[]{:S(2)}) collective-permute-start(bf16[4,7296]{1,0:T(4,128)(2,1)S(1)} %pack.1), channel_id=1, source_target_pairs={{0,9},{1,8},{2,11},{3,10},{4,13},{5,12},{6,15},{7,14},{8,1},{9,0},... | collective-permute-start | bytes 175112 | tf_op jit(solution)/shard_map/ppermute | solution.py:32
  5.3 1.9 %collective-permute-done = bf16[4,7296]{1,0:T(4,128)(2,1)S(1)} collective-permute-done((bf16[4,7296]{1,0:T(4,128)(2,1)S(1)}, bf16[4,7296]{1,0:T(4,128)(2,1)S(1)}, u32[]{:S(2)}, u32[]{:S(2)}) %collective-permute-start) | collective-permute-done | bytes 58400 | tf_op jit(solution)/shard_map/ppermute | solution.py:32
  7.2 0.1 pad_maximum_fusion.2
  7.2 2.7 %collective-permute-start.1 = (bf16[8,7296]{1,0:T(8,128)(2,1)S(1)}, bf16[8,7296]{1,0:T(8,128)(2,1)S(1)}, u32[]{:S(2)}, u32[]{:S(2)}) collective-permute-start(bf16[8,7296]{1,0:T(8,128)(2,1)S(1)} %pad_maximum_fusion.2), channel_id=1, source_target_pairs={{0,3},{1,4},{2,7},{3,0},{4,1},{5,6},{6,5},{7,2},{8,11},{9,12},{10,... | collective-permute-start | bytes 350216 | tf_op jit(solution)/shard_map/ppermute | solution.py:32
  9.9 2.8 %collective-permute-done.1 = bf16[8,7296]{1,0:T(8,128)(2,1)S(1)} collective-permute-done((bf16[8,7296]{1,0:T(8,128)(2,1)S(1)}, bf16[8,7296]{1,0:T(8,128)(2,1)S(1)}, u32[]{:S(2)}, u32[]{:S(2)}) %collective-permute-start.1) | collective-permute-done | bytes 116768 | tf_op jit(solution)/shard_map/ppermute | solution.py:32
  12.6 0.1 pad_maximum_fusion.1.refs_0_
  12.7 0.0 copy-start
  12.7 1.0 %collective-permute-start.2 = (bf16[16,7296]{1,0:T(8,128)(2,1)S(1)}, bf16[16,7296]{1,0:T(8,128)(2,1)S(1)}, u32[]{:S(2)}, u32[]{:S(2)}) collective-permute-start(bf16[16,7296]{1,0:T(8,128)(2,1)S(1)} %pad_maximum_fusion.1.refs_0_), channel_id=1, source_target_pairs={{0,5},{1,2},{2,1},{3,6},{4,7},{5,0},{6,3},{7,4},{8,13},{9,10},{10,... | collective-permute-start | bytes 700424 | tf_op jit(solution)/shard_map/ppermute | solution.py:32
  13.8 4.2 %load.1 = (bf16[1,7168,256]{2,1,0:T(8,128)(2,1)S(1)}, bf16[1,7168,256]{2,1,0:T(8,128)(2,1)S(1)}, bf16[1,256,7168]{2,1,0:T(8,128)(2,1)S(1)}, f32[8,128]{1,0:T(8,128)S(1)}) custom-call(bf16[16,7296]{1,0:T(8,128)(2,1)S(1)} %pad_maximum_fusion.1.refs_0_, bf16[1,7168,256]{2,1,0:T(8,128)(2,1)} %refs_1_.1, bf16[1,7168,256]{2,1,0:T(8,128)(2,1)} %refs_2_.1, ...), custom_call_target="tpu_custom_call" | custom-call | bytes 11010048 | tf_op jit(solution)/shard_map/load/pallas_call | solution.py:106
  18.0 0.3 collective-permute-done.2
  18.3 0.1 pad_maximum_fusion.own_ref
  18.4 0.5 %collective-permute-start.3 = (bf16[32,7296]{1,0:T(8,128)(2,1)S(1)}, bf16[32,7296]{1,0:T(8,128)(2,1)S(1)}, u32[]{:S(2)}, u32[]{:S(2)}) collective-permute-start(bf16[32,7296]{1,0:T(8,128)(2,1)S(1)} %pad_maximum_fusion.own_ref), channel_id=1, source_target_pairs={{0,1},{1,0},{2,3},{3,2},{4,5},{5,4},{6,7},{7,6},{8,9},{9,8},{10,11... | collective-permute-start | bytes 1400840 | tf_op jit(solution)/shard_map/ppermute | solution.py:32
  18.9 1.5 %collective-permute-done.3.other_ref = bf16[32,7296]{1,0:T(8,128)(2,1)S(1)} collective-permute-done((bf16[32,7296]{1,0:T(8,128)(2,1)S(1)}, bf16[32,7296]{1,0:T(8,128)(2,1)S(1)}, u32[]{:S(2)}, u32[]{:S(2)}) %collective-permute-start.3) | collective-permute-done | bytes 466976 | tf_op jit(solution)/shard_map/ppermute | solution.py:32
  20.3 0.0 copy-done
  20.3 2.1 %experts.1 = (f32[32,7168]{1,0:T(8,128)S(1)}, bf16[32,7168]{1,0:T(8,128)(2,1)S(1)}) custom-call(f32[8,128]{1,0:T(8,128)S(1)} %get-tuple-element.15.loaded_ref, bf16[32,7296]{1,0:T(8,128)(2,1)S(1)} %pad_maximum_fusion.own_ref, bf16[32,7296]{1,0:T(8,128)(2,1)S(1)} %collective-permute-done.3.other_ref, bf16[56,128]{1,0:T(8,128)(2,1)S(1)} %bitcast.8, ...), custom_call_target="tpu_custom_call" | custom-call | tf_op jit(solution)/shard_map/experts/pallas_call | solution.py:208
  22.4 0.4 %collective-permute-start.4 = (bf16[32,7168]{1,0:T(8,128)(2,1)S(1)}, bf16[32,7168]{1,0:T(8,128)(2,1)S(1)}, u32[]{:S(2)}, u32[]{:S(2)}) collective-permute-start(bf16[32,7168]{1,0:T(8,128)(2,1)S(1)} %get-tuple-element.21), channel_id=1, source_target_pairs={{0,1},{1,0},{2,3},{3,2},{4,5},{5,4},{6,7},{7,6},{8,9},{9,8},{10,11... | collective-permute-start | bytes 1376264 | tf_op jit(solution)/shard_map/ppermute | solution.py:32
  22.9 1.4 %collective-permute-done.4 = bf16[32,7168]{1,0:T(8,128)(2,1)S(1)} collective-permute-done((bf16[32,7168]{1,0:T(8,128)(2,1)S(1)}, bf16[32,7168]{1,0:T(8,128)(2,1)S(1)}, u32[]{:S(2)}, u32[]{:S(2)}) %collective-permute-start.4) | collective-permute-done | bytes 458784 | tf_op jit(solution)/shard_map/ppermute | solution.py:32
  24.3 0.1 convert_add_fusion.after_ref
  24.5 1.8 %collective-permute-start.5 = (bf16[16,7168]{1,0:T(8,128)(2,1)S(1)}, bf16[16,7168]{1,0:T(8,128)(2,1)S(1)}, u32[]{:S(2)}, u32[]{:S(2)}) collective-permute-start(bf16[16,7168]{1,0:T(8,128)(2,1)S(1)} %slice.41), channel_id=1, source_target_pairs={{0,5},{1,2},{2,1},{3,6},{4,7},{5,0},{6,3},{7,4},{8,13},{9,10},{10,... | collective-permute-start | bytes 688136 | tf_op jit(solution)/shard_map/ppermute | solution.py:32
  26.9 2.6 %attention.1 = bf16[1,128,512]{2,1,0:T(8,128)(2,1)S(1)} custom-call(f32[32,7168]{1,0:T(8,128)S(1)} %convert_add_fusion.after_ref, s32[1]{0:T(128)S(6)} %copy.13.lengths_ref, bf16[1,576,128]{2,1,0:T(8,128)(2,1)} %bitcast.11, bf16[1,576,1280]{2,1,0:T(8,128)(2,1)} %bitcast.9), custom_call_target="tpu_custom_call" | custom-call | flops 360000000 | bytes 1700000 | tf_op jit(solution)/shard_map/attention/pallas_call | solution.py:151
  29.5 0.4 %collective-permute-done.5 = bf16[16,7168]{1,0:T(8,128)(2,1)S(1)} collective-permute-done((bf16[16,7168]{1,0:T(8,128)(2,1)S(1)}, bf16[16,7168]{1,0:T(8,128)(2,1)S(1)}, u32[]{:S(2)}, u32[]{:S(2)}) %collective-permute-start.5) | collective-permute-done | bytes 229408 | tf_op jit(solution)/shard_map/ppermute | solution.py:32
  30.0 1.5 %collective-permute-start.6 = (bf16[8,7168]{1,0:T(8,128)(2,1)S(1)}, bf16[8,7168]{1,0:T(8,128)(2,1)S(1)}, u32[]{:S(2)}, u32[]{:S(2)}) collective-permute-start(bf16[8,7168]{1,0:T(8,128)(2,1)S(1)} %slice.42), channel_id=1, source_target_pairs={{0,3},{1,4},{2,7},{3,0},{4,1},{5,6},{6,5},{7,2},{8,11},{9,12},{10,... | collective-permute-start | bytes 344072 | tf_op jit(solution)/shard_map/ppermute | solution.py:32
  31.6 0.9 %copy.12 = bf16[1,1,128,512]{3,1,2,0:T(2,128)(2,1)} copy(bf16[1,1,128,512]{3,2,1,0:T(8,128)(2,1)S(1)} %bitcast.7) | data formatting | bytes 262144
  32.5 1.8 %collective-permute-done.6 = bf16[8,7168]{1,0:T(8,128)(2,1)S(1)} collective-permute-done((bf16[8,7168]{1,0:T(8,128)(2,1)S(1)}, bf16[8,7168]{1,0:T(8,128)(2,1)S(1)}, u32[]{:S(2)}, u32[]{:S(2)}) %collective-permute-start.6) | collective-permute-done | bytes 114720 | tf_op jit(solution)/shard_map/ppermute | solution.py:32
  34.4 3.4 %collective-permute-start.7 = (bf16[4,7168]{1,0:T(4,128)(2,1)S(1)}, bf16[4,7168]{1,0:T(4,128)(2,1)S(1)}, u32[]{:S(2)}, u32[]{:S(2)}) collective-permute-start(bf16[4,7168]{1,0:T(4,128)(2,1)S(1)} %slice.43), channel_id=1, source_target_pairs={{0,9},{1,8},{2,11},{3,10},{4,13},{5,12},{6,15},{7,14},{8,1},{9,0},... | collective-permute-start | bytes 172040 | tf_op jit(solution)/shard_map/ppermute | solution.py:32
  37.8 3.2 %collective-permute-done.7 = bf16[4,7168]{1,0:T(4,128)(2,1)S(1)} collective-permute-done((bf16[4,7168]{1,0:T(4,128)(2,1)S(1)}, bf16[4,7168]{1,0:T(4,128)(2,1)S(1)}, u32[]{:S(2)}, u32[]{:S(2)}) %collective-permute-start.7) | collective-permute-done | bytes 57376 | tf_op jit(solution)/shard_map/ppermute | solution.py:32
  40.9 0.7 %fusion = bf16[4,7168]{1,0:T(4,128)(2,1)} fusion(f32[8,7168]{1,0:T(8,128)S(1)} %slice_add_fusion.1, bf16[4,7168]{1,0:T(4,128)(2,1)S(1)} %collective-permute-done.7), kind=kLoop, calls=%fused_computation.10 | loop fusion | flops 86016 | bytes 229376 | tf_op jit(solution)/shard_map/convert_element_type | solution.py:244
  (5 shorter events, 0.1 us)
Async XLA Ops:
  1.5 5.6 %collective-permute-start = (bf16[4,7296]{1,0:T(4,128)(2,1)S(1)}, bf16[4,7296]{1,0:T(4,128)(2,1)S(1)}, u32[]{:S(2)}, u32[]{:S(2)}) collective-permute-start(bf16[4,7296]{1,0:T(4,128)(2,1)S(1)} %pack.1), channel_id=1, source_target_pairs={{0,9},{1,8},{2,11},{3,10},{4,13},{5,12},{6,15},{7,14},{8,1},{9,0},... | collective-permute-start | bytes 175112 | tf_op jit(solution)/shard_map/ppermute | solution.py:32
  7.2 5.4 %collective-permute-start.1 = (bf16[8,7296]{1,0:T(8,128)(2,1)S(1)}, bf16[8,7296]{1,0:T(8,128)(2,1)S(1)}, u32[]{:S(2)}, u32[]{:S(2)}) collective-permute-start(bf16[8,7296]{1,0:T(8,128)(2,1)S(1)} %pad_maximum_fusion.2), channel_id=1, source_target_pairs={{0,3},{1,4},{2,7},{3,0},{4,1},{5,6},{6,5},{7,2},{8,11},{9,12},{10,... | collective-permute-start | bytes 350216 | tf_op jit(solution)/shard_map/ppermute | solution.py:32
  12.7 7.6 %copy-start = (bf16[7168]{0:T(1024)(128)(2,1)S(1)}, bf16[7168]{0:T(1024)(128)(2,1)}, u32[]{:S(2)}) copy-start(bf16[7168]{0:T(1024)(128)(2,1)} %param.13) | copy-start | bytes 43012
  12.7 5.6 %collective-permute-start.2 = (bf16[16,7296]{1,0:T(8,128)(2,1)S(1)}, bf16[16,7296]{1,0:T(8,128)(2,1)S(1)}, u32[]{:S(2)}, u32[]{:S(2)}) collective-permute-start(bf16[16,7296]{1,0:T(8,128)(2,1)S(1)} %pad_maximum_fusion.1.refs_0_), channel_id=1, source_target_pairs={{0,5},{1,2},{2,1},{3,6},{4,7},{5,0},{6,3},{7,4},{8,13},{9,10},{10,... | collective-permute-start | bytes 700424 | tf_op jit(solution)/shard_map/ppermute | solution.py:32
  18.4 1.9 %collective-permute-start.3 = (bf16[32,7296]{1,0:T(8,128)(2,1)S(1)}, bf16[32,7296]{1,0:T(8,128)(2,1)S(1)}, u32[]{:S(2)}, u32[]{:S(2)}) collective-permute-start(bf16[32,7296]{1,0:T(8,128)(2,1)S(1)} %pad_maximum_fusion.own_ref), channel_id=1, source_target_pairs={{0,1},{1,0},{2,3},{3,2},{4,5},{5,4},{6,7},{7,6},{8,9},{9,8},{10,11... | collective-permute-start | bytes 1400840 | tf_op jit(solution)/shard_map/ppermute | solution.py:32
  22.4 1.9 %collective-permute-start.4 = (bf16[32,7168]{1,0:T(8,128)(2,1)S(1)}, bf16[32,7168]{1,0:T(8,128)(2,1)S(1)}, u32[]{:S(2)}, u32[]{:S(2)}) collective-permute-start(bf16[32,7168]{1,0:T(8,128)(2,1)S(1)} %get-tuple-element.21), channel_id=1, source_target_pairs={{0,1},{1,0},{2,3},{3,2},{4,5},{5,4},{6,7},{7,6},{8,9},{9,8},{10,11... | collective-permute-start | bytes 1376264 | tf_op jit(solution)/shard_map/ppermute | solution.py:32
  24.5 5.5 %collective-permute-start.5 = (bf16[16,7168]{1,0:T(8,128)(2,1)S(1)}, bf16[16,7168]{1,0:T(8,128)(2,1)S(1)}, u32[]{:S(2)}, u32[]{:S(2)}) collective-permute-start(bf16[16,7168]{1,0:T(8,128)(2,1)S(1)} %slice.41), channel_id=1, source_target_pairs={{0,5},{1,2},{2,1},{3,6},{4,7},{5,0},{6,3},{7,4},{8,13},{9,10},{10,... | collective-permute-start | bytes 688136 | tf_op jit(solution)/shard_map/ppermute | solution.py:32
  30.0 4.3 %collective-permute-start.6 = (bf16[8,7168]{1,0:T(8,128)(2,1)S(1)}, bf16[8,7168]{1,0:T(8,128)(2,1)S(1)}, u32[]{:S(2)}, u32[]{:S(2)}) collective-permute-start(bf16[8,7168]{1,0:T(8,128)(2,1)S(1)} %slice.42), channel_id=1, source_target_pairs={{0,3},{1,4},{2,7},{3,0},{4,1},{5,6},{6,5},{7,2},{8,11},{9,12},{10,... | collective-permute-start | bytes 344072 | tf_op jit(solution)/shard_map/ppermute | solution.py:32
  34.4 6.6 %collective-permute-start.7 = (bf16[4,7168]{1,0:T(4,128)(2,1)S(1)}, bf16[4,7168]{1,0:T(4,128)(2,1)S(1)}, u32[]{:S(2)}, u32[]{:S(2)}) collective-permute-start(bf16[4,7168]{1,0:T(4,128)(2,1)S(1)} %slice.43), channel_id=1, source_target_pairs={{0,9},{1,8},{2,11},{3,10},{4,13},{5,12},{6,15},{7,14},{8,1},{9,0},... | collective-permute-start | bytes 172040 | tf_op jit(solution)/shard_map/ppermute | solution.py:32

commit v3 on v2

--- a/solution.py
+++ b/solution.py
@@ -9,6 +9,7 @@
 
 SPLIT = 4
 CHUNK = 1024
+LOADS = 4
 VALUE_DIM = 512
 LANES = 128
 VMEM_LIMIT = 24 * 1024 * 1024
@@ -21,11 +22,9 @@
 
 def exchange_steps(node_count):
     nodes = range(node_count)
-    far = [bit for bit in range(3, node_count.bit_length() - 1)]
-    steps = [[node ^ (1 << bit) ^ (1 if bit == far[-1] else 0) for node in nodes] for bit in reversed(far)]
-    for first, second in ((3, 5), (5, 3)):
-        steps.append([node ^ (second if (node & 7).bit_count() % 2 else first) for node in nodes])
-    return steps + [[node ^ 1 for node in nodes]]
+    far = [[node ^ (1 << bit) for node in nodes] for bit in reversed(range(3, node_count.bit_length() - 1))]
+    near = [[node ^ masks[node % 2] for node in nodes] for masks in ((2, 4), (4, 2), (6, 6))]
+    return far, near, [node ^ 1 for node in nodes]
 
 
 def trade(value, partners):
@@ -85,13 +84,17 @@
     )(*map(in_hbm, (tokens, routes.T, gates.T)))
 
 
-def load_kernel(*refs):
-    count = len(refs) // 2 - 1
-    sources, targets, done_ref, sem = refs[1 : 1 + count], refs[1 + count : -2], refs[-2], refs[-1]
-    copies = [
-        pltpu.make_async_copy(source, target, sem.at[index])
-        for index, (source, target) in enumerate(zip(sources, targets))
-    ]
+def load_kernel(count, extra, *refs):
+    sources, targets = refs[:count], refs[count + extra : -2]
+    done_ref, sem = refs[-2:]
+    copies = []
+    for index, (source, target) in enumerate(zip(sources, targets)):
+        step = source.shape[1] // LOADS
+        for part in range(LOADS):
+            block = pl.ds(part * step, step)
+            copies.append(
+                pltpu.make_async_copy(source.at[:, block], target.at[:, block], sem.at[index * LOADS + part])
+            )
     for copy in copies:
         copy.start()
     for copy in copies:
@@ -99,23 +102,23 @@
     done_ref[...] = jnp.zeros(done_ref.shape, done_ref.dtype)
 
 
-def load(after, arrays):
+def load(after, arrays, *others):
     anywhere = pl.BlockSpec(memory_space=pl.ANY)
     vmem = pl.BlockSpec(memory_space=pltpu.VMEM)
     hbm = pl.BlockSpec(memory_space=pltpu.HBM)
     return pl.pallas_call(
-        load_kernel,
+        functools.partial(load_kernel, len(arrays), 1 + len(others)),
         out_shape=tuple(pltpu.VMEM(a.shape, a.dtype) for a in arrays)
         + (jax.ShapeDtypeStruct((8, LANES), jnp.float32),),
-        in_specs=[anywhere] + [hbm] * len(arrays),
+        in_specs=[hbm] * len(arrays) + [anywhere] * (1 + len(others)),
         out_specs=(vmem,) * (len(arrays) + 1),
-        scratch_shapes=[pltpu.SemaphoreType.DMA((len(arrays),))],
+        scratch_shapes=[pltpu.SemaphoreType.DMA((len(arrays) * LOADS,))],
         compiler_params=pltpu.CompilerParams(vmem_limit_bytes=VMEM_LIMIT),
         cost_estimate=pl.CostEstimate(
             flops=0, bytes_accessed=sum(a.size * a.dtype.itemsize for a in arrays), transcendentals=0
         ),
         name="load",
-    )(after, *map(in_hbm, arrays))
+    )(*map(in_hbm, arrays), after, *others)
 
 
 def attention_kernel(after_ref, lengths_ref, queries_hbm, cache_hbm, attended_ref, queries_ref, cache_ref, sem):
@@ -163,83 +166,96 @@
     )(after, lengths, *map(in_hbm, (queries, cache)))
 
 
-def experts_kernel(picks, loaded_ref, own_ref, other_ref, gain_ref, gate_ref, up_ref, down_ref, sum_ref, send_ref):
+def experts_kernel(picks, count, loaded_ref, *refs):
+    pieces, (gain_ref, gate_ref, up_ref, down_ref) = refs[:count], refs[count : count + 4]
+    outputs = refs[count + 4 :]
     width = gate_ref.shape[1]
-    half = own_ref.shape[0]
-    count = 2 * half
-    gate_part = jnp.zeros((count, gate_ref.shape[2]), jnp.float32)
-    up_part = jnp.zeros((count, up_ref.shape[2]), jnp.float32)
-    squares = jnp.zeros((count, LANES), jnp.float32)
+    rows = [piece.shape[0] for piece in pieces]
+    total = sum(rows)
+    gate_part = jnp.zeros((total, gate_ref.shape[2]), jnp.float32)
+    up_part = jnp.zeros((total, up_ref.shape[2]), jnp.float32)
+    squares = [jnp.zeros((size, LANES), jnp.float32) for size in rows]
     for start in range(0, width, CHUNK):
-        chunk = pl.ds(start, min(CHUNK, width - start))
-        rows = jnp.concatenate([own_ref[:, chunk], other_ref[:, chunk]], axis=0).astype(jnp.float32)
+        stop = min(start + CHUNK, width)
         scaled = []
-        for lane in range(0, rows.shape[1], LANES):
-            part = rows[:, lane : lane + LANES]
-            squares = squares + part * part
-            index = (start + lane) // LANES
-            scaled.append((part * gain_ref[index : index + 1, :].astype(jnp.float32)).astype(jnp.bfloat16))
+        for lane in range(start, stop, LANES):
+            gain = gain_ref[lane // LANES : lane // LANES + 1, :].astype(jnp.float32)
+            column = []
+            for index, piece in enumerate(pieces):
+                part = piece[:, lane : lane + LANES].astype(jnp.float32)
+                squares[index] = squares[index] + part * part
+                column.append(part * gain)
+            scaled.append(jnp.concatenate(column, axis=0).astype(jnp.bfloat16))
         scaled = jnp.concatenate(scaled, axis=1)
-        gate_part += jnp.dot(scaled, gate_ref[0, chunk, :], preferred_element_type=jnp.float32)
-        up_part += jnp.dot(scaled, up_ref[0, chunk, :], preferred_element_type=jnp.float32)
+        gate_part += jnp.dot(scaled, gate_ref[0, start:stop, :], preferred_element_type=jnp.float32)
+        up_part += jnp.dot(scaled, up_ref[0, start:stop, :], preferred_element_type=jnp.float32)
+    squares = jnp.concatenate(squares, axis=0)
     inverse = lax.rsqrt(jnp.sum(squares, axis=-1, keepdims=True) / width + norm_eps)
     gate_part = gate_part * inverse
     up_part = up_part * inverse
-    notes = jnp.concatenate([own_ref[:, width:], other_ref[:, width:]], axis=0).astype(jnp.float32)
+    notes = jnp.concatenate([piece[:, width:].astype(jnp.float32) for piece in pieces], axis=0)
     replica = (lax.axis_index("node") // SPLIT).astype(jnp.float32)
-    share = jnp.zeros((count, 1), jnp.float32)
+    share = jnp.zeros((total, 1), jnp.float32)
     for pick in range(picks):
         weight = notes[:, picks + pick : picks + pick + 1] + notes[:, 2 * picks + pick : 2 * picks + pick + 1]
         share = share + jnp.where(notes[:, pick : pick + 1] == replica, weight, 0.0)
     hidden = gate_part / (1.0 + jnp.exp(-gate_part)) * up_part * share
     hidden = hidden.astype(jnp.bfloat16)
     for start in range(0, width, CHUNK):
-        chunk = pl.ds(start, min(CHUNK, width - start))
-        part = jnp.dot(hidden, down_ref[0, :, chunk], preferred_element_type=jnp.float32)
-        sum_ref[:, chunk] = part[:half]
-        send_ref[:, chunk] = part[half:].astype(jnp.bfloat16)
-
-
-def experts(loaded, own, other, picks, norm_gain, w_gate, w_up, w_down):
-    half = own.shape[0]
-    width = w_gate.shape[1]
-    weights = [pltpu.with_memory_space_constraint(w, pltpu.VMEM) for w in (w_gate, w_up, w_down)]
+        stop = min(start + CHUNK, width)
+        part = jnp.dot(hidden, down_ref[0, :, start:stop], preferred_element_type=jnp.float32)
+        first = 0
+        for size, output in zip(rows, outputs):
+            output[:, start:stop] = part[first : first + size].astype(output.dtype)
+            first += size
+
+
+def experts(loaded, pieces, picks, gain, weights):
+    count = len(pieces)
+    width = weights[0].shape[1]
+    types = [jnp.float32] * (count // 2) + [jnp.bfloat16] * (count - count // 2)
     vmem = pl.BlockSpec(memory_space=pltpu.VMEM)
     return pl.pallas_call(
-        functools.partial(experts_kernel, picks),
-        out_shape=(
-            jax.ShapeDtypeStruct((half, width), jnp.float32),
-            jax.ShapeDtypeStruct((half, width), jnp.bfloat16),
+        functools.partial(experts_kernel, picks, count),
+        out_shape=tuple(
+            jax.ShapeDtypeStruct((piece.shape[0], width), kind) for piece, kind in zip(pieces, types)
         ),
-        in_specs=[pl.BlockSpec(memory_space=pl.ANY)] + [vmem] * 6,
-        out_specs=(vmem, vmem),
+        in_specs=[pl.BlockSpec(memory_space=pl.ANY)] + [vmem] * (count + 4),
+        out_specs=(vmem,) * count,
         compiler_params=pltpu.CompilerParams(vmem_limit_bytes=VMEM_LIMIT),
         name="experts",
-    )(loaded, own, other, norm_gain.reshape(-1, LANES), *weights)
+    )(loaded, *pieces, gain, *(pltpu.with_memory_space_constraint(w, pltpu.VMEM) for w in weights))
 
 
 def per_device(tokens, routes, gates, norm_gain, w_gate, w_up, w_down, queries, cache, lengths):
-    node_count = lax.axis_size("node")
-    steps = exchange_steps(node_count)
+    far, near, core = exchange_steps(lax.axis_size("node"))
+    gain = norm_gain.reshape(-1, LANES)
+
     rows = pack(tokens, routes, gates)
-    for partners in steps[:-2]:
-        rows = jnp.concatenate([rows, trade(rows, partners)], axis=0)
-    *weights, loaded = load(rows, (w_gate, w_up, w_down))
-    arrived, loaded = lax.optimization_barrier((trade(rows, steps[-2]), loaded))
-    rows = jnp.concatenate([rows, arrived], axis=0)
-    other = trade(rows, steps[-1])
-
-    total, send = experts(loaded, rows, other, routes.shape[1], norm_gain, *weights)
-    total = total + trade(send, steps[-1]).astype(jnp.float32)
-    attended = attention(total, lengths, queries, cache)
-    for partners in reversed(steps[:-1]):
+    gate, loaded = load(rows, (w_gate,))
+    for partners in far:
+        arrived, loaded = lax.optimization_barrier((trade(rows, partners), loaded))
+        rows = jnp.concatenate([rows, arrived], axis=0)
+    up, down, loaded = load(rows, (w_up, w_down), loaded)
+    weights = (gate, up, down)
+    pieces = [rows] + [trade(rows, partners) for partners in near]
+    pieces[-1], loaded = lax.optimization_barrier((pieces[-1], loaded))
+    pieces += [trade(piece, core) for piece in pieces]
+
+    outputs = experts(loaded, pieces, routes.shape[1], gain, weights)
+    own, other = outputs[:4], outputs[4:]
+    sums = [mine + trade(theirs, core).astype(jnp.float32) for mine, theirs in zip(own[1:], other[1:])]
+    attended = attention(sums[-1], lengths, queries, cache)
+    backs = [trade(part.astype(jnp.bfloat16), partners) for part, partners in zip(sums, near)]
+    total = own[0] + trade(other[0], core).astype(jnp.float32)
+    backs[-1], attended = lax.optimization_barrier((backs[-1], attended))
+    attention_out = attended.reshape(1, -1)
+    for back in backs:
+        total = total + back.astype(jnp.float32)
+    for partners in reversed(far):
         half = total.shape[0] // 2
         arrived = trade(total[half:].astype(jnp.bfloat16), partners)
-        if partners is steps[-2]:
-            arrived, attended = lax.optimization_barrier((arrived, attended))
-            attention_out = attended.reshape(1, -1)
-        if partners is steps[-3]:
-            arrived, attention_out = lax.optimization_barrier((arrived, attention_out))
+        arrived, attention_out = lax.optimization_barrier((arrived, attention_out))
         total = total[:half] + arrived.astype(jnp.float32)
     moe_out = total.astype(jnp.bfloat16)
 

time: 41.8 us -> 37.7 us (0.902)
  the two profiles are of different devices: /device:TPU:1 before, /device:TPU:0 now
where the time goes in v3:
time: 37.7 us; the launch traced here: 37.5 us
  starting transfers between devices  17.1 us (45%)
  Pallas kernels  10.8 us (29%)
  waiting for transfers between devices  6.32 us (17%)
  between operations  1.37 us (4%)
  local copies, waits for them, and re-layouts  0.94 us (2%)
  other arithmetic  0.89 us (2%)
    ppermute x16, starting transfers between devices, trade(): return lax.ppermute(value, 'node', list(enumerate(partners)))  17.1 us
    ppermute x16, waiting for transfers between devices, trade(): return lax.ppermute(value, 'node', list(enumerate(partners)))  6.32 us
    pallas_call x2, Pallas kernels, load(): pl.pallas_call(functools.partial(load_kernel, len(arrays), 1 + len(others...  5.21 us
    pallas_call x1, Pallas kernels, attention(): pl.pallas_call(attention_kernel, out_shape=jax.ShapeDtypeStruct((1, heads...  2.62 us
    pallas_call x1, Pallas kernels, experts(): pl.pallas_call(functools.partial(experts_kernel, picks, count), out_shape...  2.13 us
    unnamed x3, local copies, waits for them, and re-layouts  0.91 us
    pallas_call x1, Pallas kernels, pack(): pl.pallas_call(pack_kernel, out_shape=jax.ShapeDtypeStruct((count, width...  0.88 us
  transfers between devices with their start and end apart: 16, of which 9 were waited for; matrix products, arithmetic and copies ran while one was open for 3% of the time, Pallas kernels for 21%

profile of v3, /device:TPU:0, one launch (start us, length us, event | category | flops | bytes accessed | tf_op | source)
XLA Modules:
  0.0 37.5 jit_solution(10114486009579378806)
XLA Ops:
  0.6 0.9 %pack.1.refs_1_ = bf16[4,7296]{1,0:T(4,128)(2,1)S(1)} custom-call(bf16[4,7168]{1,0:T(4,128)(2,1)} %tokens_hbm.1, s32[2,4]{1,0:T(2,128)} %bitcast.12, f32[2,4]{1,0:T(2,128)} %bitcast.13), custom_call_target="tpu_custom_call" | custom-call | tf_op jit(solution)/shard_map/pack/pallas_call | solution.py:72
  1.5 4.1 %collective-permute-start = (bf16[4,7296]{1,0:T(4,128)(2,1)S(1)}, bf16[4,7296]{1,0:T(4,128)(2,1)S(1)}, u32[]{:S(2)}, u32[]{:S(2)}) collective-permute-start(bf16[4,7296]{1,0:T(4,128)(2,1)S(1)} %pack.1.refs_1_), channel_id=1, source_target_pairs={{0,8},{1,9},{2,10},{3,11},{4,12},{5,13},{6,14},{7,15},{8,0},{9,1},... | collective-permute-start | bytes 175112 | tf_op jit(solution)/shard_map/ppermute | solution.py:31
  5.6 2.0 %load.2 = (bf16[1,7168,256]{2,1,0:T(8,128)(2,1)S(1)}, f32[8,128]{1,0:T(8,128)S(1)}) custom-call(bf16[1,7168,256]{2,1,0:T(8,128)(2,1)} %refs_0_.2, bf16[4,7296]{1,0:T(4,128)(2,1)S(1)} %pack.1.refs_1_), custom_call_target="tpu_custom_call" | custom-call | bytes 3670016 | tf_op jit(solution)/shard_map/load/pallas_call | solution.py:109
  7.7 0.7 %collective-permute-done = bf16[4,7296]{1,0:T(4,128)(2,1)S(1)} collective-permute-done((bf16[4,7296]{1,0:T(4,128)(2,1)S(1)}, bf16[4,7296]{1,0:T(4,128)(2,1)S(1)}, u32[]{:S(2)}, u32[]{:S(2)}) %collective-permute-start) | collective-permute-done | bytes 58400 | tf_op jit(solution)/shard_map/ppermute | solution.py:31
  8.5 2.4 %collective-permute-start.1 = (bf16[8,7296]{1,0:T(8,128)(2,1)S(1)}, bf16[8,7296]{1,0:T(8,128)(2,1)S(1)}, u32[]{:S(2)}, u32[]{:S(2)}) collective-permute-start(bf16[8,7296]{1,0:T(8,128)(2,1)S(1)} %pad_maximum_fusion.refs_2_.refs_0_), channel_id=1, source_target_pairs={{0,6},{1,7},{2,4},{3,5},{4,2},{5,3},{6,0},{7,1},{8,14},{9,15},{10,... | collective-permute-start | bytes 350216 | tf_op jit(solution)/shard_map/ppermute | solution.py:31
  10.9 0.4 %collective-permute-start.2 = (bf16[8,7296]{1,0:T(8,128)(2,1)S(1)}, bf16[8,7296]{1,0:T(8,128)(2,1)S(1)}, u32[]{:S(2)}, u32[]{:S(2)}) collective-permute-start(bf16[8,7296]{1,0:T(8,128)(2,1)S(1)} %pad_maximum_fusion.refs_2_.refs_0_), channel_id=1, source_target_pairs={{0,2},{1,5},{2,0},{3,7},{4,6},{5,1},{6,4},{7,3},{8,10},{9,13},{10,... | collective-permute-start | bytes 350216 | tf_op jit(solution)/shard_map/ppermute | solution.py:31
  11.3 1.0 %collective-permute-start.3 = (bf16[8,7296]{1,0:T(8,128)(2,1)S(1)}, bf16[8,7296]{1,0:T(8,128)(2,1)S(1)}, u32[]{:S(2)}, u32[]{:S(2)}) collective-permute-start(bf16[8,7296]{1,0:T(8,128)(2,1)S(1)} %pad_maximum_fusion.refs_2_.refs_0_), channel_id=1, source_target_pairs={{0,4},{1,3},{2,6},{3,1},{4,0},{5,7},{6,2},{7,5},{8,12},{9,11},{10,... | collective-permute-start | bytes 350216 | tf_op jit(solution)/shard_map/ppermute | solution.py:31
  12.4 3.2 %load.3 = (bf16[1,7168,256]{2,1,0:T(8,128)(2,1)S(1)}, bf16[1,256,7168]{2,1,0:T(8,128)(2,1)S(1)}, f32[8,128]{1,0:T(8,128)S(1)}) custom-call(bf16[1,7168,256]{2,1,0:T(8,128)(2,1)} %refs_0_.3, bf16[1,256,7168]{2,1,0:T(8,128)(2,1)} %refs_1_.1, bf16[8,7296]{1,0:T(8,128)(2,1)S(1)} %pad_maximum_fusion.refs_2_.refs_0_, f32[8,128]{1,0:T(8,128)S(1)} %get-tuple-element.25.refs_3_), custom_call_target="tpu_custom_call" | custom-call | bytes 7340032 | tf_op jit(solution)/shard_map/load/pallas_call | solution.py:109
  15.5 0.6 %collective-permute-start.7 = (bf16[8,7296]{1,0:T(8,128)(2,1)S(1)}, bf16[8,7296]{1,0:T(8,128)(2,1)S(1)}, u32[]{:S(2)}, u32[]{:S(2)}) collective-permute-start(bf16[8,7296]{1,0:T(8,128)(2,1)S(1)} %collective-permute-done.1.refs_3_), channel_id=1, source_target_pairs={{0,1},{1,0},{2,3},{3,2},{4,5},{5,4},{6,7},{7,6},{8,9},{9,8},{10,11... | collective-permute-start | bytes 350216 | tf_op jit(solution)/shard_map/ppermute | solution.py:31
  16.1 0.1 collective-permute-start.5
  16.2 0.2 collective-permute-done.3.refs_2_
  16.4 0.2 collective-permute-start.6
  16.6 0.4 %collective-permute-done.7.refs_7_ = bf16[8,7296]{1,0:T(8,128)(2,1)S(1)} collective-permute-done((bf16[8,7296]{1,0:T(8,128)(2,1)S(1)}, bf16[8,7296]{1,0:T(8,128)(2,1)S(1)}, u32[]{:S(2)}, u32[]{:S(2)}) %collective-permute-start.7) | collective-permute-done | bytes 116768 | tf_op jit(solution)/shard_map/ppermute | solution.py:31
  17.1 0.4 collective-permute-done.5.refs_5_
  17.5 0.3 collective-permute-done.6.refs_6_
  17.8 2.1 %experts.1 = (f32[8,7168]{1,0:T(8,128)S(1)}, f32[8,7168]{1,0:T(8,128)S(1)}, f32[8,7168]{1,0:T(8,128)S(1)}, f32[8,7168]{1,0:T(8,128)S(1)}, bf16[8,7168]{1,0:T(8,1...) custom-call(f32[8,128]{1,0:T(8,128)S(1)} %get-tuple-element.27.loaded_ref, ...), custom_call_target="tpu_custom_call" | custom-call | tf_op jit(solution)/shard_map/experts/pallas_call | solution.py:218
  19.9 0.3 collective-permute-start.9
  20.2 0.3 collective-permute-start.11
  20.5 0.2 collective-permute-start.13
  20.7 0.3 collective-permute-start.8
  21.0 0.3 collective-permute-done.9
  21.3 1.9 %collective-permute-start.10 = (bf16[8,7168]{1,0:T(8,128)(2,1)S(1)}, bf16[8,7168]{1,0:T(8,128)(2,1)S(1)}, u32[]{:S(2)}, u32[]{:S(2)}) collective-permute-start(bf16[8,7168]{1,0:T(8,128)(2,1)S(1)} %add_convert_fusion.1), channel_id=1, source_target_pairs={{0,2},{1,5},{2,0},{3,7},{4,6},{5,1},{6,4},{7,3},{8,10},{9,13},{10,... | collective-permute-start | bytes 344072 | tf_op jit(solution)/shard_map/ppermute | solution.py:31
  23.3 1.1 %collective-permute-start.14 = (bf16[8,7168]{1,0:T(8,128)(2,1)S(1)}, bf16[8,7168]{1,0:T(8,128)(2,1)S(1)}, u32[]{:S(2)}, u32[]{:S(2)}) collective-permute-start(bf16[8,7168]{1,0:T(8,128)(2,1)S(1)} %get-tuple-element.44), channel_id=1, source_target_pairs={{0,6},{1,7},{2,4},{3,5},{4,2},{5,3},{6,0},{7,1},{8,14},{9,15},{10,... | collective-permute-start | bytes 344072 | tf_op jit(solution)/shard_map/ppermute | solution.py:31
  24.4 0.9 %collective-permute-start.12 = (bf16[8,7168]{1,0:T(8,128)(2,1)S(1)}, bf16[8,7168]{1,0:T(8,128)(2,1)S(1)}, u32[]{:S(2)}, u32[]{:S(2)}) collective-permute-start(bf16[8,7168]{1,0:T(8,128)(2,1)S(1)} %add_convert_fusion), channel_id=1, source_target_pairs={{0,4},{1,3},{2,6},{3,1},{4,0},{5,7},{6,2},{7,5},{8,12},{9,11},{10,... | collective-permute-start | bytes 344072 | tf_op jit(solution)/shard_map/ppermute | solution.py:31
  26.0 2.6 %attention.1 = bf16[1,128,512]{2,1,0:T(8,128)(2,1)S(1)} custom-call(f32[8,7168]{1,0:T(8,128)S(1)} %get-tuple-element.45.after_ref, s32[1]{0:T(128)S(6)} %copy.13.lengths_ref, bf16[1,576,128]{2,1,0:T(8,128)(2,1)} %bitcast.11, bf16[1,576,1280]{2,1,0:T(8,128)(2,1)} %bitcast.9), custom_call_target="tpu_custom_call" | custom-call | flops 360000000 | bytes 1700000 | tf_op jit(solution)/shard_map/attention/pallas_call | solution.py:154
  28.6 0.8 %collective-permute-done.14 = bf16[8,7168]{1,0:T(8,128)(2,1)S(1)} collective-permute-done((bf16[8,7168]{1,0:T(8,128)(2,1)S(1)}, bf16[8,7168]{1,0:T(8,128)(2,1)S(1)}, u32[]{:S(2)}, u32[]{:S(2)}) %collective-permute-start.14) | collective-permute-done | bytes 114720 | tf_op jit(solution)/shard_map/ppermute | solution.py:31
  29.4 0.6 %collective-permute-done.12 = bf16[8,7168]{1,0:T(8,128)(2,1)S(1)} collective-permute-done((bf16[8,7168]{1,0:T(8,128)(2,1)S(1)}, bf16[8,7168]{1,0:T(8,128)(2,1)S(1)}, u32[]{:S(2)}, u32[]{:S(2)}) %collective-permute-start.12) | collective-permute-done | bytes 114720 | tf_op jit(solution)/shard_map/ppermute | solution.py:31
  30.0 0.1 convert_add_fusion
  30.1 3.3 %collective-permute-start.15 = (bf16[4,7168]{1,0:T(4,128)(2,1)S(1)}, bf16[4,7168]{1,0:T(4,128)(2,1)S(1)}, u32[]{:S(2)}, u32[]{:S(2)}) collective-permute-start(bf16[4,7168]{1,0:T(4,128)(2,1)S(1)} %slice.15), channel_id=1, source_target_pairs={{0,8},{1,9},{2,10},{3,11},{4,12},{5,13},{6,14},{7,15},{8,0},{9,1},... | collective-permute-start | bytes 172040 | tf_op jit(solution)/shard_map/ppermute | solution.py:31
  33.4 0.9 %copy.12 = bf16[1,1,128,512]{3,1,2,0:T(2,128)(2,1)} copy(bf16[1,1,128,512]{3,2,1,0:T(8,128)(2,1)S(1)} %bitcast.7) | data formatting | bytes 262144
  34.3 2.5 %collective-permute-done.15 = bf16[4,7168]{1,0:T(4,128)(2,1)S(1)} collective-permute-done((bf16[4,7168]{1,0:T(4,128)(2,1)S(1)}, bf16[4,7168]{1,0:T(4,128)(2,1)S(1)}, u32[]{:S(2)}, u32[]{:S(2)}) %collective-permute-start.15) | collective-permute-done | bytes 57376 | tf_op jit(solution)/shard_map/ppermute | solution.py:31
  36.8 0.7 %fusion = bf16[4,7168]{1,0:T(4,128)(2,1)} fusion(f32[8,7168]{1,0:T(8,128)S(1)} %convert_add_fusion, bf16[4,7168]{1,0:T(4,128)(2,1)S(1)} %collective-permute-done.15), kind=kLoop, calls=%fused_computation.7 | loop fusion | flops 86016 | bytes 229376 | tf_op jit(solution)/shard_map/convert_element_type | solution.py:260
  (15 shorter events, 0.2 us)
Async XLA Ops:
  1.5 6.9 %collective-permute-start = (bf16[4,7296]{1,0:T(4,128)(2,1)S(1)}, bf16[4,7296]{1,0:T(4,128)(2,1)S(1)}, u32[]{:S(2)}, u32[]{:S(2)}) collective-permute-start(bf16[4,7296]{1,0:T(4,128)(2,1)S(1)} %pack.1.refs_1_), channel_id=1, source_target_pairs={{0,8},{1,9},{2,10},{3,11},{4,12},{5,13},{6,14},{7,15},{8,0},{9,1},... | collective-permute-start | bytes 175112 | tf_op jit(solution)/shard_map/ppermute | solution.py:31
  8.5 9.3 %copy-start = (bf16[7168]{0:T(1024)(128)(2,1)S(1)}, bf16[7168]{0:T(1024)(128)(2,1)}, u32[]{:S(2)}) copy-start(bf16[7168]{0:T(1024)(128)(2,1)} %param.13) | copy-start | bytes 43012
  8.5 7.0 %collective-permute-start.1 = (bf16[8,7296]{1,0:T(8,128)(2,1)S(1)}, bf16[8,7296]{1,0:T(8,128)(2,1)S(1)}, u32[]{:S(2)}, u32[]{:S(2)}) collective-permute-start(bf16[8,7296]{1,0:T(8,128)(2,1)S(1)} %pad_maximum_fusion.refs_2_.refs_0_), channel_id=1, source_target_pairs={{0,6},{1,7},{2,4},{3,5},{4,2},{5,3},{6,0},{7,1},{8,14},{9,15},{10,... | collective-permute-start | bytes 350216 | tf_op jit(solution)/shard_map/ppermute | solution.py:31
  10.9 5.3 %collective-permute-start.2 = (bf16[8,7296]{1,0:T(8,128)(2,1)S(1)}, bf16[8,7296]{1,0:T(8,128)(2,1)S(1)}, u32[]{:S(2)}, u32[]{:S(2)}) collective-permute-start(bf16[8,7296]{1,0:T(8,128)(2,1)S(1)} %pad_maximum_fusion.refs_2_.refs_0_), channel_id=1, source_target_pairs={{0,2},{1,5},{2,0},{3,7},{4,6},{5,1},{6,4},{7,3},{8,10},{9,13},{10,... | collective-permute-start | bytes 350216 | tf_op jit(solution)/shard_map/ppermute | solution.py:31
  11.3 5.1 %collective-permute-start.3 = (bf16[8,7296]{1,0:T(8,128)(2,1)S(1)}, bf16[8,7296]{1,0:T(8,128)(2,1)S(1)}, u32[]{:S(2)}, u32[]{:S(2)}) collective-permute-start(bf16[8,7296]{1,0:T(8,128)(2,1)S(1)} %pad_maximum_fusion.refs_2_.refs_0_), channel_id=1, source_target_pairs={{0,4},{1,3},{2,6},{3,1},{4,0},{5,7},{6,2},{7,5},{8,12},{9,11},{10,... | collective-permute-start | bytes 350216 | tf_op jit(solution)/shard_map/ppermute | solution.py:31
  12.3 4.3 %collective-permute-start.4 = (bf16[8,7296]{1,0:T(8,128)(2,1)S(1)}, bf16[8,7296]{1,0:T(8,128)(2,1)S(1)}, u32[]{:S(2)}, u32[]{:S(2)}) collective-permute-start(bf16[8,7296]{1,0:T(8,128)(2,1)S(1)} %pad_maximum_fusion.refs_2_.refs_0_), channel_id=1, source_target_pairs={{0,1},{1,0},{2,3},{3,2},{4,5},{5,4},{6,7},{7,6},{8,9},{9,8},{10,11... | collective-permute-start | bytes 350216 | tf_op jit(solution)/shard_map/ppermute | solution.py:31
  15.5 1.5 %collective-permute-start.7 = (bf16[8,7296]{1,0:T(8,128)(2,1)S(1)}, bf16[8,7296]{1,0:T(8,128)(2,1)S(1)}, u32[]{:S(2)}, u32[]{:S(2)}) collective-permute-start(bf16[8,7296]{1,0:T(8,128)(2,1)S(1)} %collective-permute-done.1.refs_3_), channel_id=1, source_target_pairs={{0,1},{1,0},{2,3},{3,2},{4,5},{5,4},{6,7},{7,6},{8,9},{9,8},{10,11... | collective-permute-start | bytes 350216 | tf_op jit(solution)/shard_map/ppermute | solution.py:31
  16.1 1.3 %collective-permute-start.5 = (bf16[8,7296]{1,0:T(8,128)(2,1)S(1)}, bf16[8,7296]{1,0:T(8,128)(2,1)S(1)}, u32[]{:S(2)}, u32[]{:S(2)}) collective-permute-start(bf16[8,7296]{1,0:T(8,128)(2,1)S(1)} %collective-permute-done.2.refs_1_), channel_id=1, source_target_pairs={{0,1},{1,0},{2,3},{3,2},{4,5},{5,4},{6,7},{7,6},{8,9},{9,8},{10,11... | collective-permute-start | bytes 350216 | tf_op jit(solution)/shard_map/ppermute | solution.py:31
  16.4 1.3 %collective-permute-start.6 = (bf16[8,7296]{1,0:T(8,128)(2,1)S(1)}, bf16[8,7296]{1,0:T(8,128)(2,1)S(1)}, u32[]{:S(2)}, u32[]{:S(2)}) collective-permute-start(bf16[8,7296]{1,0:T(8,128)(2,1)S(1)} %collective-permute-done.3.refs_2_), channel_id=1, source_target_pairs={{0,1},{1,0},{2,3},{3,2},{4,5},{5,4},{6,7},{7,6},{8,9},{9,8},{10,11... | collective-permute-start | bytes 350216 | tf_op jit(solution)/shard_map/ppermute | solution.py:31
  19.9 1.4 %collective-permute-start.9 = (bf16[8,7168]{1,0:T(8,128)(2,1)S(1)}, bf16[8,7168]{1,0:T(8,128)(2,1)S(1)}, u32[]{:S(2)}, u32[]{:S(2)}) collective-permute-start(bf16[8,7168]{1,0:T(8,128)(2,1)S(1)} %get-tuple-element.35), channel_id=1, source_target_pairs={{0,1},{1,0},{2,3},{3,2},{4,5},{5,4},{6,7},{7,6},{8,9},{9,8},{10,11... | collective-permute-start | bytes 344072 | tf_op jit(solution)/shard_map/ppermute | solution.py:31
  20.2 4.2 %collective-permute-start.11 = (bf16[8,7168]{1,0:T(8,128)(2,1)S(1)}, bf16[8,7168]{1,0:T(8,128)(2,1)S(1)}, u32[]{:S(2)}, u32[]{:S(2)}) collective-permute-start(bf16[8,7168]{1,0:T(8,128)(2,1)S(1)} %get-tuple-element.37), channel_id=1, source_target_pairs={{0,1},{1,0},{2,3},{3,2},{4,5},{5,4},{6,7},{7,6},{8,9},{9,8},{10,11... | collective-permute-start | bytes 344072 | tf_op jit(solution)/shard_map/ppermute | solution.py:31
  20.5 2.8 %collective-permute-start.13 = (bf16[8,7168]{1,0:T(8,128)(2,1)S(1)}, bf16[8,7168]{1,0:T(8,128)(2,1)S(1)}, u32[]{:S(2)}, u32[]{:S(2)}) collective-permute-start(bf16[8,7168]{1,0:T(8,128)(2,1)S(1)} %get-tuple-element.39), channel_id=1, source_target_pairs={{0,1},{1,0},{2,3},{3,2},{4,5},{5,4},{6,7},{7,6},{8,9},{9,8},{10,11... | collective-permute-start | bytes 344072 | tf_op jit(solution)/shard_map/ppermute | solution.py:31
  20.7 8.8 %collective-permute-start.8 = (bf16[8,7168]{1,0:T(8,128)(2,1)S(1)}, bf16[8,7168]{1,0:T(8,128)(2,1)S(1)}, u32[]{:S(2)}, u32[]{:S(2)}) collective-permute-start(bf16[8,7168]{1,0:T(8,128)(2,1)S(1)} %get-tuple-element.33), channel_id=1, source_target_pairs={{0,1},{1,0},{2,3},{3,2},{4,5},{5,4},{6,7},{7,6},{8,9},{9,8},{10,11... | collective-permute-start | bytes 344072 | tf_op jit(solution)/shard_map/ppermute | solution.py:31
  21.3 8.1 %collective-permute-start.10 = (bf16[8,7168]{1,0:T(8,128)(2,1)S(1)}, bf16[8,7168]{1,0:T(8,128)(2,1)S(1)}, u32[]{:S(2)}, u32[]{:S(2)}) collective-permute-start(bf16[8,7168]{1,0:T(8,128)(2,1)S(1)} %add_convert_fusion.1), channel_id=1, source_target_pairs={{0,2},{1,5},{2,0},{3,7},{4,6},{5,1},{6,4},{7,3},{8,10},{9,13},{10,... | collective-permute-start | bytes 344072 | tf_op jit(solution)/shard_map/ppermute | solution.py:31
  23.3 6.1 %collective-permute-start.14 = (bf16[8,7168]{1,0:T(8,128)(2,1)S(1)}, bf16[8,7168]{1,0:T(8,128)(2,1)S(1)}, u32[]{:S(2)}, u32[]{:S(2)}) collective-permute-start(bf16[8,7168]{1,0:T(8,128)(2,1)S(1)} %get-tuple-element.44), channel_id=1, source_target_pairs={{0,6},{1,7},{2,4},{3,5},{4,2},{5,3},{6,0},{7,1},{8,14},{9,15},{10,... | collective-permute-start | bytes 344072 | tf_op jit(solution)/shard_map/ppermute | solution.py:31
  24.4 5.6 %collective-permute-start.12 = (bf16[8,7168]{1,0:T(8,128)(2,1)S(1)}, bf16[8,7168]{1,0:T(8,128)(2,1)S(1)}, u32[]{:S(2)}, u32[]{:S(2)}) collective-permute-start(bf16[8,7168]{1,0:T(8,128)(2,1)S(1)} %add_convert_fusion), channel_id=1, source_target_pairs={{0,4},{1,3},{2,6},{3,1},{4,0},{5,7},{6,2},{7,5},{8,12},{9,11},{10,... | collective-permute-start | bytes 344072 | tf_op jit(solution)/shard_map/ppermute | solution.py:31
  30.1 6.7 %collective-permute-start.15 = (bf16[4,7168]{1,0:T(4,128)(2,1)S(1)}, bf16[4,7168]{1,0:T(4,128)(2,1)S(1)}, u32[]{:S(2)}, u32[]{:S(2)}) collective-permute-start(bf16[4,7168]{1,0:T(4,128)(2,1)S(1)} %slice.15), channel_id=1, source_target_pairs={{0,8},{1,9},{2,10},{3,11},{4,12},{5,13},{6,14},{7,15},{8,0},{9,1},... | collective-permute-start | bytes 172040 | tf_op jit(solution)/shard_map/ppermute | solution.py:31

commit v4 on v3

--- a/solution.py
+++ b/solution.py
@@ -9,7 +9,6 @@
 
 SPLIT = 4
 CHUNK = 1024
-LOADS = 4
 VALUE_DIM = 512
 LANES = 128
 VMEM_LIMIT = 24 * 1024 * 1024
@@ -84,43 +83,6 @@
     )(*map(in_hbm, (tokens, routes.T, gates.T)))
 
 
-def load_kernel(count, extra, *refs):
-    sources, targets = refs[:count], refs[count + extra : -2]
-    done_ref, sem = refs[-2:]
-    copies = []
-    for index, (source, target) in enumerate(zip(sources, targets)):
-        step = source.shape[1] // LOADS
-        for part in range(LOADS):
-            block = pl.ds(part * step, step)
-            copies.append(
-                pltpu.make_async_copy(source.at[:, block], target.at[:, block], sem.at[index * LOADS + part])
-            )
-    for copy in copies:
-        copy.start()
-    for copy in copies:
-        copy.wait()
-    done_ref[...] = jnp.zeros(done_ref.shape, done_ref.dtype)
-
-
-def load(after, arrays, *others):
-    anywhere = pl.BlockSpec(memory_space=pl.ANY)
-    vmem = pl.BlockSpec(memory_space=pltpu.VMEM)
-    hbm = pl.BlockSpec(memory_space=pltpu.HBM)
-    return pl.pallas_call(
-        functools.partial(load_kernel, len(arrays), 1 + len(others)),
-        out_shape=tuple(pltpu.VMEM(a.shape, a.dtype) for a in arrays)
-        + (jax.ShapeDtypeStruct((8, LANES), jnp.float32),),
-        in_specs=[hbm] * len(arrays) + [anywhere] * (1 + len(others)),
-        out_specs=(vmem,) * (len(arrays) + 1),
-        scratch_shapes=[pltpu.SemaphoreType.DMA((len(arrays) * LOADS,))],
-        compiler_params=pltpu.CompilerParams(vmem_limit_bytes=VMEM_LIMIT),
-        cost_estimate=pl.CostEstimate(
-            flops=0, bytes_accessed=sum(a.size * a.dtype.itemsize for a in arrays), transcendentals=0
-        ),
-        name="load",
-    )(*map(in_hbm, arrays), after, *others)
-
-
 def attention_kernel(after_ref, lengths_ref, queries_hbm, cache_hbm, attended_ref, queries_ref, cache_ref, sem):
     copies = [
         pltpu.make_async_copy(queries_hbm, queries_ref, sem.at[0]),
@@ -161,7 +123,7 @@
             pltpu.SemaphoreType.DMA((2,)),
         ],
         compiler_params=pltpu.CompilerParams(vmem_limit_bytes=VMEM_LIMIT),
-        cost_estimate=pl.CostEstimate(flops=360_000_000, bytes_accessed=1_700_000, transcendentals=164_000),
+        cost_estimate=pl.CostEstimate(flops=4_000_000_000, bytes_accessed=1_700_000, transcendentals=164_000),
         name="attention",
     )(after, lengths, *map(in_hbm, (queries, cache)))
 
@@ -172,8 +134,9 @@
     width = gate_ref.shape[1]
     rows = [piece.shape[0] for piece in pieces]
     total = sum(rows)
-    gate_part = jnp.zeros((total, gate_ref.shape[2]), jnp.float32)
-    up_part = jnp.zeros((total, up_ref.shape[2]), jnp.float32)
+    padding = -total % LANES
+    gate_part = jnp.zeros((total + padding, gate_ref.shape[2]), jnp.float32)
+    up_part = jnp.zeros((total + padding, up_ref.shape[2]), jnp.float32)
     squares = [jnp.zeros((size, LANES), jnp.float32) for size in rows]
     for start in range(0, width, CHUNK):
         stop = min(start + CHUNK, width)
@@ -185,14 +148,16 @@
                 part = piece[:, lane : lane + LANES].astype(jnp.float32)
                 squares[index] = squares[index] + part * part
                 column.append(part * gain)
+            if padding:
+                column.append(jnp.zeros((padding, LANES), jnp.float32))
             scaled.append(jnp.concatenate(column, axis=0).astype(jnp.bfloat16))
         scaled = jnp.concatenate(scaled, axis=1)
         gate_part += jnp.dot(scaled, gate_ref[0, start:stop, :], preferred_element_type=jnp.float32)
         up_part += jnp.dot(scaled, up_ref[0, start:stop, :], preferred_element_type=jnp.float32)
     squares = jnp.concatenate(squares, axis=0)
     inverse = lax.rsqrt(jnp.sum(squares, axis=-1, keepdims=True) / width + norm_eps)
-    gate_part = gate_part * inverse
-    up_part = up_part * inverse
+    gate_part = gate_part[:total] * inverse
+    up_part = up_part[:total] * inverse
     notes = jnp.concatenate([piece[:, width:].astype(jnp.float32) for piece in pieces], axis=0)
     replica = (lax.axis_index("node") // SPLIT).astype(jnp.float32)
     share = jnp.zeros((total, 1), jnp.float32)
@@ -201,6 +166,8 @@
         share = share + jnp.where(notes[:, pick : pick + 1] == replica, weight, 0.0)
     hidden = gate_part / (1.0 + jnp.exp(-gate_part)) * up_part * share
     hidden = hidden.astype(jnp.bfloat16)
+    if padding:
+        hidden = jnp.concatenate([hidden, jnp.zeros((padding, hidden.shape[1]), hidden.dtype)], axis=0)
     for start in range(0, width, CHUNK):
         stop = min(start + CHUNK, width)
         part = jnp.dot(hidden, down_ref[0, :, start:stop], preferred_element_type=jnp.float32)
@@ -224,7 +191,7 @@
         out_specs=(vmem,) * count,
         compiler_params=pltpu.CompilerParams(vmem_limit_bytes=VMEM_LIMIT),
         name="experts",
-    )(loaded, *pieces, gain, *(pltpu.with_memory_space_constraint(w, pltpu.VMEM) for w in weights))
+    )(loaded, *pieces, gain, *weights)
 
 
 def per_device(tokens, routes, gates, norm_gain, w_gate, w_up, w_down, queries, cache, lengths):
@@ -232,31 +199,35 @@
     gain = norm_gain.reshape(-1, LANES)
 
     rows = pack(tokens, routes, gates)
-    gate, loaded = load(rows, (w_gate,))
     for partners in far:
-        arrived, loaded = lax.optimization_barrier((trade(rows, partners), loaded))
-        rows = jnp.concatenate([rows, arrived], axis=0)
-    up, down, loaded = load(rows, (w_up, w_down), loaded)
-    weights = (gate, up, down)
+        rows = jnp.concatenate([rows, trade(rows, partners)], axis=0)
+    attended = attention(rows, lengths, queries, cache)
+    weights = (w_gate, w_up, w_down)
     pieces = [rows] + [trade(rows, partners) for partners in near]
-    pieces[-1], loaded = lax.optimization_barrier((pieces[-1], loaded))
+    pieces[-1], attended = lax.optimization_barrier((pieces[-1], attended))
     pieces += [trade(piece, core) for piece in pieces]
 
-    outputs = experts(loaded, pieces, routes.shape[1], gain, weights)
+    outputs = experts(attended, pieces, routes.shape[1], gain, weights)
     own, other = outputs[:4], outputs[4:]
     sums = [mine + trade(theirs, core).astype(jnp.float32) for mine, theirs in zip(own[1:], other[1:])]
-    attended = attention(sums[-1], lengths, queries, cache)
-    backs = [trade(part.astype(jnp.bfloat16), partners) for part, partners in zip(sums, near)]
+    half = rows.shape[0] // 2
+    backs = [trade(part.astype(jnp.bfloat16), partners) for part, partners in zip(sums[:2], near[:2])]
+    both = sums[2].astype(jnp.bfloat16)
+    back_far = trade(both[half:], near[2])
+    back_near = trade(both[:half], near[2])
     total = own[0] + trade(other[0], core).astype(jnp.float32)
-    backs[-1], attended = lax.optimization_barrier((backs[-1], attended))
     attention_out = attended.reshape(1, -1)
+    back_far, attention_out = lax.optimization_barrier((back_far, attention_out))
     for back in backs:
         total = total + back.astype(jnp.float32)
-    for partners in reversed(far):
-        half = total.shape[0] // 2
-        arrived = trade(total[half:].astype(jnp.bfloat16), partners)
-        arrived, attention_out = lax.optimization_barrier((arrived, attention_out))
-        total = total[:half] + arrived.astype(jnp.float32)
+    send = (total[half:] + back_far.astype(jnp.float32)).astype(jnp.bfloat16)
+    total = total[:half] + back_near.astype(jnp.float32)
+    for index, partners in enumerate(reversed(far)):
+        if index:
+            half = total.shape[0] // 2
+            send, total = total[half:].astype(jnp.bfloat16), total[:half]
+        total = total + trade(send, partners).astype(jnp.float32)
+    moe_out = total.astype(jnp.bfloat16)
     moe_out = total.astype(jnp.bfloat16)
 
     return (moe_out, attention_out)

time: 37.7 us -> 36.5 us (0.968)
  Pallas kernels: 10.8 us -> 5.4 us
  waiting for transfers between devices: 6.32 us -> 9.03 us
  starting transfers between devices: 17.1 us -> 18.6 us
    pallas_call x2 -> x0, Pallas kernels: 5.21 us -> none  [load(): pl.pallas_call(functools.partial(load_kernel, len(arrays), 1 + len(others...]
    ppermute x16 -> x17, waiting for transfers between devices: 6.32 us -> 9.03 us  [trade(): return lax.ppermute(value, 'node', list(enumerate(partners)))]
    ppermute x16 -> x17, starting transfers between devices: 17.1 us -> 18.6 us  [trade(): return lax.ppermute(value, 'node', list(enumerate(partners)))]
    unnamed x3 -> x9, local copies, waits for them, and re-layouts: 0.91 us -> 0.92 us
  transfers between devices with their start and end apart: 16 -> 17, of which waited for: 9 -> 8; matrix products, arithmetic and copies ran while one was open for 3% -> 3% of each run, Pallas kernels for 21% -> 8%
where the time goes in v4:
time: 36.5 us; the launch traced here: 36.3 us
  starting transfers between devices  18.6 us (51%)
  waiting for transfers between devices  9.03 us (25%)
  Pallas kernels  5.4 us (15%)
  between operations  1.39 us (4%)
  local copies, waits for them, and re-layouts  0.96 us (3%)
  other arithmetic  0.92 us (3%)
    ppermute x17, starting transfers between devices, trade(): return lax.ppermute(value, 'node', list(enumerate(partners)))  18.6 us
    ppermute x17, waiting for transfers between devices, trade(): return lax.ppermute(value, 'node', list(enumerate(partners)))  9.03 us
    pallas_call x1, Pallas kernels, attention(): pl.pallas_call(attention_kernel, out_shape=jax.ShapeDtypeStruct((1, heads...  2.74 us
    pallas_call x1, Pallas kernels, experts(): pl.pallas_call(functools.partial(experts_kernel, picks, count), out_shape...  1.78 us
    unnamed x9, local copies, waits for them, and re-layouts  0.92 us
    pallas_call x1, Pallas kernels, pack(): pl.pallas_call(pack_kernel, out_shape=jax.ShapeDtypeStruct((count, width...  0.88 us
  transfers between devices with their start and end apart: 17, of which 8 were waited for; matrix products, arithmetic and copies ran while one was open for 3% of the time, Pallas kernels for 8%

profile of v4, /device:TPU:0, one launch (start us, length us, event | category | flops | bytes accessed | tf_op | source)
XLA Modules:
  0.0 36.3 jit_solution(17163448695865140484)
XLA Ops:
  0.6 0.9 %pack.1 = bf16[4,7296]{1,0:T(4,128)(2,1)S(1)} custom-call(bf16[4,7168]{1,0:T(4,128)(2,1)} %tokens_hbm.1, s32[2,4]{1,0:T(2,128)} %bitcast.10, f32[2,4]{1,0:T(2,128)} %bitcast.11), custom_call_target="tpu_custom_call" | custom-call | tf_op jit(solution)/shard_map/pack/pallas_call | solution.py:71
  1.5 4.1 %collective-permute-start = (bf16[4,7296]{1,0:T(4,128)(2,1)S(1)}, bf16[4,7296]{1,0:T(4,128)(2,1)S(1)}, u32[]{:S(2)}, u32[]{:S(2)}) collective-permute-start(bf16[4,7296]{1,0:T(4,128)(2,1)S(1)} %pack.1), channel_id=1, source_target_pairs={{0,8},{1,9},{2,10},{3,11},{4,12},{5,13},{6,14},{7,15},{8,0},{9,1},... | collective-permute-start | bytes 175112 | tf_op jit(solution)/shard_map/ppermute | solution.py:30
  6.3 2.1 %collective-permute-done = bf16[4,7296]{1,0:T(4,128)(2,1)S(1)} collective-permute-done((bf16[4,7296]{1,0:T(4,128)(2,1)S(1)}, bf16[4,7296]{1,0:T(4,128)(2,1)S(1)}, u32[]{:S(2)}, u32[]{:S(2)}) %collective-permute-start) | collective-permute-done | bytes 58400 | tf_op jit(solution)/shard_map/ppermute | solution.py:30
  8.4 0.1 pad_maximum_fusion.after_ref.refs_0_
  8.5 2.4 %collective-permute-start.1 = (bf16[8,7296]{1,0:T(8,128)(2,1)S(1)}, bf16[8,7296]{1,0:T(8,128)(2,1)S(1)}, u32[]{:S(2)}, u32[]{:S(2)}) collective-permute-start(bf16[8,7296]{1,0:T(8,128)(2,1)S(1)} %pad_maximum_fusion.after_ref.refs_0_), channel_id=1, source_target_pairs={{0,6},{1,7},{2,4},{3,5},{4,2},{5,3},{6,0},{7,1},{8,14},{9,15},{10,... | collective-permute-start | bytes 350216 | tf_op jit(solution)/shard_map/ppermute | solution.py:30
  10.9 0.4 %collective-permute-start.2 = (bf16[8,7296]{1,0:T(8,128)(2,1)S(1)}, bf16[8,7296]{1,0:T(8,128)(2,1)S(1)}, u32[]{:S(2)}, u32[]{:S(2)}) collective-permute-start(bf16[8,7296]{1,0:T(8,128)(2,1)S(1)} %pad_maximum_fusion.after_ref.refs_0_), channel_id=1, source_target_pairs={{0,2},{1,5},{2,0},{3,7},{4,6},{5,1},{6,4},{7,3},{8,10},{9,13},{10,... | collective-permute-start | bytes 350216 | tf_op jit(solution)/shard_map/ppermute | solution.py:30
  11.3 1.0 %collective-permute-start.3 = (bf16[8,7296]{1,0:T(8,128)(2,1)S(1)}, bf16[8,7296]{1,0:T(8,128)(2,1)S(1)}, u32[]{:S(2)}, u32[]{:S(2)}) collective-permute-start(bf16[8,7296]{1,0:T(8,128)(2,1)S(1)} %pad_maximum_fusion.after_ref.refs_0_), channel_id=1, source_target_pairs={{0,4},{1,3},{2,6},{3,1},{4,0},{5,7},{6,2},{7,5},{8,12},{9,11},{10,... | collective-permute-start | bytes 350216 | tf_op jit(solution)/shard_map/ppermute | solution.py:30
  12.4 0.0 copy-start.3
  12.4 2.7 %attention.1.loaded_ref = bf16[1,128,512]{2,1,0:T(8,128)(2,1)S(1)} custom-call(bf16[8,7296]{1,0:T(8,128)(2,1)S(1)} %pad_maximum_fusion.after_ref.refs_0_, s32[1]{0:T(128)S(6)} %copy.13.lengths_ref, bf16[1,576,128]{2,1,0:T(8,128)(2,1)} %bitcast.13, bf16[1,576,1280]{2,1,0:T(8,128)(2,1)} %bitcast.12), custom_call_target="tpu_custom_call" | custom-call | flops 4000000000 | bytes 1700000 | tf_op jit(solution)/shard_map/attention/pallas_call | solution.py:116
  15.1 0.0 collective-permute-done.1.refs_3_
  15.1 0.6 %collective-permute-start.7 = (bf16[8,7296]{1,0:T(8,128)(2,1)S(1)}, bf16[8,7296]{1,0:T(8,128)(2,1)S(1)}, u32[]{:S(2)}, u32[]{:S(2)}) collective-permute-start(bf16[8,7296]{1,0:T(8,128)(2,1)S(1)} %collective-permute-done.1.refs_3_), channel_id=1, source_target_pairs={{0,1},{1,0},{2,3},{3,2},{4,5},{5,4},{6,7},{7,6},{8,9},{9,8},{10,11... | collective-permute-start | bytes 350216 | tf_op jit(solution)/shard_map/ppermute | solution.py:30
  15.7 0.1 collective-permute-start.5
  15.8 0.6 %collective-permute-done.3.refs_2_ = bf16[8,7296]{1,0:T(8,128)(2,1)S(1)} collective-permute-done((bf16[8,7296]{1,0:T(8,128)(2,1)S(1)}, bf16[8,7296]{1,0:T(8,128)(2,1)S(1)}, u32[]{:S(2)}, u32[]{:S(2)}) %collective-permute-start.3) | collective-permute-done | bytes 116768 | tf_op jit(solution)/shard_map/ppermute | solution.py:30
  16.4 0.2 collective-permute-done.7.refs_7_
  16.7 0.4 collective-permute-done.5.refs_5_
  17.0 0.7 %collective-permute-done.6.refs_6_ = bf16[8,7296]{1,0:T(8,128)(2,1)S(1)} collective-permute-done((bf16[8,7296]{1,0:T(8,128)(2,1)S(1)}, bf16[8,7296]{1,0:T(8,128)(2,1)S(1)}, u32[]{:S(2)}, u32[]{:S(2)}) %collective-permute-start.6) | collective-permute-done | bytes 116768 | tf_op jit(solution)/shard_map/ppermute | solution.py:30
  17.8 1.8 %experts.1 = (f32[8,7168]{1,0:T(8,128)S(1)}, f32[8,7168]{1,0:T(8,128)S(1)}, f32[8,7168]{1,0:T(8,128)S(1)}, f32[8,7168]{1,0:T(8,128)S(1)}, bf16[8,7168]{1,0:T(8,1...) custom-call(bf16[1,128,512]{2,1,0:T(8,128)(2,1)S(1)} %attention.1.loaded_ref, ...), custom_call_target="tpu_custom_call" | custom-call | tf_op jit(solution)/shard_map/experts/pallas_call | solution.py:185
  19.6 0.2 collective-permute-start.9
  19.8 0.4 %collective-permute-start.13 = (bf16[8,7168]{1,0:T(8,128)(2,1)S(1)}, bf16[8,7168]{1,0:T(8,128)(2,1)S(1)}, u32[]{:S(2)}, u32[]{:S(2)}) collective-permute-start(bf16[8,7168]{1,0:T(8,128)(2,1)S(1)} %get-tuple-element.23), channel_id=1, source_target_pairs={{0,1},{1,0},{2,3},{3,2},{4,5},{5,4},{6,7},{7,6},{8,9},{9,8},{10,11... | collective-permute-start | bytes 344072 | tf_op jit(solution)/shard_map/ppermute | solution.py:30
  20.1 0.1 collective-permute-start.11
  20.3 0.4 %collective-permute-start.8 = (bf16[8,7168]{1,0:T(8,128)(2,1)S(1)}, bf16[8,7168]{1,0:T(8,128)(2,1)S(1)}, u32[]{:S(2)}, u32[]{:S(2)}) collective-permute-start(bf16[8,7168]{1,0:T(8,128)(2,1)S(1)} %get-tuple-element.17), channel_id=1, source_target_pairs={{0,1},{1,0},{2,3},{3,2},{4,5},{5,4},{6,7},{7,6},{8,9},{9,8},{10,11... | collective-permute-start | bytes 344072 | tf_op jit(solution)/shard_map/ppermute | solution.py:30
  20.6 0.3 collective-permute-done.9
  21.0 1.5 %collective-permute-start.10 = (bf16[8,7168]{1,0:T(8,128)(2,1)S(1)}, bf16[8,7168]{1,0:T(8,128)(2,1)S(1)}, u32[]{:S(2)}, u32[]{:S(2)}) collective-permute-start(bf16[8,7168]{1,0:T(8,128)(2,1)S(1)} %add_convert_fusion.2), channel_id=1, source_target_pairs={{0,2},{1,5},{2,0},{3,7},{4,6},{5,1},{6,4},{7,3},{8,10},{9,13},{10,... | collective-permute-start | bytes 344072 | tf_op jit(solution)/shard_map/ppermute | solution.py:30
  22.5 1.4 %collective-permute-start.12 = (bf16[8,7168]{1,0:T(8,128)(2,1)S(1)}, bf16[8,7168]{1,0:T(8,128)(2,1)S(1)}, u32[]{:S(2)}, u32[]{:S(2)}) collective-permute-start(bf16[8,7168]{1,0:T(8,128)(2,1)S(1)} %add_convert_fusion.1), channel_id=1, source_target_pairs={{0,4},{1,3},{2,6},{3,1},{4,0},{5,7},{6,2},{7,5},{8,12},{9,11},{10,... | collective-permute-start | bytes 344072 | tf_op jit(solution)/shard_map/ppermute | solution.py:30
  24.0 0.8 %collective-permute-start.15 = (bf16[4,7168]{1,0:T(4,128)(2,1)S(1)}, bf16[4,7168]{1,0:T(4,128)(2,1)S(1)}, u32[]{:S(2)}, u32[]{:S(2)}) collective-permute-start(bf16[4,7168]{1,0:T(4,128)(2,1)S(1)} %get-tuple-element.27), channel_id=1, source_target_pairs={{0,6},{1,7},{2,4},{3,5},{4,2},{5,3},{6,0},{7,1},{8,14},{9,15},{10,... | collective-permute-start | bytes 172040 | tf_op jit(solution)/shard_map/ppermute | solution.py:30
  24.8 0.9 %copy.12 = bf16[1,1,128,512]{3,1,2,0:T(2,128)(2,1)} copy(bf16[1,1,128,512]{3,2,1,0:T(8,128)(2,1)S(1)} %bitcast.7) | data formatting | bytes 262144
  25.7 2.2 %collective-permute-start.14 = (bf16[4,7168]{1,0:T(4,128)(2,1)S(1)}, bf16[4,7168]{1,0:T(4,128)(2,1)S(1)}, u32[]{:S(2)}, u32[]{:S(2)}) collective-permute-start(bf16[4,7168]{1,0:T(4,128)(2,1)S(1)} %get-tuple-element.26), channel_id=1, source_target_pairs={{0,6},{1,7},{2,4},{3,5},{4,2},{5,3},{6,0},{7,1},{8,14},{9,15},{10,... | collective-permute-start | bytes 172040 | tf_op jit(solution)/shard_map/ppermute | solution.py:30
  27.9 1.8 %collective-permute-done.15 = bf16[4,7168]{1,0:T(4,128)(2,1)S(1)} collective-permute-done((bf16[4,7168]{1,0:T(4,128)(2,1)S(1)}, bf16[4,7168]{1,0:T(4,128)(2,1)S(1)}, u32[]{:S(2)}, u32[]{:S(2)}) %collective-permute-start.15) | collective-permute-done | bytes 57376 | tf_op jit(solution)/shard_map/ppermute | solution.py:30
  29.7 0.1 convert_add_fusion
  29.8 3.0 %collective-permute-start.16 = (bf16[4,7168]{1,0:T(4,128)(2,1)S(1)}, bf16[4,7168]{1,0:T(4,128)(2,1)S(1)}, u32[]{:S(2)}, u32[]{:S(2)}) collective-permute-start(bf16[4,7168]{1,0:T(4,128)(2,1)S(1)} %fusion), channel_id=1, source_target_pairs={{0,8},{1,9},{2,10},{3,11},{4,12},{5,13},{6,14},{7,15},{8,0},{9,1},... | collective-permute-start | bytes 172040 | tf_op jit(solution)/shard_map/ppermute | solution.py:30
  32.9 2.8 %collective-permute-done.16 = bf16[4,7168]{1,0:T(4,128)(2,1)S(1)} collective-permute-done((bf16[4,7168]{1,0:T(4,128)(2,1)S(1)}, bf16[4,7168]{1,0:T(4,128)(2,1)S(1)}, u32[]{:S(2)}, u32[]{:S(2)}) %collective-permute-start.16) | collective-permute-done | bytes 57376 | tf_op jit(solution)/shard_map/ppermute | solution.py:30
  35.7 0.7 %fusion.2 = bf16[4,7168]{1,0:T(4,128)(2,1)} fusion(f32[8,7168]{1,0:T(8,128)S(1)} %convert_add_fusion, bf16[4,7168]{1,0:T(4,128)(2,1)S(1)} %collective-permute-done.16, bf16[4,7168]{1,0:T(4,128)(2,1)S(1)} %collective-permute-done.14), kind=kLoop, calls=%fused_computation.9 | loop fusion | flops 143360 | bytes 286720 | tf_op jit(solution)/shard_map/convert_element_type | solution.py:231
  (22 shorter events, 0.2 us)
Async XLA Ops:
  1.5 6.9 %collective-permute-start = (bf16[4,7296]{1,0:T(4,128)(2,1)S(1)}, bf16[4,7296]{1,0:T(4,128)(2,1)S(1)}, u32[]{:S(2)}, u32[]{:S(2)}) collective-permute-start(bf16[4,7296]{1,0:T(4,128)(2,1)S(1)} %pack.1), channel_id=1, source_target_pairs={{0,8},{1,9},{2,10},{3,11},{4,12},{5,13},{6,14},{7,15},{8,0},{9,1},... | collective-permute-start | bytes 175112 | tf_op jit(solution)/shard_map/ppermute | solution.py:30
  8.5 6.6 %collective-permute-start.1 = (bf16[8,7296]{1,0:T(8,128)(2,1)S(1)}, bf16[8,7296]{1,0:T(8,128)(2,1)S(1)}, u32[]{:S(2)}, u32[]{:S(2)}) collective-permute-start(bf16[8,7296]{1,0:T(8,128)(2,1)S(1)} %pad_maximum_fusion.after_ref.refs_0_), channel_id=1, source_target_pairs={{0,6},{1,7},{2,4},{3,5},{4,2},{5,3},{6,0},{7,1},{8,14},{9,15},{10,... | collective-permute-start | bytes 350216 | tf_op jit(solution)/shard_map/ppermute | solution.py:30
  10.9 4.8 %collective-permute-start.2 = (bf16[8,7296]{1,0:T(8,128)(2,1)S(1)}, bf16[8,7296]{1,0:T(8,128)(2,1)S(1)}, u32[]{:S(2)}, u32[]{:S(2)}) collective-permute-start(bf16[8,7296]{1,0:T(8,128)(2,1)S(1)} %pad_maximum_fusion.after_ref.refs_0_), channel_id=1, source_target_pairs={{0,2},{1,5},{2,0},{3,7},{4,6},{5,1},{6,4},{7,3},{8,10},{9,13},{10,... | collective-permute-start | bytes 350216 | tf_op jit(solution)/shard_map/ppermute | solution.py:30
  11.3 5.1 %collective-permute-start.3 = (bf16[8,7296]{1,0:T(8,128)(2,1)S(1)}, bf16[8,7296]{1,0:T(8,128)(2,1)S(1)}, u32[]{:S(2)}, u32[]{:S(2)}) collective-permute-start(bf16[8,7296]{1,0:T(8,128)(2,1)S(1)} %pad_maximum_fusion.after_ref.refs_0_), channel_id=1, source_target_pairs={{0,4},{1,3},{2,6},{3,1},{4,0},{5,7},{6,2},{7,5},{8,12},{9,11},{10,... | collective-permute-start | bytes 350216 | tf_op jit(solution)/shard_map/ppermute | solution.py:30
  12.3 4.1 %collective-permute-start.4 = (bf16[8,7296]{1,0:T(8,128)(2,1)S(1)}, bf16[8,7296]{1,0:T(8,128)(2,1)S(1)}, u32[]{:S(2)}, u32[]{:S(2)}) collective-permute-start(bf16[8,7296]{1,0:T(8,128)(2,1)S(1)} %pad_maximum_fusion.after_ref.refs_0_), channel_id=1, source_target_pairs={{0,1},{1,0},{2,3},{3,2},{4,5},{5,4},{6,7},{7,6},{8,9},{9,8},{10,11... | collective-permute-start | bytes 350216 | tf_op jit(solution)/shard_map/ppermute | solution.py:30
  12.3 5.4 %copy-start = (bf16[1,7168,256]{2,1,0:T(8,128)(2,1)S(1)}, bf16[1,7168,256]{2,1,0:T(8,128)(2,1)}, u32[]{:S(2)}) copy-start(bf16[1,7168,256]{2,1,0:T(8,128)(2,1)} %refs_9_.1) | copy-start | bytes 11010052
  12.3 5.4 %copy-start.1 = (bf16[1,7168,256]{2,1,0:T(8,128)(2,1)S(1)}, bf16[1,7168,256]{2,1,0:T(8,128)(2,1)}, u32[]{:S(2)}) copy-start(bf16[1,7168,256]{2,1,0:T(8,128)(2,1)} %refs_10_.1) | copy-start | bytes 11010052
  12.3 5.4 %copy-start.2 = (bf16[1,256,7168]{2,1,0:T(8,128)(2,1)S(1)}, bf16[1,256,7168]{2,1,0:T(8,128)(2,1)}, u32[]{:S(2)}) copy-start(bf16[1,256,7168]{2,1,0:T(8,128)(2,1)} %refs_11_.1) | copy-start | bytes 11010052
  12.4 5.4 %copy-start.3 = (bf16[7168]{0:T(1024)(128)(2,1)S(1)}, bf16[7168]{0:T(1024)(128)(2,1)}, u32[]{:S(2)}) copy-start(bf16[7168]{0:T(1024)(128)(2,1)} %param.13) | copy-start | bytes 43012
  15.1 1.5 %collective-permute-start.7 = (bf16[8,7296]{1,0:T(8,128)(2,1)S(1)}, bf16[8,7296]{1,0:T(8,128)(2,1)S(1)}, u32[]{:S(2)}, u32[]{:S(2)}) collective-permute-start(bf16[8,7296]{1,0:T(8,128)(2,1)S(1)} %collective-permute-done.1.refs_3_), channel_id=1, source_target_pairs={{0,1},{1,0},{2,3},{3,2},{4,5},{5,4},{6,7},{7,6},{8,9},{9,8},{10,11... | collective-permute-start | bytes 350216 | tf_op jit(solution)/shard_map/ppermute | solution.py:30
  15.7 1.3 %collective-permute-start.5 = (bf16[8,7296]{1,0:T(8,128)(2,1)S(1)}, bf16[8,7296]{1,0:T(8,128)(2,1)S(1)}, u32[]{:S(2)}, u32[]{:S(2)}) collective-permute-start(bf16[8,7296]{1,0:T(8,128)(2,1)S(1)} %collective-permute-done.2.refs_1_), channel_id=1, source_target_pairs={{0,1},{1,0},{2,3},{3,2},{4,5},{5,4},{6,7},{7,6},{8,9},{9,8},{10,11... | collective-permute-start | bytes 350216 | tf_op jit(solution)/shard_map/ppermute | solution.py:30
  16.4 1.3 %collective-permute-start.6 = (bf16[8,7296]{1,0:T(8,128)(2,1)S(1)}, bf16[8,7296]{1,0:T(8,128)(2,1)S(1)}, u32[]{:S(2)}, u32[]{:S(2)}) collective-permute-start(bf16[8,7296]{1,0:T(8,128)(2,1)S(1)} %collective-permute-done.3.refs_2_), channel_id=1, source_target_pairs={{0,1},{1,0},{2,3},{3,2},{4,5},{5,4},{6,7},{7,6},{8,9},{9,8},{10,11... | collective-permute-start | bytes 350216 | tf_op jit(solution)/shard_map/ppermute | solution.py:30
  19.6 1.4 %collective-permute-start.9 = (bf16[8,7168]{1,0:T(8,128)(2,1)S(1)}, bf16[8,7168]{1,0:T(8,128)(2,1)S(1)}, u32[]{:S(2)}, u32[]{:S(2)}) collective-permute-start(bf16[8,7168]{1,0:T(8,128)(2,1)S(1)} %get-tuple-element.19), channel_id=1, source_target_pairs={{0,1},{1,0},{2,3},{3,2},{4,5},{5,4},{6,7},{7,6},{8,9},{9,8},{10,11... | collective-permute-start | bytes 344072 | tf_op jit(solution)/shard_map/ppermute | solution.py:30
  19.8 4.1 %collective-permute-start.13 = (bf16[8,7168]{1,0:T(8,128)(2,1)S(1)}, bf16[8,7168]{1,0:T(8,128)(2,1)S(1)}, u32[]{:S(2)}, u32[]{:S(2)}) collective-permute-start(bf16[8,7168]{1,0:T(8,128)(2,1)S(1)} %get-tuple-element.23), channel_id=1, source_target_pairs={{0,1},{1,0},{2,3},{3,2},{4,5},{5,4},{6,7},{7,6},{8,9},{9,8},{10,11... | collective-permute-start | bytes 344072 | tf_op jit(solution)/shard_map/ppermute | solution.py:30
  20.1 2.4 %collective-permute-start.11 = (bf16[8,7168]{1,0:T(8,128)(2,1)S(1)}, bf16[8,7168]{1,0:T(8,128)(2,1)S(1)}, u32[]{:S(2)}, u32[]{:S(2)}) collective-permute-start(bf16[8,7168]{1,0:T(8,128)(2,1)S(1)} %get-tuple-element.21), channel_id=1, source_target_pairs={{0,1},{1,0},{2,3},{3,2},{4,5},{5,4},{6,7},{7,6},{8,9},{9,8},{10,11... | collective-permute-start | bytes 344072 | tf_op jit(solution)/shard_map/ppermute | solution.py:30
  20.3 9.5 %collective-permute-start.8 = (bf16[8,7168]{1,0:T(8,128)(2,1)S(1)}, bf16[8,7168]{1,0:T(8,128)(2,1)S(1)}, u32[]{:S(2)}, u32[]{:S(2)}) collective-permute-start(bf16[8,7168]{1,0:T(8,128)(2,1)S(1)} %get-tuple-element.17), channel_id=1, source_target_pairs={{0,1},{1,0},{2,3},{3,2},{4,5},{5,4},{6,7},{7,6},{8,9},{9,8},{10,11... | collective-permute-start | bytes 344072 | tf_op jit(solution)/shard_map/ppermute | solution.py:30
  21.0 8.8 %collective-permute-start.10 = (bf16[8,7168]{1,0:T(8,128)(2,1)S(1)}, bf16[8,7168]{1,0:T(8,128)(2,1)S(1)}, u32[]{:S(2)}, u32[]{:S(2)}) collective-permute-start(bf16[8,7168]{1,0:T(8,128)(2,1)S(1)} %add_convert_fusion.2), channel_id=1, source_target_pairs={{0,2},{1,5},{2,0},{3,7},{4,6},{5,1},{6,4},{7,3},{8,10},{9,13},{10,... | collective-permute-start | bytes 344072 | tf_op jit(solution)/shard_map/ppermute | solution.py:30
  22.5 7.2 %collective-permute-start.12 = (bf16[8,7168]{1,0:T(8,128)(2,1)S(1)}, bf16[8,7168]{1,0:T(8,128)(2,1)S(1)}, u32[]{:S(2)}, u32[]{:S(2)}) collective-permute-start(bf16[8,7168]{1,0:T(8,128)(2,1)S(1)} %add_convert_fusion.1), channel_id=1, source_target_pairs={{0,4},{1,3},{2,6},{3,1},{4,0},{5,7},{6,2},{7,5},{8,12},{9,11},{10,... | collective-permute-start | bytes 344072 | tf_op jit(solution)/shard_map/ppermute | solution.py:30
  24.0 5.7 %collective-permute-start.15 = (bf16[4,7168]{1,0:T(4,128)(2,1)S(1)}, bf16[4,7168]{1,0:T(4,128)(2,1)S(1)}, u32[]{:S(2)}, u32[]{:S(2)}) collective-permute-start(bf16[4,7168]{1,0:T(4,128)(2,1)S(1)} %get-tuple-element.27), channel_id=1, source_target_pairs={{0,6},{1,7},{2,4},{3,5},{4,2},{5,3},{6,0},{7,1},{8,14},{9,15},{10,... | collective-permute-start | bytes 172040 | tf_op jit(solution)/shard_map/ppermute | solution.py:30
  25.7 7.2 %collective-permute-start.14 = (bf16[4,7168]{1,0:T(4,128)(2,1)S(1)}, bf16[4,7168]{1,0:T(4,128)(2,1)S(1)}, u32[]{:S(2)}, u32[]{:S(2)}) collective-permute-start(bf16[4,7168]{1,0:T(4,128)(2,1)S(1)} %get-tuple-element.26), channel_id=1, source_target_pairs={{0,6},{1,7},{2,4},{3,5},{4,2},{5,3},{6,0},{7,1},{8,14},{9,15},{10,... | collective-permute-start | bytes 172040 | tf_op jit(solution)/shard_map/ppermute | solution.py:30
  29.8 5.8 %collective-permute-start.16 = (bf16[4,7168]{1,0:T(4,128)(2,1)S(1)}, bf16[4,7168]{1,0:T(4,128)(2,1)S(1)}, u32[]{:S(2)}, u32[]{:S(2)}) collective-permute-start(bf16[4,7168]{1,0:T(4,128)(2,1)S(1)} %fusion), channel_id=1, source_target_pairs={{0,8},{1,9},{2,10},{3,11},{4,12},{5,13},{6,14},{7,15},{8,0},{9,1},... | collective-permute-start | bytes 172040 | tf_op jit(solution)/shard_map/ppermute | solution.py:30

commit v5 on v4

--- a/solution.py
+++ b/solution.py
@@ -199,12 +199,16 @@
     gain = norm_gain.reshape(-1, LANES)
 
     rows = pack(tokens, routes, gates)
-    for partners in far:
+    for partners in far[:-1]:
         rows = jnp.concatenate([rows, trade(rows, partners)], axis=0)
+    arrived = trade(rows, far[-1])
+    diagonal = trade(rows, near[2])
+    rows = jnp.concatenate([rows, arrived], axis=0)
     attended = attention(rows, lengths, queries, cache)
     weights = (w_gate, w_up, w_down)
-    pieces = [rows] + [trade(rows, partners) for partners in near]
-    pieces[-1], attended = lax.optimization_barrier((pieces[-1], attended))
+    pieces = [rows] + [trade(rows, partners) for partners in near[:2]]
+    pieces[1], attended = lax.optimization_barrier((pieces[1], attended))
+    pieces.append(jnp.concatenate([diagonal, trade(arrived, near[2])], axis=0))
     pieces += [trade(piece, core) for piece in pieces]
 
     outputs = experts(attended, pieces, routes.shape[1], gain, weights)

time: 36.5 us -> 35.9 us (0.984)
  waiting for transfers between devices: 9.03 us -> 6.7 us
  starting transfers between devices: 18.6 us -> 20.3 us
    ppermute x17 -> x18, waiting for transfers between devices: 9.03 us -> 6.7 us  [trade(): return lax.ppermute(value, 'node', list(enumerate(partners)))]
    ppermute x17 -> x18, starting transfers between devices: 18.6 us -> 20.3 us  [trade(): return lax.ppermute(value, 'node', list(enumerate(partners)))]
  transfers between devices with their start and end apart: 17 -> 18, of which waited for: 8 -> 7; matrix products, arithmetic and copies ran while one was open for 3% -> 4% of each run, Pallas kernels for 8% -> 8%
where the time goes in v5:
time: 35.9 us; the launch traced here: 35.7 us
  starting transfers between devices  20.3 us (57%)
  waiting for transfers between devices  6.7 us (19%)
  Pallas kernels  5.4 us (15%)
  between operations  1.41 us (4%)
  other arithmetic  0.99 us (3%)
  local copies, waits for them, and re-layouts  0.96 us (3%)
    ppermute x18, starting transfers between devices, trade(): return lax.ppermute(value, 'node', list(enumerate(partners)))  20.3 us
    ppermute x18, waiting for transfers between devices, trade(): return lax.ppermute(value, 'node', list(enumerate(partners)))  6.7 us
    pallas_call x1, Pallas kernels, attention(): pl.pallas_call(attention_kernel, out_shape=jax.ShapeDtypeStruct((1, heads...  2.75 us
    pallas_call x1, Pallas kernels, experts(): pl.pallas_call(functools.partial(experts_kernel, picks, count), out_shape...  1.78 us
    unnamed x9, local copies, waits for them, and re-layouts  0.92 us
    pallas_call x1, Pallas kernels, pack(): pl.pallas_call(pack_kernel, out_shape=jax.ShapeDtypeStruct((count, width...  0.88 us
  transfers between devices with their start and end apart: 18, of which 7 were waited for; matrix products, arithmetic and copies ran while one was open for 4% of the time, Pallas kernels for 8%

profile of v5, /device:TPU:0, one launch (start us, length us, event | category | flops | bytes accessed | tf_op | source)
XLA Modules:
  0.0 35.7 jit_solution(6860121807914369128)
XLA Ops:
  0.6 0.9 %pack.1 = bf16[4,7296]{1,0:T(4,128)(2,1)S(1)} custom-call(bf16[4,7168]{1,0:T(4,128)(2,1)} %tokens_hbm.1, s32[2,4]{1,0:T(2,128)} %bitcast.10, f32[2,4]{1,0:T(2,128)} %bitcast.11), custom_call_target="tpu_custom_call" | custom-call | tf_op jit(solution)/shard_map/pack/pallas_call | solution.py:71
  1.5 4.1 %collective-permute-start = (bf16[4,7296]{1,0:T(4,128)(2,1)S(1)}, bf16[4,7296]{1,0:T(4,128)(2,1)S(1)}, u32[]{:S(2)}, u32[]{:S(2)}) collective-permute-start(bf16[4,7296]{1,0:T(4,128)(2,1)S(1)} %pack.1), channel_id=1, source_target_pairs={{0,8},{1,9},{2,10},{3,11},{4,12},{5,13},{6,14},{7,15},{8,0},{9,1},... | collective-permute-start | bytes 175112 | tf_op jit(solution)/shard_map/ppermute | solution.py:30
  5.6 2.5 %collective-permute-start.3 = (bf16[4,7296]{1,0:T(4,128)(2,1)S(1)}, bf16[4,7296]{1,0:T(4,128)(2,1)S(1)}, u32[]{:S(2)}, u32[]{:S(2)}) collective-permute-start(bf16[4,7296]{1,0:T(4,128)(2,1)S(1)} %pack.1), channel_id=1, source_target_pairs={{0,6},{1,7},{2,4},{3,5},{4,2},{5,3},{6,0},{7,1},{8,14},{9,15},{10,... | collective-permute-start | bytes 175112 | tf_op jit(solution)/shard_map/ppermute | solution.py:30
  8.8 0.1 pad_maximum_fusion.after_ref.refs_0_
  8.9 1.5 %collective-permute-start.1 = (bf16[8,7296]{1,0:T(8,128)(2,1)S(1)}, bf16[8,7296]{1,0:T(8,128)(2,1)S(1)}, u32[]{:S(2)}, u32[]{:S(2)}) collective-permute-start(bf16[8,7296]{1,0:T(8,128)(2,1)S(1)} %pad_maximum_fusion.after_ref.refs_0_), channel_id=1, source_target_pairs={{0,2},{1,5},{2,0},{3,7},{4,6},{5,1},{6,4},{7,3},{8,10},{9,13},{10,... | collective-permute-start | bytes 350216 | tf_op jit(solution)/shard_map/ppermute | solution.py:30
  10.3 1.1 %collective-permute-start.2 = (bf16[8,7296]{1,0:T(8,128)(2,1)S(1)}, bf16[8,7296]{1,0:T(8,128)(2,1)S(1)}, u32[]{:S(2)}, u32[]{:S(2)}) collective-permute-start(bf16[8,7296]{1,0:T(8,128)(2,1)S(1)} %pad_maximum_fusion.after_ref.refs_0_), channel_id=1, source_target_pairs={{0,4},{1,3},{2,6},{3,1},{4,0},{5,7},{6,2},{7,5},{8,12},{9,11},{10,... | collective-permute-start | bytes 350216 | tf_op jit(solution)/shard_map/ppermute | solution.py:30
  11.4 1.0 %collective-permute-start.4 = (bf16[4,7296]{1,0:T(4,128)(2,1)S(1)}, bf16[4,7296]{1,0:T(4,128)(2,1)S(1)}, u32[]{:S(2)}, u32[]{:S(2)}) collective-permute-start(bf16[4,7296]{1,0:T(4,128)(2,1)S(1)} %collective-permute-done), channel_id=1, source_target_pairs={{0,6},{1,7},{2,4},{3,5},{4,2},{5,3},{6,0},{7,1},{8,14},{9,15},{10,... | collective-permute-start | bytes 175112 | tf_op jit(solution)/shard_map/ppermute | solution.py:30
  12.4 2.7 %attention.1.loaded_ref = bf16[1,128,512]{2,1,0:T(8,128)(2,1)S(1)} custom-call(bf16[8,7296]{1,0:T(8,128)(2,1)S(1)} %pad_maximum_fusion.after_ref.refs_0_, s32[1]{0:T(128)S(6)} %copy.13.lengths_ref, bf16[1,576,128]{2,1,0:T(8,128)(2,1)} %bitcast.13, bf16[1,576,1280]{2,1,0:T(8,128)(2,1)} %bitcast.12), custom_call_target="tpu_custom_call" | custom-call | flops 4000000000 | bytes 1700000 | tf_op jit(solution)/shard_map/attention/pallas_call | solution.py:116
  15.2 1.5 %collective-permute-done.4 = bf16[4,7296]{1,0:T(4,128)(2,1)S(1)} collective-permute-done((bf16[4,7296]{1,0:T(4,128)(2,1)S(1)}, bf16[4,7296]{1,0:T(4,128)(2,1)S(1)}, u32[]{:S(2)}, u32[]{:S(2)}) %collective-permute-start.4) | collective-permute-done | bytes 58400 | tf_op jit(solution)/shard_map/ppermute | solution.py:30
  16.7 0.1 pad_maximum_fusion.1.refs_3_
  16.8 0.1 collective-permute-start.8
  16.8 0.5 %collective-permute-start.6 = (bf16[8,7296]{1,0:T(8,128)(2,1)S(1)}, bf16[8,7296]{1,0:T(8,128)(2,1)S(1)}, u32[]{:S(2)}, u32[]{:S(2)}) collective-permute-start(bf16[8,7296]{1,0:T(8,128)(2,1)S(1)} %collective-permute-done.1.refs_1_), channel_id=1, source_target_pairs={{0,1},{1,0},{2,3},{3,2},{4,5},{5,4},{6,7},{7,6},{8,9},{9,8},{10,11... | collective-permute-start | bytes 350216 | tf_op jit(solution)/shard_map/ppermute | solution.py:30
  17.3 0.1 collective-permute-start.7
  17.4 0.7 %collective-permute-done.8.refs_7_ = bf16[8,7296]{1,0:T(8,128)(2,1)S(1)} collective-permute-done((bf16[8,7296]{1,0:T(8,128)(2,1)S(1)}, bf16[8,7296]{1,0:T(8,128)(2,1)S(1)}, u32[]{:S(2)}, u32[]{:S(2)}) %collective-permute-start.8) | collective-permute-done | bytes 116768 | tf_op jit(solution)/shard_map/ppermute | solution.py:30
  18.1 0.2 collective-permute-done.6.refs_5_
  18.3 0.4 collective-permute-done.7.refs_6_
  18.7 1.8 %experts.1 = (f32[8,7168]{1,0:T(8,128)S(1)}, f32[8,7168]{1,0:T(8,128)S(1)}, f32[8,7168]{1,0:T(8,128)S(1)}, f32[8,7168]{1,0:T(8,128)S(1)}, bf16[8,7168]{1,0:T(8,1...) custom-call(bf16[1,128,512]{2,1,0:T(8,128)(2,1)S(1)} %attention.1.loaded_ref, ...), custom_call_target="tpu_custom_call" | custom-call | tf_op jit(solution)/shard_map/experts/pallas_call | solution.py:185
  20.5 0.2 collective-permute-start.10
  20.7 0.3 collective-permute-start.14
  21.0 0.2 collective-permute-start.12
  21.2 0.3 collective-permute-start.9
  21.6 0.3 collective-permute-done.10
  21.9 1.3 %collective-permute-start.11 = (bf16[8,7168]{1,0:T(8,128)(2,1)S(1)}, bf16[8,7168]{1,0:T(8,128)(2,1)S(1)}, u32[]{:S(2)}, u32[]{:S(2)}) collective-permute-start(bf16[8,7168]{1,0:T(8,128)(2,1)S(1)} %add_convert_fusion.2), channel_id=1, source_target_pairs={{0,2},{1,5},{2,0},{3,7},{4,6},{5,1},{6,4},{7,3},{8,10},{9,13},{10,... | collective-permute-start | bytes 344072 | tf_op jit(solution)/shard_map/ppermute | solution.py:30
  23.2 1.2 %collective-permute-start.13 = (bf16[8,7168]{1,0:T(8,128)(2,1)S(1)}, bf16[8,7168]{1,0:T(8,128)(2,1)S(1)}, u32[]{:S(2)}, u32[]{:S(2)}) collective-permute-start(bf16[8,7168]{1,0:T(8,128)(2,1)S(1)} %add_convert_fusion.1), channel_id=1, source_target_pairs={{0,4},{1,3},{2,6},{3,1},{4,0},{5,7},{6,2},{7,5},{8,12},{9,11},{10,... | collective-permute-start | bytes 344072 | tf_op jit(solution)/shard_map/ppermute | solution.py:30
  24.4 1.3 %collective-permute-start.16 = (bf16[4,7168]{1,0:T(4,128)(2,1)S(1)}, bf16[4,7168]{1,0:T(4,128)(2,1)S(1)}, u32[]{:S(2)}, u32[]{:S(2)}) collective-permute-start(bf16[4,7168]{1,0:T(4,128)(2,1)S(1)} %get-tuple-element.27), channel_id=1, source_target_pairs={{0,6},{1,7},{2,4},{3,5},{4,2},{5,3},{6,0},{7,1},{8,14},{9,15},{10,... | collective-permute-start | bytes 172040 | tf_op jit(solution)/shard_map/ppermute | solution.py:30
  25.7 0.9 %copy.12 = bf16[1,1,128,512]{3,1,2,0:T(2,128)(2,1)} copy(bf16[1,1,128,512]{3,2,1,0:T(8,128)(2,1)S(1)} %bitcast.7) | data formatting | bytes 262144
  26.6 1.7 %collective-permute-start.15 = (bf16[4,7168]{1,0:T(4,128)(2,1)S(1)}, bf16[4,7168]{1,0:T(4,128)(2,1)S(1)}, u32[]{:S(2)}, u32[]{:S(2)}) collective-permute-start(bf16[4,7168]{1,0:T(4,128)(2,1)S(1)} %get-tuple-element.26), channel_id=1, source_target_pairs={{0,6},{1,7},{2,4},{3,5},{4,2},{5,3},{6,0},{7,1},{8,14},{9,15},{10,... | collective-permute-start | bytes 172040 | tf_op jit(solution)/shard_map/ppermute | solution.py:30
  28.3 1.5 %collective-permute-done.16 = bf16[4,7168]{1,0:T(4,128)(2,1)S(1)} collective-permute-done((bf16[4,7168]{1,0:T(4,128)(2,1)S(1)}, bf16[4,7168]{1,0:T(4,128)(2,1)S(1)}, u32[]{:S(2)}, u32[]{:S(2)}) %collective-permute-start.16) | collective-permute-done | bytes 57376 | tf_op jit(solution)/shard_map/ppermute | solution.py:30
  29.8 0.1 convert_add_fusion
  29.9 3.0 %collective-permute-start.17 = (bf16[4,7168]{1,0:T(4,128)(2,1)S(1)}, bf16[4,7168]{1,0:T(4,128)(2,1)S(1)}, u32[]{:S(2)}, u32[]{:S(2)}) collective-permute-start(bf16[4,7168]{1,0:T(4,128)(2,1)S(1)} %fusion), channel_id=1, source_target_pairs={{0,8},{1,9},{2,10},{3,11},{4,12},{5,13},{6,14},{7,15},{8,0},{9,1},... | collective-permute-start | bytes 172040 | tf_op jit(solution)/shard_map/ppermute | solution.py:30
  32.9 2.2 %collective-permute-done.17 = bf16[4,7168]{1,0:T(4,128)(2,1)S(1)} collective-permute-done((bf16[4,7168]{1,0:T(4,128)(2,1)S(1)}, bf16[4,7168]{1,0:T(4,128)(2,1)S(1)}, u32[]{:S(2)}, u32[]{:S(2)}) %collective-permute-start.17) | collective-permute-done | bytes 57376 | tf_op jit(solution)/shard_map/ppermute | solution.py:30
  35.1 0.7 %fusion.2 = bf16[4,7168]{1,0:T(4,128)(2,1)} fusion(f32[8,7168]{1,0:T(8,128)S(1)} %convert_add_fusion, bf16[4,7168]{1,0:T(4,128)(2,1)S(1)} %collective-permute-done.17, bf16[4,7168]{1,0:T(4,128)(2,1)S(1)} %collective-permute-done.15), kind=kLoop, calls=%fused_computation.10 | loop fusion | flops 143360 | bytes 286720 | tf_op jit(solution)/shard_map/convert_element_type | solution.py:235
  (25 shorter events, 0.2 us)
Async XLA Ops:
  1.5 7.3 %collective-permute-start = (bf16[4,7296]{1,0:T(4,128)(2,1)S(1)}, bf16[4,7296]{1,0:T(4,128)(2,1)S(1)}, u32[]{:S(2)}, u32[]{:S(2)}) collective-permute-start(bf16[4,7296]{1,0:T(4,128)(2,1)S(1)} %pack.1), channel_id=1, source_target_pairs={{0,8},{1,9},{2,10},{3,11},{4,12},{5,13},{6,14},{7,15},{8,0},{9,1},... | collective-permute-start | bytes 175112 | tf_op jit(solution)/shard_map/ppermute | solution.py:30
  5.6 9.6 %collective-permute-start.3 = (bf16[4,7296]{1,0:T(4,128)(2,1)S(1)}, bf16[4,7296]{1,0:T(4,128)(2,1)S(1)}, u32[]{:S(2)}, u32[]{:S(2)}) collective-permute-start(bf16[4,7296]{1,0:T(4,128)(2,1)S(1)} %pack.1), channel_id=1, source_target_pairs={{0,6},{1,7},{2,4},{3,5},{4,2},{5,3},{6,0},{7,1},{8,14},{9,15},{10,... | collective-permute-start | bytes 175112 | tf_op jit(solution)/shard_map/ppermute | solution.py:30
  8.9 8.0 %collective-permute-start.1 = (bf16[8,7296]{1,0:T(8,128)(2,1)S(1)}, bf16[8,7296]{1,0:T(8,128)(2,1)S(1)}, u32[]{:S(2)}, u32[]{:S(2)}) collective-permute-start(bf16[8,7296]{1,0:T(8,128)(2,1)S(1)} %pad_maximum_fusion.after_ref.refs_0_), channel_id=1, source_target_pairs={{0,2},{1,5},{2,0},{3,7},{4,6},{5,1},{6,4},{7,3},{8,10},{9,13},{10,... | collective-permute-start | bytes 350216 | tf_op jit(solution)/shard_map/ppermute | solution.py:30
  10.3 7.0 %collective-permute-start.2 = (bf16[8,7296]{1,0:T(8,128)(2,1)S(1)}, bf16[8,7296]{1,0:T(8,128)(2,1)S(1)}, u32[]{:S(2)}, u32[]{:S(2)}) collective-permute-start(bf16[8,7296]{1,0:T(8,128)(2,1)S(1)} %pad_maximum_fusion.after_ref.refs_0_), channel_id=1, source_target_pairs={{0,4},{1,3},{2,6},{3,1},{4,0},{5,7},{6,2},{7,5},{8,12},{9,11},{10,... | collective-permute-start | bytes 350216 | tf_op jit(solution)/shard_map/ppermute | solution.py:30
  11.4 6.0 %collective-permute-start.5 = (bf16[8,7296]{1,0:T(8,128)(2,1)S(1)}, bf16[8,7296]{1,0:T(8,128)(2,1)S(1)}, u32[]{:S(2)}, u32[]{:S(2)}) collective-permute-start(bf16[8,7296]{1,0:T(8,128)(2,1)S(1)} %pad_maximum_fusion.after_ref.refs_0_), channel_id=1, source_target_pairs={{0,1},{1,0},{2,3},{3,2},{4,5},{5,4},{6,7},{7,6},{8,9},{9,8},{10,11... | collective-permute-start | bytes 350216 | tf_op jit(solution)/shard_map/ppermute | solution.py:30
  11.4 5.3 %collective-permute-start.4 = (bf16[4,7296]{1,0:T(4,128)(2,1)S(1)}, bf16[4,7296]{1,0:T(4,128)(2,1)S(1)}, u32[]{:S(2)}, u32[]{:S(2)}) collective-permute-start(bf16[4,7296]{1,0:T(4,128)(2,1)S(1)} %collective-permute-done), channel_id=1, source_target_pairs={{0,6},{1,7},{2,4},{3,5},{4,2},{5,3},{6,0},{7,1},{8,14},{9,15},{10,... | collective-permute-start | bytes 175112 | tf_op jit(solution)/shard_map/ppermute | solution.py:30
  12.4 6.3 %copy-start = (bf16[1,7168,256]{2,1,0:T(8,128)(2,1)S(1)}, bf16[1,7168,256]{2,1,0:T(8,128)(2,1)}, u32[]{:S(2)}) copy-start(bf16[1,7168,256]{2,1,0:T(8,128)(2,1)} %refs_9_.1) | copy-start | bytes 11010052
  12.4 6.3 %copy-start.1 = (bf16[1,7168,256]{2,1,0:T(8,128)(2,1)S(1)}, bf16[1,7168,256]{2,1,0:T(8,128)(2,1)}, u32[]{:S(2)}) copy-start(bf16[1,7168,256]{2,1,0:T(8,128)(2,1)} %refs_10_.1) | copy-start | bytes 11010052
  12.4 6.3 %copy-start.2 = (bf16[1,256,7168]{2,1,0:T(8,128)(2,1)S(1)}, bf16[1,256,7168]{2,1,0:T(8,128)(2,1)}, u32[]{:S(2)}) copy-start(bf16[1,256,7168]{2,1,0:T(8,128)(2,1)} %refs_11_.1) | copy-start | bytes 11010052
  12.4 6.3 %copy-start.3 = (bf16[7168]{0:T(1024)(128)(2,1)S(1)}, bf16[7168]{0:T(1024)(128)(2,1)}, u32[]{:S(2)}) copy-start(bf16[7168]{0:T(1024)(128)(2,1)} %param.13) | copy-start | bytes 43012
  16.8 1.4 %collective-permute-start.8 = (bf16[8,7296]{1,0:T(8,128)(2,1)S(1)}, bf16[8,7296]{1,0:T(8,128)(2,1)S(1)}, u32[]{:S(2)}, u32[]{:S(2)}) collective-permute-start(bf16[8,7296]{1,0:T(8,128)(2,1)S(1)} %pad_maximum_fusion.1.refs_3_), channel_id=1, source_target_pairs={{0,1},{1,0},{2,3},{3,2},{4,5},{5,4},{6,7},{7,6},{8,9},{9,8},{10,11... | collective-permute-start | bytes 350216 | tf_op jit(solution)/shard_map/ppermute | solution.py:30
  16.8 1.5 %collective-permute-start.6 = (bf16[8,7296]{1,0:T(8,128)(2,1)S(1)}, bf16[8,7296]{1,0:T(8,128)(2,1)S(1)}, u32[]{:S(2)}, u32[]{:S(2)}) collective-permute-start(bf16[8,7296]{1,0:T(8,128)(2,1)S(1)} %collective-permute-done.1.refs_1_), channel_id=1, source_target_pairs={{0,1},{1,0},{2,3},{3,2},{4,5},{5,4},{6,7},{7,6},{8,9},{9,8},{10,11... | collective-permute-start | bytes 350216 | tf_op jit(solution)/shard_map/ppermute | solution.py:30
  17.3 1.3 %collective-permute-start.7 = (bf16[8,7296]{1,0:T(8,128)(2,1)S(1)}, bf16[8,7296]{1,0:T(8,128)(2,1)S(1)}, u32[]{:S(2)}, u32[]{:S(2)}) collective-permute-start(bf16[8,7296]{1,0:T(8,128)(2,1)S(1)} %collective-permute-done.2.refs_2_), channel_id=1, source_target_pairs={{0,1},{1,0},{2,3},{3,2},{4,5},{5,4},{6,7},{7,6},{8,9},{9,8},{10,11... | collective-permute-start | bytes 350216 | tf_op jit(solution)/shard_map/ppermute | solution.py:30
  20.5 1.4 %collective-permute-start.10 = (bf16[8,7168]{1,0:T(8,128)(2,1)S(1)}, bf16[8,7168]{1,0:T(8,128)(2,1)S(1)}, u32[]{:S(2)}, u32[]{:S(2)}) collective-permute-start(bf16[8,7168]{1,0:T(8,128)(2,1)S(1)} %get-tuple-element.19), channel_id=1, source_target_pairs={{0,1},{1,0},{2,3},{3,2},{4,5},{5,4},{6,7},{7,6},{8,9},{9,8},{10,11... | collective-permute-start | bytes 344072 | tf_op jit(solution)/shard_map/ppermute | solution.py:30
  20.7 3.6 %collective-permute-start.14 = (bf16[8,7168]{1,0:T(8,128)(2,1)S(1)}, bf16[8,7168]{1,0:T(8,128)(2,1)S(1)}, u32[]{:S(2)}, u32[]{:S(2)}) collective-permute-start(bf16[8,7168]{1,0:T(8,128)(2,1)S(1)} %get-tuple-element.23), channel_id=1, source_target_pairs={{0,1},{1,0},{2,3},{3,2},{4,5},{5,4},{6,7},{7,6},{8,9},{9,8},{10,11... | collective-permute-start | bytes 344072 | tf_op jit(solution)/shard_map/ppermute | solution.py:30
  21.0 2.1 %collective-permute-start.12 = (bf16[8,7168]{1,0:T(8,128)(2,1)S(1)}, bf16[8,7168]{1,0:T(8,128)(2,1)S(1)}, u32[]{:S(2)}, u32[]{:S(2)}) collective-permute-start(bf16[8,7168]{1,0:T(8,128)(2,1)S(1)} %get-tuple-element.21), channel_id=1, source_target_pairs={{0,1},{1,0},{2,3},{3,2},{4,5},{5,4},{6,7},{7,6},{8,9},{9,8},{10,11... | collective-permute-start | bytes 344072 | tf_op jit(solution)/shard_map/ppermute | solution.py:30
  21.2 8.6 %collective-permute-start.9 = (bf16[8,7168]{1,0:T(8,128)(2,1)S(1)}, bf16[8,7168]{1,0:T(8,128)(2,1)S(1)}, u32[]{:S(2)}, u32[]{:S(2)}) collective-permute-start(bf16[8,7168]{1,0:T(8,128)(2,1)S(1)} %get-tuple-element.17), channel_id=1, source_target_pairs={{0,1},{1,0},{2,3},{3,2},{4,5},{5,4},{6,7},{7,6},{8,9},{9,8},{10,11... | collective-permute-start | bytes 344072 | tf_op jit(solution)/shard_map/ppermute | solution.py:30
  21.9 7.9 %collective-permute-start.11 = (bf16[8,7168]{1,0:T(8,128)(2,1)S(1)}, bf16[8,7168]{1,0:T(8,128)(2,1)S(1)}, u32[]{:S(2)}, u32[]{:S(2)}) collective-permute-start(bf16[8,7168]{1,0:T(8,128)(2,1)S(1)} %add_convert_fusion.2), channel_id=1, source_target_pairs={{0,2},{1,5},{2,0},{3,7},{4,6},{5,1},{6,4},{7,3},{8,10},{9,13},{10,... | collective-permute-start | bytes 344072 | tf_op jit(solution)/shard_map/ppermute | solution.py:30
  23.2 6.6 %collective-permute-start.13 = (bf16[8,7168]{1,0:T(8,128)(2,1)S(1)}, bf16[8,7168]{1,0:T(8,128)(2,1)S(1)}, u32[]{:S(2)}, u32[]{:S(2)}) collective-permute-start(bf16[8,7168]{1,0:T(8,128)(2,1)S(1)} %add_convert_fusion.1), channel_id=1, source_target_pairs={{0,4},{1,3},{2,6},{3,1},{4,0},{5,7},{6,2},{7,5},{8,12},{9,11},{10,... | collective-permute-start | bytes 344072 | tf_op jit(solution)/shard_map/ppermute | solution.py:30
  24.4 5.4 %collective-permute-start.16 = (bf16[4,7168]{1,0:T(4,128)(2,1)S(1)}, bf16[4,7168]{1,0:T(4,128)(2,1)S(1)}, u32[]{:S(2)}, u32[]{:S(2)}) collective-permute-start(bf16[4,7168]{1,0:T(4,128)(2,1)S(1)} %get-tuple-element.27), channel_id=1, source_target_pairs={{0,6},{1,7},{2,4},{3,5},{4,2},{5,3},{6,0},{7,1},{8,14},{9,15},{10,... | collective-permute-start | bytes 172040 | tf_op jit(solution)/shard_map/ppermute | solution.py:30
  26.6 6.3 %collective-permute-start.15 = (bf16[4,7168]{1,0:T(4,128)(2,1)S(1)}, bf16[4,7168]{1,0:T(4,128)(2,1)S(1)}, u32[]{:S(2)}, u32[]{:S(2)}) collective-permute-start(bf16[4,7168]{1,0:T(4,128)(2,1)S(1)} %get-tuple-element.26), channel_id=1, source_target_pairs={{0,6},{1,7},{2,4},{3,5},{4,2},{5,3},{6,0},{7,1},{8,14},{9,15},{10,... | collective-permute-start | bytes 172040 | tf_op jit(solution)/shard_map/ppermute | solution.py:30
  29.9 5.2 %collective-permute-start.17 = (bf16[4,7168]{1,0:T(4,128)(2,1)S(1)}, bf16[4,7168]{1,0:T(4,128)(2,1)S(1)}, u32[]{:S(2)}, u32[]{:S(2)}) collective-permute-start(bf16[4,7168]{1,0:T(4,128)(2,1)S(1)} %fusion), channel_id=1, source_target_pairs={{0,8},{1,9},{2,10},{3,11},{4,12},{5,13},{6,14},{7,15},{8,0},{9,1},... | collective-permute-start | bytes 172040 | tf_op jit(solution)/shard_map/ppermute | solution.py:30

commit v6 on v5

--- a/solution.py
+++ b/solution.py
@@ -83,6 +83,23 @@
     )(*map(in_hbm, (tokens, routes.T, gates.T)))
 
 
+def join_kernel(upper_ref, lower_ref, rows_ref):
+    half = upper_ref.shape[0]
+    rows_ref[:half] = upper_ref[...]
+    rows_ref[half:] = lower_ref[...]
+
+
+def join(upper, lower):
+    half, width = upper.shape
+    return pl.pallas_call(
+        join_kernel,
+        out_shape=jax.ShapeDtypeStruct((2 * half, width), upper.dtype),
+        compiler_params=pltpu.CompilerParams(vmem_limit_bytes=VMEM_LIMIT),
+        cost_estimate=pl.CostEstimate(flops=4_000_000_000, bytes_accessed=500_000, transcendentals=0),
+        name="join",
+    )(upper, lower)
+
+
 def attention_kernel(after_ref, lengths_ref, queries_hbm, cache_hbm, attended_ref, queries_ref, cache_ref, sem):
     copies = [
         pltpu.make_async_copy(queries_hbm, queries_ref, sem.at[0]),
@@ -123,7 +140,7 @@
             pltpu.SemaphoreType.DMA((2,)),
         ],
         compiler_params=pltpu.CompilerParams(vmem_limit_bytes=VMEM_LIMIT),
-        cost_estimate=pl.CostEstimate(flops=4_000_000_000, bytes_accessed=1_700_000, transcendentals=164_000),
+        cost_estimate=pl.CostEstimate(flops=360_000_000, bytes_accessed=1_700_000, transcendentals=164_000),
         name="attention",
     )(after, lengths, *map(in_hbm, (queries, cache)))
 
@@ -203,7 +220,7 @@
         rows = jnp.concatenate([rows, trade(rows, partners)], axis=0)
     arrived = trade(rows, far[-1])
     diagonal = trade(rows, near[2])
-    rows = jnp.concatenate([rows, arrived], axis=0)
+    rows = join(rows, arrived)
     attended = attention(rows, lengths, queries, cache)
     weights = (w_gate, w_up, w_down)
     pieces = [rows] + [trade(rows, partners) for partners in near[:2]]
@@ -211,7 +228,7 @@
     pieces.append(jnp.concatenate([diagonal, trade(arrived, near[2])], axis=0))
     pieces += [trade(piece, core) for piece in pieces]
 
-    outputs = experts(attended, pieces, routes.shape[1], gain, weights)
+    outputs = experts(rows, pieces, routes.shape[1], gain, weights)
     own, other = outputs[:4], outputs[4:]
     sums = [mine + trade(theirs, core).astype(jnp.float32) for mine, theirs in zip(own[1:], other[1:])]
     half = rows.shape[0] // 2

time: 35.9 us -> 35.1 us (0.978)
  waiting for transfers between devices: 6.7 us -> 5.65 us
  Pallas kernels: 5.4 us -> 6.04 us
  starting transfers between devices: 20.3 us -> 19.9 us
    ppermute x18, waiting for transfers between devices: 6.7 us -> 5.65 us  [trade(): return lax.ppermute(value, 'node', list(enumerate(partners)))]
    pallas_call x1, Pallas kernels: 2.75 us -> 3.35 us  [attention(): pl.pallas_call(attention_kernel, out_shape=jax.ShapeDtypeStruct((1, heads...]
    ppermute x18, starting transfers between devices: 20.3 us -> 19.9 us  [trade(): return lax.ppermute(value, 'node', list(enumerate(partners)))]
  transfers between devices with their start and end apart: 18 -> 18, of which waited for: 7 -> 7; matrix products, arithmetic and copies ran while one was open for 4% -> 3% of each run, Pallas kernels for 8% -> 10%
where the time goes in v6:
time: 35.1 us; the launch traced here: 34.9 us
  starting transfers between devices  19.9 us (57%)
  Pallas kernels  6.04 us (17%)
  waiting for transfers between devices  5.65 us (16%)
  between operations  1.42 us (4%)
  local copies, waits for them, and re-layouts  0.96 us (3%)
  other arithmetic  0.93 us (3%)
    ppermute x18, starting transfers between devices, trade(): return lax.ppermute(value, 'node', list(enumerate(partners)))  19.9 us
    ppermute x18, waiting for transfers between devices, trade(): return lax.ppermute(value, 'node', list(enumerate(partners)))  5.65 us
    pallas_call x1, Pallas kernels, attention(): pl.pallas_call(attention_kernel, out_shape=jax.ShapeDtypeStruct((1, heads...  3.35 us
    pallas_call x1, Pallas kernels, experts(): pl.pallas_call(functools.partial(experts_kernel, picks, count), out_shape...  1.77 us
    unnamed x9, local copies, waits for them, and re-layouts  0.92 us
    pallas_call x1, Pallas kernels, pack(): pl.pallas_call(pack_kernel, out_shape=jax.ShapeDtypeStruct((count, width...  0.88 us
  transfers between devices with their start and end apart: 18, of which 7 were waited for; matrix products, arithmetic and copies ran while one was open for 3% of the time, Pallas kernels for 10%

profile of v6, /device:TPU:0, one launch (start us, length us, event | category | flops | bytes accessed | tf_op | source)
XLA Modules:
  0.0 34.9 jit_solution(9038730824230418428)
XLA Ops:
  0.6 0.9 %pack.1.upper_ref = bf16[4,7296]{1,0:T(4,128)(2,1)S(1)} custom-call(bf16[4,7168]{1,0:T(4,128)(2,1)} %tokens_hbm.1, s32[2,4]{1,0:T(2,128)} %bitcast.12, f32[2,4]{1,0:T(2,128)} %bitcast.13), custom_call_target="tpu_custom_call" | custom-call | tf_op jit(solution)/shard_map/pack/pallas_call | solution.py:71
  1.5 4.1 %collective-permute-start = (bf16[4,7296]{1,0:T(4,128)(2,1)S(1)}, bf16[4,7296]{1,0:T(4,128)(2,1)S(1)}, u32[]{:S(2)}, u32[]{:S(2)}) collective-permute-start(bf16[4,7296]{1,0:T(4,128)(2,1)S(1)} %pack.1.upper_ref), channel_id=1, source_target_pairs={{0,8},{1,9},{2,10},{3,11},{4,12},{5,13},{6,14},{7,15},{8,0},{9,1},... | collective-permute-start | bytes 175112 | tf_op jit(solution)/shard_map/ppermute | solution.py:30
  5.6 2.5 %collective-permute-start.3 = (bf16[4,7296]{1,0:T(4,128)(2,1)S(1)}, bf16[4,7296]{1,0:T(4,128)(2,1)S(1)}, u32[]{:S(2)}, u32[]{:S(2)}) collective-permute-start(bf16[4,7296]{1,0:T(4,128)(2,1)S(1)} %pack.1.upper_ref), channel_id=1, source_target_pairs={{0,6},{1,7},{2,4},{3,5},{4,2},{5,3},{6,0},{7,1},{8,14},{9,15},{10,... | collective-permute-start | bytes 175112 | tf_op jit(solution)/shard_map/ppermute | solution.py:30
  8.8 0.0 copy-start.3
  8.8 0.0 collective-permute-done.lower_ref
  8.8 1.9 %collective-permute-start.4 = (bf16[4,7296]{1,0:T(4,128)(2,1)S(1)}, bf16[4,7296]{1,0:T(4,128)(2,1)S(1)}, u32[]{:S(2)}, u32[]{:S(2)}) collective-permute-start(bf16[4,7296]{1,0:T(4,128)(2,1)S(1)} %collective-permute-done.lower_ref), channel_id=1, source_target_pairs={{0,6},{1,7},{2,4},{3,5},{4,2},{5,3},{6,0},{7,1},{8,14},{9,15},{10,... | collective-permute-start | bytes 175112 | tf_op jit(solution)/shard_map/ppermute | solution.py:30
  10.8 1.1 %collective-permute-start.1 = (bf16[8,7296]{1,0:T(8,128)(2,1)S(1)}, bf16[8,7296]{1,0:T(8,128)(2,1)S(1)}, u32[]{:S(2)}, u32[]{:S(2)}) collective-permute-start(bf16[8,7296]{1,0:T(8,128)(2,1)S(1)} %join.1.after_ref.loaded_ref.refs_0_), channel_id=1, source_target_pairs={{0,2},{1,5},{2,0},{3,7},{4,6},{5,1},{6,4},{7,3},{8,10},{9,13},{10,... | collective-permute-start | bytes 350216 | tf_op jit(solution)/shard_map/ppermute | solution.py:30
  11.9 0.6 %collective-permute-start.2 = (bf16[8,7296]{1,0:T(8,128)(2,1)S(1)}, bf16[8,7296]{1,0:T(8,128)(2,1)S(1)}, u32[]{:S(2)}, u32[]{:S(2)}) collective-permute-start(bf16[8,7296]{1,0:T(8,128)(2,1)S(1)} %join.1.after_ref.loaded_ref.refs_0_), channel_id=1, source_target_pairs={{0,4},{1,3},{2,6},{3,1},{4,0},{5,7},{6,2},{7,5},{8,12},{9,11},{10,... | collective-permute-start | bytes 350216 | tf_op jit(solution)/shard_map/ppermute | solution.py:30
  12.5 3.4 %attention.1 = bf16[1,128,512]{2,1,0:T(8,128)(2,1)S(1)} custom-call(bf16[8,7296]{1,0:T(8,128)(2,1)S(1)} %join.1.after_ref.loaded_ref.refs_0_, s32[1]{0:T(128)S(6)} %copy.13.lengths_ref, bf16[1,576,128]{2,1,0:T(8,128)(2,1)} %bitcast.11, bf16[1,576,1280]{2,1,0:T(8,128)(2,1)} %bitcast.9), custom_call_target="tpu_custom_call" | custom-call | flops 360000000 | bytes 1700000 | tf_op jit(solution)/shard_map/attention/pallas_call | solution.py:133
  15.8 0.1 pad_maximum_fusion.refs_3_
  15.9 0.1 collective-permute-start.8
  16.0 0.5 %collective-permute-start.6 = (bf16[8,7296]{1,0:T(8,128)(2,1)S(1)}, bf16[8,7296]{1,0:T(8,128)(2,1)S(1)}, u32[]{:S(2)}, u32[]{:S(2)}) collective-permute-start(bf16[8,7296]{1,0:T(8,128)(2,1)S(1)} %collective-permute-done.1.refs_1_), channel_id=1, source_target_pairs={{0,1},{1,0},{2,3},{3,2},{4,5},{5,4},{6,7},{7,6},{8,9},{9,8},{10,11... | collective-permute-start | bytes 350216 | tf_op jit(solution)/shard_map/ppermute | solution.py:30
  16.5 0.2 collective-permute-done.2.refs_2_
  16.7 0.6 %collective-permute-done.8.refs_7_ = bf16[8,7296]{1,0:T(8,128)(2,1)S(1)} collective-permute-done((bf16[8,7296]{1,0:T(8,128)(2,1)S(1)}, bf16[8,7296]{1,0:T(8,128)(2,1)S(1)}, u32[]{:S(2)}, u32[]{:S(2)}) %collective-permute-start.8) | collective-permute-done | bytes 116768 | tf_op jit(solution)/shard_map/ppermute | solution.py:30
  17.3 0.2 collective-permute-done.6.refs_5_
  17.5 0.5 %collective-permute-done.7.refs_6_ = bf16[8,7296]{1,0:T(8,128)(2,1)S(1)} collective-permute-done((bf16[8,7296]{1,0:T(8,128)(2,1)S(1)}, bf16[8,7296]{1,0:T(8,128)(2,1)S(1)}, u32[]{:S(2)}, u32[]{:S(2)}) %collective-permute-start.7) | collective-permute-done | bytes 116768 | tf_op jit(solution)/shard_map/ppermute | solution.py:30
  18.0 1.8 %experts.1 = (f32[8,7168]{1,0:T(8,128)S(1)}, f32[8,7168]{1,0:T(8,128)S(1)}, f32[8,7168]{1,0:T(8,128)S(1)}, f32[8,7168]{1,0:T(8,128)S(1)}, bf16[8,7168]{1,0:T(8,1...) custom-call(bf16[8,7296]{1,0:T(8,128)(2,1)S(1)} %join.1.after_ref.loaded_ref.ref, ...), custom_call_target="tpu_custom_call" | custom-call | tf_op jit(solution)/shard_map/experts/pallas_call | solution.py:202
  19.8 0.2 collective-permute-start.10
  20.0 0.4 %collective-permute-start.14 = (bf16[8,7168]{1,0:T(8,128)(2,1)S(1)}, bf16[8,7168]{1,0:T(8,128)(2,1)S(1)}, u32[]{:S(2)}, u32[]{:S(2)}) collective-permute-start(bf16[8,7168]{1,0:T(8,128)(2,1)S(1)} %get-tuple-element.22), channel_id=1, source_target_pairs={{0,1},{1,0},{2,3},{3,2},{4,5},{5,4},{6,7},{7,6},{8,9},{9,8},{10,11... | collective-permute-start | bytes 344072 | tf_op jit(solution)/shard_map/ppermute | solution.py:30
  20.4 0.1 collective-permute-start.12
  20.5 0.4 %collective-permute-start.9 = (bf16[8,7168]{1,0:T(8,128)(2,1)S(1)}, bf16[8,7168]{1,0:T(8,128)(2,1)S(1)}, u32[]{:S(2)}, u32[]{:S(2)}) collective-permute-start(bf16[8,7168]{1,0:T(8,128)(2,1)S(1)} %get-tuple-element.16), channel_id=1, source_target_pairs={{0,1},{1,0},{2,3},{3,2},{4,5},{5,4},{6,7},{7,6},{8,9},{9,8},{10,11... | collective-permute-start | bytes 344072 | tf_op jit(solution)/shard_map/ppermute | solution.py:30
  20.9 0.3 collective-permute-done.10
  21.2 1.2 %collective-permute-start.11 = (bf16[8,7168]{1,0:T(8,128)(2,1)S(1)}, bf16[8,7168]{1,0:T(8,128)(2,1)S(1)}, u32[]{:S(2)}, u32[]{:S(2)}) collective-permute-start(bf16[8,7168]{1,0:T(8,128)(2,1)S(1)} %add_convert_fusion.2), channel_id=1, source_target_pairs={{0,2},{1,5},{2,0},{3,7},{4,6},{5,1},{6,4},{7,3},{8,10},{9,13},{10,... | collective-permute-start | bytes 344072 | tf_op jit(solution)/shard_map/ppermute | solution.py:30
  22.5 1.0 %collective-permute-start.13 = (bf16[8,7168]{1,0:T(8,128)(2,1)S(1)}, bf16[8,7168]{1,0:T(8,128)(2,1)S(1)}, u32[]{:S(2)}, u32[]{:S(2)}) collective-permute-start(bf16[8,7168]{1,0:T(8,128)(2,1)S(1)} %add_convert_fusion.1), channel_id=1, source_target_pairs={{0,4},{1,3},{2,6},{3,1},{4,0},{5,7},{6,2},{7,5},{8,12},{9,11},{10,... | collective-permute-start | bytes 344072 | tf_op jit(solution)/shard_map/ppermute | solution.py:30
  23.6 1.4 %collective-permute-start.16 = (bf16[4,7168]{1,0:T(4,128)(2,1)S(1)}, bf16[4,7168]{1,0:T(4,128)(2,1)S(1)}, u32[]{:S(2)}, u32[]{:S(2)}) collective-permute-start(bf16[4,7168]{1,0:T(4,128)(2,1)S(1)} %get-tuple-element.27), channel_id=1, source_target_pairs={{0,6},{1,7},{2,4},{3,5},{4,2},{5,3},{6,0},{7,1},{8,14},{9,15},{10,... | collective-permute-start | bytes 172040 | tf_op jit(solution)/shard_map/ppermute | solution.py:30
  25.1 0.9 %copy.12 = bf16[1,1,128,512]{3,1,2,0:T(2,128)(2,1)} copy(bf16[1,1,128,512]{3,2,1,0:T(8,128)(2,1)S(1)} %bitcast.7) | data formatting | bytes 262144
  26.0 1.6 %collective-permute-start.15 = (bf16[4,7168]{1,0:T(4,128)(2,1)S(1)}, bf16[4,7168]{1,0:T(4,128)(2,1)S(1)}, u32[]{:S(2)}, u32[]{:S(2)}) collective-permute-start(bf16[4,7168]{1,0:T(4,128)(2,1)S(1)} %get-tuple-element.26), channel_id=1, source_target_pairs={{0,6},{1,7},{2,4},{3,5},{4,2},{5,3},{6,0},{7,1},{8,14},{9,15},{10,... | collective-permute-start | bytes 172040 | tf_op jit(solution)/shard_map/ppermute | solution.py:30
  27.5 1.4 %collective-permute-done.16 = bf16[4,7168]{1,0:T(4,128)(2,1)S(1)} collective-permute-done((bf16[4,7168]{1,0:T(4,128)(2,1)S(1)}, bf16[4,7168]{1,0:T(4,128)(2,1)S(1)}, u32[]{:S(2)}, u32[]{:S(2)}) %collective-permute-start.16) | collective-permute-done | bytes 57376 | tf_op jit(solution)/shard_map/ppermute | solution.py:30
  29.0 0.1 convert_add_fusion
  29.1 2.8 %collective-permute-start.17 = (bf16[4,7168]{1,0:T(4,128)(2,1)S(1)}, bf16[4,7168]{1,0:T(4,128)(2,1)S(1)}, u32[]{:S(2)}, u32[]{:S(2)}) collective-permute-start(bf16[4,7168]{1,0:T(4,128)(2,1)S(1)} %fusion), channel_id=1, source_target_pairs={{0,8},{1,9},{2,10},{3,11},{4,12},{5,13},{6,14},{7,15},{8,0},{9,1},... | collective-permute-start | bytes 172040 | tf_op jit(solution)/shard_map/ppermute | solution.py:30
  31.9 2.4 %collective-permute-done.17 = bf16[4,7168]{1,0:T(4,128)(2,1)S(1)} collective-permute-done((bf16[4,7168]{1,0:T(4,128)(2,1)S(1)}, bf16[4,7168]{1,0:T(4,128)(2,1)S(1)}, u32[]{:S(2)}, u32[]{:S(2)}) %collective-permute-start.17) | collective-permute-done | bytes 57376 | tf_op jit(solution)/shard_map/ppermute | solution.py:30
  34.2 0.7 %fusion.2 = bf16[4,7168]{1,0:T(4,128)(2,1)} fusion(f32[8,7168]{1,0:T(8,128)S(1)} %convert_add_fusion, bf16[4,7168]{1,0:T(4,128)(2,1)S(1)} %collective-permute-done.17, bf16[4,7168]{1,0:T(4,128)(2,1)S(1)} %collective-permute-done.15), kind=kLoop, calls=%fused_computation.9 | loop fusion | flops 143360 | bytes 286720 | tf_op jit(solution)/shard_map/convert_element_type | solution.py:252
  (25 shorter events, 0.3 us)
Async XLA Ops:
  1.5 7.3 %collective-permute-start = (bf16[4,7296]{1,0:T(4,128)(2,1)S(1)}, bf16[4,7296]{1,0:T(4,128)(2,1)S(1)}, u32[]{:S(2)}, u32[]{:S(2)}) collective-permute-start(bf16[4,7296]{1,0:T(4,128)(2,1)S(1)} %pack.1.upper_ref), channel_id=1, source_target_pairs={{0,8},{1,9},{2,10},{3,11},{4,12},{5,13},{6,14},{7,15},{8,0},{9,1},... | collective-permute-start | bytes 175112 | tf_op jit(solution)/shard_map/ppermute | solution.py:30
  5.6 10.2 %collective-permute-start.3 = (bf16[4,7296]{1,0:T(4,128)(2,1)S(1)}, bf16[4,7296]{1,0:T(4,128)(2,1)S(1)}, u32[]{:S(2)}, u32[]{:S(2)}) collective-permute-start(bf16[4,7296]{1,0:T(4,128)(2,1)S(1)} %pack.1.upper_ref), channel_id=1, source_target_pairs={{0,6},{1,7},{2,4},{3,5},{4,2},{5,3},{6,0},{7,1},{8,14},{9,15},{10,... | collective-permute-start | bytes 175112 | tf_op jit(solution)/shard_map/ppermute | solution.py:30
  8.8 9.2 %copy-start.3 = (bf16[7168]{0:T(1024)(128)(2,1)S(1)}, bf16[7168]{0:T(1024)(128)(2,1)}, u32[]{:S(2)}) copy-start(bf16[7168]{0:T(1024)(128)(2,1)} %param.13) | copy-start | bytes 43012
  8.8 7.0 %collective-permute-start.4 = (bf16[4,7296]{1,0:T(4,128)(2,1)S(1)}, bf16[4,7296]{1,0:T(4,128)(2,1)S(1)}, u32[]{:S(2)}, u32[]{:S(2)}) collective-permute-start(bf16[4,7296]{1,0:T(4,128)(2,1)S(1)} %collective-permute-done.lower_ref), channel_id=1, source_target_pairs={{0,6},{1,7},{2,4},{3,5},{4,2},{5,3},{6,0},{7,1},{8,14},{9,15},{10,... | collective-permute-start | bytes 175112 | tf_op jit(solution)/shard_map/ppermute | solution.py:30
  10.7 7.3 %copy-start = (bf16[1,7168,256]{2,1,0:T(8,128)(2,1)S(1)}, bf16[1,7168,256]{2,1,0:T(8,128)(2,1)}, u32[]{:S(2)}) copy-start(bf16[1,7168,256]{2,1,0:T(8,128)(2,1)} %refs_9_.1) | copy-start | bytes 11010052
  10.7 7.3 %copy-start.1 = (bf16[1,7168,256]{2,1,0:T(8,128)(2,1)S(1)}, bf16[1,7168,256]{2,1,0:T(8,128)(2,1)}, u32[]{:S(2)}) copy-start(bf16[1,7168,256]{2,1,0:T(8,128)(2,1)} %refs_10_.1) | copy-start | bytes 11010052
  10.7 7.3 %copy-start.2 = (bf16[1,256,7168]{2,1,0:T(8,128)(2,1)S(1)}, bf16[1,256,7168]{2,1,0:T(8,128)(2,1)}, u32[]{:S(2)}) copy-start(bf16[1,256,7168]{2,1,0:T(8,128)(2,1)} %refs_11_.1) | copy-start | bytes 11010052
  10.8 5.2 %collective-permute-start.1 = (bf16[8,7296]{1,0:T(8,128)(2,1)S(1)}, bf16[8,7296]{1,0:T(8,128)(2,1)S(1)}, u32[]{:S(2)}, u32[]{:S(2)}) collective-permute-start(bf16[8,7296]{1,0:T(8,128)(2,1)S(1)} %join.1.after_ref.loaded_ref.refs_0_), channel_id=1, source_target_pairs={{0,2},{1,5},{2,0},{3,7},{4,6},{5,1},{6,4},{7,3},{8,10},{9,13},{10,... | collective-permute-start | bytes 350216 | tf_op jit(solution)/shard_map/ppermute | solution.py:30
  11.9 4.8 %collective-permute-start.2 = (bf16[8,7296]{1,0:T(8,128)(2,1)S(1)}, bf16[8,7296]{1,0:T(8,128)(2,1)S(1)}, u32[]{:S(2)}, u32[]{:S(2)}) collective-permute-start(bf16[8,7296]{1,0:T(8,128)(2,1)S(1)} %join.1.after_ref.loaded_ref.refs_0_), channel_id=1, source_target_pairs={{0,4},{1,3},{2,6},{3,1},{4,0},{5,7},{6,2},{7,5},{8,12},{9,11},{10,... | collective-permute-start | bytes 350216 | tf_op jit(solution)/shard_map/ppermute | solution.py:30
  12.5 4.2 %collective-permute-start.5 = (bf16[8,7296]{1,0:T(8,128)(2,1)S(1)}, bf16[8,7296]{1,0:T(8,128)(2,1)S(1)}, u32[]{:S(2)}, u32[]{:S(2)}) collective-permute-start(bf16[8,7296]{1,0:T(8,128)(2,1)S(1)} %join.1.after_ref.loaded_ref.refs_0_), channel_id=1, source_target_pairs={{0,1},{1,0},{2,3},{3,2},{4,5},{5,4},{6,7},{7,6},{8,9},{9,8},{10,11... | collective-permute-start | bytes 350216 | tf_op jit(solution)/shard_map/ppermute | solution.py:30
  15.9 1.4 %collective-permute-start.8 = (bf16[8,7296]{1,0:T(8,128)(2,1)S(1)}, bf16[8,7296]{1,0:T(8,128)(2,1)S(1)}, u32[]{:S(2)}, u32[]{:S(2)}) collective-permute-start(bf16[8,7296]{1,0:T(8,128)(2,1)S(1)} %pad_maximum_fusion.refs_3_), channel_id=1, source_target_pairs={{0,1},{1,0},{2,3},{3,2},{4,5},{5,4},{6,7},{7,6},{8,9},{9,8},{10,11... | collective-permute-start | bytes 350216 | tf_op jit(solution)/shard_map/ppermute | solution.py:30
  16.0 1.5 %collective-permute-start.6 = (bf16[8,7296]{1,0:T(8,128)(2,1)S(1)}, bf16[8,7296]{1,0:T(8,128)(2,1)S(1)}, u32[]{:S(2)}, u32[]{:S(2)}) collective-permute-start(bf16[8,7296]{1,0:T(8,128)(2,1)S(1)} %collective-permute-done.1.refs_1_), channel_id=1, source_target_pairs={{0,1},{1,0},{2,3},{3,2},{4,5},{5,4},{6,7},{7,6},{8,9},{9,8},{10,11... | collective-permute-start | bytes 350216 | tf_op jit(solution)/shard_map/ppermute | solution.py:30
  16.7 1.3 %collective-permute-start.7 = (bf16[8,7296]{1,0:T(8,128)(2,1)S(1)}, bf16[8,7296]{1,0:T(8,128)(2,1)S(1)}, u32[]{:S(2)}, u32[]{:S(2)}) collective-permute-start(bf16[8,7296]{1,0:T(8,128)(2,1)S(1)} %collective-permute-done.2.refs_2_), channel_id=1, source_target_pairs={{0,1},{1,0},{2,3},{3,2},{4,5},{5,4},{6,7},{7,6},{8,9},{9,8},{10,11... | collective-permute-start | bytes 350216 | tf_op jit(solution)/shard_map/ppermute | solution.py:30
  19.8 1.4 %collective-permute-start.10 = (bf16[8,7168]{1,0:T(8,128)(2,1)S(1)}, bf16[8,7168]{1,0:T(8,128)(2,1)S(1)}, u32[]{:S(2)}, u32[]{:S(2)}) collective-permute-start(bf16[8,7168]{1,0:T(8,128)(2,1)S(1)} %get-tuple-element.18), channel_id=1, source_target_pairs={{0,1},{1,0},{2,3},{3,2},{4,5},{5,4},{6,7},{7,6},{8,9},{9,8},{10,11... | collective-permute-start | bytes 344072 | tf_op jit(solution)/shard_map/ppermute | solution.py:30
  20.0 3.5 %collective-permute-start.14 = (bf16[8,7168]{1,0:T(8,128)(2,1)S(1)}, bf16[8,7168]{1,0:T(8,128)(2,1)S(1)}, u32[]{:S(2)}, u32[]{:S(2)}) collective-permute-start(bf16[8,7168]{1,0:T(8,128)(2,1)S(1)} %get-tuple-element.22), channel_id=1, source_target_pairs={{0,1},{1,0},{2,3},{3,2},{4,5},{5,4},{6,7},{7,6},{8,9},{9,8},{10,11... | collective-permute-start | bytes 344072 | tf_op jit(solution)/shard_map/ppermute | solution.py:30
  20.4 2.1 %collective-permute-start.12 = (bf16[8,7168]{1,0:T(8,128)(2,1)S(1)}, bf16[8,7168]{1,0:T(8,128)(2,1)S(1)}, u32[]{:S(2)}, u32[]{:S(2)}) collective-permute-start(bf16[8,7168]{1,0:T(8,128)(2,1)S(1)} %get-tuple-element.20), channel_id=1, source_target_pairs={{0,1},{1,0},{2,3},{3,2},{4,5},{5,4},{6,7},{7,6},{8,9},{9,8},{10,11... | collective-permute-start | bytes 344072 | tf_op jit(solution)/shard_map/ppermute | solution.py:30
  20.5 8.4 %collective-permute-start.9 = (bf16[8,7168]{1,0:T(8,128)(2,1)S(1)}, bf16[8,7168]{1,0:T(8,128)(2,1)S(1)}, u32[]{:S(2)}, u32[]{:S(2)}) collective-permute-start(bf16[8,7168]{1,0:T(8,128)(2,1)S(1)} %get-tuple-element.16), channel_id=1, source_target_pairs={{0,1},{1,0},{2,3},{3,2},{4,5},{5,4},{6,7},{7,6},{8,9},{9,8},{10,11... | collective-permute-start | bytes 344072 | tf_op jit(solution)/shard_map/ppermute | solution.py:30
  21.2 7.7 %collective-permute-start.11 = (bf16[8,7168]{1,0:T(8,128)(2,1)S(1)}, bf16[8,7168]{1,0:T(8,128)(2,1)S(1)}, u32[]{:S(2)}, u32[]{:S(2)}) collective-permute-start(bf16[8,7168]{1,0:T(8,128)(2,1)S(1)} %add_convert_fusion.2), channel_id=1, source_target_pairs={{0,2},{1,5},{2,0},{3,7},{4,6},{5,1},{6,4},{7,3},{8,10},{9,13},{10,... | collective-permute-start | bytes 344072 | tf_op jit(solution)/shard_map/ppermute | solution.py:30
  22.5 6.5 %collective-permute-start.13 = (bf16[8,7168]{1,0:T(8,128)(2,1)S(1)}, bf16[8,7168]{1,0:T(8,128)(2,1)S(1)}, u32[]{:S(2)}, u32[]{:S(2)}) collective-permute-start(bf16[8,7168]{1,0:T(8,128)(2,1)S(1)} %add_convert_fusion.1), channel_id=1, source_target_pairs={{0,4},{1,3},{2,6},{3,1},{4,0},{5,7},{6,2},{7,5},{8,12},{9,11},{10,... | collective-permute-start | bytes 344072 | tf_op jit(solution)/shard_map/ppermute | solution.py:30
  23.6 5.3 %collective-permute-start.16 = (bf16[4,7168]{1,0:T(4,128)(2,1)S(1)}, bf16[4,7168]{1,0:T(4,128)(2,1)S(1)}, u32[]{:S(2)}, u32[]{:S(2)}) collective-permute-start(bf16[4,7168]{1,0:T(4,128)(2,1)S(1)} %get-tuple-element.27), channel_id=1, source_target_pairs={{0,6},{1,7},{2,4},{3,5},{4,2},{5,3},{6,0},{7,1},{8,14},{9,15},{10,... | collective-permute-start | bytes 172040 | tf_op jit(solution)/shard_map/ppermute | solution.py:30
  26.0 5.9 %collective-permute-start.15 = (bf16[4,7168]{1,0:T(4,128)(2,1)S(1)}, bf16[4,7168]{1,0:T(4,128)(2,1)S(1)}, u32[]{:S(2)}, u32[]{:S(2)}) collective-permute-start(bf16[4,7168]{1,0:T(4,128)(2,1)S(1)} %get-tuple-element.26), channel_id=1, source_target_pairs={{0,6},{1,7},{2,4},{3,5},{4,2},{5,3},{6,0},{7,1},{8,14},{9,15},{10,... | collective-permute-start | bytes 172040 | tf_op jit(solution)/shard_map/ppermute | solution.py:30
  29.1 5.1 %collective-permute-start.17 = (bf16[4,7168]{1,0:T(4,128)(2,1)S(1)}, bf16[4,7168]{1,0:T(4,128)(2,1)S(1)}, u32[]{:S(2)}, u32[]{:S(2)}) collective-permute-start(bf16[4,7168]{1,0:T(4,128)(2,1)S(1)} %fusion), channel_id=1, source_target_pairs={{0,8},{1,9},{2,10},{3,11},{4,12},{5,13},{6,14},{7,15},{8,0},{9,1},... | collective-permute-start | bytes 172040 | tf_op jit(solution)/shard_map/ppermute | solution.py:30

commit v7 on v6

--- a/solution.py
+++ b/solution.py
@@ -207,6 +207,7 @@
         in_specs=[pl.BlockSpec(memory_space=pl.ANY)] + [vmem] * (count + 4),
         out_specs=(vmem,) * count,
         compiler_params=pltpu.CompilerParams(vmem_limit_bytes=VMEM_LIMIT),
+        cost_estimate=pl.CostEstimate(flops=2_000_000_000, bytes_accessed=500_000, transcendentals=0),
         name="experts",
     )(loaded, *pieces, gain, *weights)
 
@@ -226,7 +227,8 @@
     pieces = [rows] + [trade(rows, partners) for partners in near[:2]]
     pieces[1], attended = lax.optimization_barrier((pieces[1], attended))
     pieces.append(jnp.concatenate([diagonal, trade(arrived, near[2])], axis=0))
-    pieces += [trade(piece, core) for piece in pieces]
+    held, attended = lax.optimization_barrier((rows, attended))
+    pieces += [trade(piece, core) for piece in [held] + pieces[1:]]
 
     outputs = experts(rows, pieces, routes.shape[1], gain, weights)
     own, other = outputs[:4], outputs[4:]

time: 35.1 us -> 35.1 us (level)
  waiting for transfers between devices: 5.65 us -> 5.1 us
  starting transfers between devices: 19.9 us -> 20.4 us
    ppermute x18, waiting for transfers between devices: 5.65 us -> 5.1 us  [trade(): return lax.ppermute(value, 'node', list(enumerate(partners)))]
    ppermute x18, starting transfers between devices: 19.9 us -> 20.4 us  [trade(): return lax.ppermute(value, 'node', list(enumerate(partners)))]
  transfers between devices with their start and end apart: 18 -> 18, of which waited for: 7 -> 8; matrix products, arithmetic and copies ran while one was open for 3% -> 3% of each run, Pallas kernels for 10% -> 10%
where the time goes in v7:
time: 35.1 us; the launch traced here: 34.9 us
  starting transfers between devices  20.4 us (58%)
  Pallas kernels  6.03 us (17%)
  waiting for transfers between devices  5.1 us (15%)
  between operations  1.42 us (4%)
  local copies, waits for them, and re-layouts  0.96 us (3%)
  other arithmetic  0.93 us (3%)
    ppermute x18, starting transfers between devices, trade(): return lax.ppermute(value, 'node', list(enumerate(partners)))  20.4 us
    ppermute x18, waiting for transfers between devices, trade(): return lax.ppermute(value, 'node', list(enumerate(partners)))  5.1 us
    pallas_call x1, Pallas kernels, attention(): pl.pallas_call(attention_kernel, out_shape=jax.ShapeDtypeStruct((1, heads...  3.34 us
    pallas_call x1, Pallas kernels, experts(): pl.pallas_call(functools.partial(experts_kernel, picks, count), out_shape...  1.77 us
    unnamed x9, local copies, waits for them, and re-layouts  0.92 us
    pallas_call x1, Pallas kernels, pack(): pl.pallas_call(pack_kernel, out_shape=jax.ShapeDtypeStruct((count, width...  0.88 us
  transfers between devices with their start and end apart: 18, of which 8 were waited for; matrix products, arithmetic and copies ran while one was open for 3% of the time, Pallas kernels for 10%

profile of v7, /device:TPU:0, one launch (start us, length us, event | category | flops | bytes accessed | tf_op | source)
XLA Modules:
  0.0 34.9 jit_solution(11767199809772144147)
XLA Ops:
  0.6 0.9 %pack.1.upper_ref = bf16[4,7296]{1,0:T(4,128)(2,1)S(1)} custom-call(bf16[4,7168]{1,0:T(4,128)(2,1)} %tokens_hbm.1, s32[2,4]{1,0:T(2,128)} %bitcast.12, f32[2,4]{1,0:T(2,128)} %bitcast.13), custom_call_target="tpu_custom_call" | custom-call | tf_op jit(solution)/shard_map/pack/pallas_call | solution.py:71
  1.5 4.1 %collective-permute-start = (bf16[4,7296]{1,0:T(4,128)(2,1)S(1)}, bf16[4,7296]{1,0:T(4,128)(2,1)S(1)}, u32[]{:S(2)}, u32[]{:S(2)}) collective-permute-start(bf16[4,7296]{1,0:T(4,128)(2,1)S(1)} %pack.1.upper_ref), channel_id=1, source_target_pairs={{0,8},{1,9},{2,10},{3,11},{4,12},{5,13},{6,14},{7,15},{8,0},{9,1},... | collective-permute-start | bytes 175112 | tf_op jit(solution)/shard_map/ppermute | solution.py:30
  5.6 2.5 %collective-permute-start.3 = (bf16[4,7296]{1,0:T(4,128)(2,1)S(1)}, bf16[4,7296]{1,0:T(4,128)(2,1)S(1)}, u32[]{:S(2)}, u32[]{:S(2)}) collective-permute-start(bf16[4,7296]{1,0:T(4,128)(2,1)S(1)} %pack.1.upper_ref), channel_id=1, source_target_pairs={{0,6},{1,7},{2,4},{3,5},{4,2},{5,3},{6,0},{7,1},{8,14},{9,15},{10,... | collective-permute-start | bytes 175112 | tf_op jit(solution)/shard_map/ppermute | solution.py:30
  8.8 1.9 %collective-permute-start.4 = (bf16[4,7296]{1,0:T(4,128)(2,1)S(1)}, bf16[4,7296]{1,0:T(4,128)(2,1)S(1)}, u32[]{:S(2)}, u32[]{:S(2)}) collective-permute-start(bf16[4,7296]{1,0:T(4,128)(2,1)S(1)} %collective-permute-done.lower_ref), channel_id=1, source_target_pairs={{0,6},{1,7},{2,4},{3,5},{4,2},{5,3},{6,0},{7,1},{8,14},{9,15},{10,... | collective-permute-start | bytes 175112 | tf_op jit(solution)/shard_map/ppermute | solution.py:30
  10.8 1.1 %collective-permute-start.1 = (bf16[8,7296]{1,0:T(8,128)(2,1)S(1)}, bf16[8,7296]{1,0:T(8,128)(2,1)S(1)}, u32[]{:S(2)}, u32[]{:S(2)}) collective-permute-start(bf16[8,7296]{1,0:T(8,128)(2,1)S(1)} %join.1.after_ref.loaded_ref.refs_0_), channel_id=1, source_target_pairs={{0,2},{1,5},{2,0},{3,7},{4,6},{5,1},{6,4},{7,3},{8,10},{9,13},{10,... | collective-permute-start | bytes 350216 | tf_op jit(solution)/shard_map/ppermute | solution.py:30
  11.9 0.6 %collective-permute-start.2 = (bf16[8,7296]{1,0:T(8,128)(2,1)S(1)}, bf16[8,7296]{1,0:T(8,128)(2,1)S(1)}, u32[]{:S(2)}, u32[]{:S(2)}) collective-permute-start(bf16[8,7296]{1,0:T(8,128)(2,1)S(1)} %join.1.after_ref.loaded_ref.refs_0_), channel_id=1, source_target_pairs={{0,4},{1,3},{2,6},{3,1},{4,0},{5,7},{6,2},{7,5},{8,12},{9,11},{10,... | collective-permute-start | bytes 350216 | tf_op jit(solution)/shard_map/ppermute | solution.py:30
  12.5 3.3 %attention.1 = bf16[1,128,512]{2,1,0:T(8,128)(2,1)S(1)} custom-call(bf16[8,7296]{1,0:T(8,128)(2,1)S(1)} %join.1.after_ref.loaded_ref.refs_0_, s32[1]{0:T(128)S(6)} %copy.13.lengths_ref, bf16[1,576,128]{2,1,0:T(8,128)(2,1)} %bitcast.11, bf16[1,576,1280]{2,1,0:T(8,128)(2,1)} %bitcast.9), custom_call_target="tpu_custom_call" | custom-call | flops 360000000 | bytes 1700000 | tf_op jit(solution)/shard_map/attention/pallas_call | solution.py:133
  15.8 0.1 pad_maximum_fusion.refs_3_
  15.9 0.1 collective-permute-start.8
  16.0 0.5 %collective-permute-start.5 = (bf16[8,7296]{1,0:T(8,128)(2,1)S(1)}, bf16[8,7296]{1,0:T(8,128)(2,1)S(1)}, u32[]{:S(2)}, u32[]{:S(2)}) collective-permute-start(bf16[8,7296]{1,0:T(8,128)(2,1)S(1)} %join.1.after_ref.loaded_ref.refs_0_), channel_id=1, source_target_pairs={{0,1},{1,0},{2,3},{3,2},{4,5},{5,4},{6,7},{7,6},{8,9},{9,8},{10,11... | collective-permute-start | bytes 350216 | tf_op jit(solution)/shard_map/ppermute | solution.py:30
  16.5 0.1 collective-permute-start.6
  16.6 0.1 collective-permute-done.2.refs_2_
  16.7 0.3 collective-permute-start.7
  17.0 0.3 collective-permute-done.8.refs_7_
  17.3 0.2 collective-permute-done.5.refs_4_
  17.5 0.3 collective-permute-done.6.refs_5_
  17.8 0.2 collective-permute-done.7.refs_6_
  18.0 1.8 %experts.1 = (f32[8,7168]{1,0:T(8,128)S(1)}, f32[8,7168]{1,0:T(8,128)S(1)}, f32[8,7168]{1,0:T(8,128)S(1)}, f32[8,7168]{1,0:T(8,128)S(1)}, bf16[8,7168]{1,0:T(8,1...) custom-call(bf16[8,7296]{1,0:T(8,128)(2,1)S(1)} %join.1.after_ref.loaded_ref.ref, ...), custom_call_target="tpu_custom_call" | custom-call | flops 2000000000 | bytes 500000 | tf_op jit(solution)/shard_map/experts/pallas_call | solution.py:202
  19.8 0.4 %collective-permute-start.10 = (bf16[8,7168]{1,0:T(8,128)(2,1)S(1)}, bf16[8,7168]{1,0:T(8,128)(2,1)S(1)}, u32[]{:S(2)}, u32[]{:S(2)}) collective-permute-start(bf16[8,7168]{1,0:T(8,128)(2,1)S(1)} %get-tuple-element.22), channel_id=1, source_target_pairs={{0,1},{1,0},{2,3},{3,2},{4,5},{5,4},{6,7},{7,6},{8,9},{9,8},{10,11... | collective-permute-start | bytes 344072 | tf_op jit(solution)/shard_map/ppermute | solution.py:30
  20.2 0.2 collective-permute-start.14
  20.4 0.3 collective-permute-start.12
  20.7 0.2 collective-permute-start.9
  20.9 0.3 collective-permute-done.10
  21.2 1.4 %collective-permute-start.11 = (bf16[8,7168]{1,0:T(8,128)(2,1)S(1)}, bf16[8,7168]{1,0:T(8,128)(2,1)S(1)}, u32[]{:S(2)}, u32[]{:S(2)}) collective-permute-start(bf16[8,7168]{1,0:T(8,128)(2,1)S(1)} %add_convert_fusion.2), channel_id=1, source_target_pairs={{0,2},{1,5},{2,0},{3,7},{4,6},{5,1},{6,4},{7,3},{8,10},{9,13},{10,... | collective-permute-start | bytes 344072 | tf_op jit(solution)/shard_map/ppermute | solution.py:30
  22.7 1.0 %collective-permute-start.13 = (bf16[8,7168]{1,0:T(8,128)(2,1)S(1)}, bf16[8,7168]{1,0:T(8,128)(2,1)S(1)}, u32[]{:S(2)}, u32[]{:S(2)}) collective-permute-start(bf16[8,7168]{1,0:T(8,128)(2,1)S(1)} %add_convert_fusion.1), channel_id=1, source_target_pairs={{0,4},{1,3},{2,6},{3,1},{4,0},{5,7},{6,2},{7,5},{8,12},{9,11},{10,... | collective-permute-start | bytes 344072 | tf_op jit(solution)/shard_map/ppermute | solution.py:30
  23.8 1.3 %collective-permute-start.16 = (bf16[4,7168]{1,0:T(4,128)(2,1)S(1)}, bf16[4,7168]{1,0:T(4,128)(2,1)S(1)}, u32[]{:S(2)}, u32[]{:S(2)}) collective-permute-start(bf16[4,7168]{1,0:T(4,128)(2,1)S(1)} %get-tuple-element.31), channel_id=1, source_target_pairs={{0,6},{1,7},{2,4},{3,5},{4,2},{5,3},{6,0},{7,1},{8,14},{9,15},{10,... | collective-permute-start | bytes 172040 | tf_op jit(solution)/shard_map/ppermute | solution.py:30
  25.1 0.9 %copy.12 = bf16[1,1,128,512]{3,1,2,0:T(2,128)(2,1)} copy(bf16[1,1,128,512]{3,2,1,0:T(8,128)(2,1)S(1)} %bitcast.7) | data formatting | bytes 262144
  26.0 1.7 %collective-permute-start.15 = (bf16[4,7168]{1,0:T(4,128)(2,1)S(1)}, bf16[4,7168]{1,0:T(4,128)(2,1)S(1)}, u32[]{:S(2)}, u32[]{:S(2)}) collective-permute-start(bf16[4,7168]{1,0:T(4,128)(2,1)S(1)} %get-tuple-element.30), channel_id=1, source_target_pairs={{0,6},{1,7},{2,4},{3,5},{4,2},{5,3},{6,0},{7,1},{8,14},{9,15},{10,... | collective-permute-start | bytes 172040 | tf_op jit(solution)/shard_map/ppermute | solution.py:30
  27.7 1.2 %collective-permute-done.16 = bf16[4,7168]{1,0:T(4,128)(2,1)S(1)} collective-permute-done((bf16[4,7168]{1,0:T(4,128)(2,1)S(1)}, bf16[4,7168]{1,0:T(4,128)(2,1)S(1)}, u32[]{:S(2)}, u32[]{:S(2)}) %collective-permute-start.16) | collective-permute-done | bytes 57376 | tf_op jit(solution)/shard_map/ppermute | solution.py:30
  29.1 2.8 %collective-permute-start.17 = (bf16[4,7168]{1,0:T(4,128)(2,1)S(1)}, bf16[4,7168]{1,0:T(4,128)(2,1)S(1)}, u32[]{:S(2)}, u32[]{:S(2)}) collective-permute-start(bf16[4,7168]{1,0:T(4,128)(2,1)S(1)} %fusion), channel_id=1, source_target_pairs={{0,8},{1,9},{2,10},{3,11},{4,12},{5,13},{6,14},{7,15},{8,0},{9,1},... | collective-permute-start | bytes 172040 | tf_op jit(solution)/shard_map/ppermute | solution.py:30
  31.8 2.4 %collective-permute-done.17 = bf16[4,7168]{1,0:T(4,128)(2,1)S(1)} collective-permute-done((bf16[4,7168]{1,0:T(4,128)(2,1)S(1)}, bf16[4,7168]{1,0:T(4,128)(2,1)S(1)}, u32[]{:S(2)}, u32[]{:S(2)}) %collective-permute-start.17) | collective-permute-done | bytes 57376 | tf_op jit(solution)/shard_map/ppermute | solution.py:30
  34.2 0.7 %fusion.2 = bf16[4,7168]{1,0:T(4,128)(2,1)} fusion(f32[8,7168]{1,0:T(8,128)S(1)} %convert_add_fusion, bf16[4,7168]{1,0:T(4,128)(2,1)S(1)} %collective-permute-done.17, bf16[4,7168]{1,0:T(4,128)(2,1)S(1)} %collective-permute-done.15), kind=kLoop, calls=%fused_computation.9 | loop fusion | flops 143360 | bytes 286720 | tf_op jit(solution)/shard_map/convert_element_type | solution.py:254
  (25 shorter events, 0.3 us)
Async XLA Ops:
  1.5 7.3 %collective-permute-start = (bf16[4,7296]{1,0:T(4,128)(2,1)S(1)}, bf16[4,7296]{1,0:T(4,128)(2,1)S(1)}, u32[]{:S(2)}, u32[]{:S(2)}) collective-permute-start(bf16[4,7296]{1,0:T(4,128)(2,1)S(1)} %pack.1.upper_ref), channel_id=1, source_target_pairs={{0,8},{1,9},{2,10},{3,11},{4,12},{5,13},{6,14},{7,15},{8,0},{9,1},... | collective-permute-start | bytes 175112 | tf_op jit(solution)/shard_map/ppermute | solution.py:30
  5.6 10.2 %collective-permute-start.3 = (bf16[4,7296]{1,0:T(4,128)(2,1)S(1)}, bf16[4,7296]{1,0:T(4,128)(2,1)S(1)}, u32[]{:S(2)}, u32[]{:S(2)}) collective-permute-start(bf16[4,7296]{1,0:T(4,128)(2,1)S(1)} %pack.1.upper_ref), channel_id=1, source_target_pairs={{0,6},{1,7},{2,4},{3,5},{4,2},{5,3},{6,0},{7,1},{8,14},{9,15},{10,... | collective-permute-start | bytes 175112 | tf_op jit(solution)/shard_map/ppermute | solution.py:30
  8.8 9.2 %copy-start.3 = (bf16[7168]{0:T(1024)(128)(2,1)S(1)}, bf16[7168]{0:T(1024)(128)(2,1)}, u32[]{:S(2)}) copy-start(bf16[7168]{0:T(1024)(128)(2,1)} %param.13) | copy-start | bytes 43012
  8.8 7.0 %collective-permute-start.4 = (bf16[4,7296]{1,0:T(4,128)(2,1)S(1)}, bf16[4,7296]{1,0:T(4,128)(2,1)S(1)}, u32[]{:S(2)}, u32[]{:S(2)}) collective-permute-start(bf16[4,7296]{1,0:T(4,128)(2,1)S(1)} %collective-permute-done.lower_ref), channel_id=1, source_target_pairs={{0,6},{1,7},{2,4},{3,5},{4,2},{5,3},{6,0},{7,1},{8,14},{9,15},{10,... | collective-permute-start | bytes 175112 | tf_op jit(solution)/shard_map/ppermute | solution.py:30
  10.7 7.3 %copy-start = (bf16[1,7168,256]{2,1,0:T(8,128)(2,1)S(1)}, bf16[1,7168,256]{2,1,0:T(8,128)(2,1)}, u32[]{:S(2)}) copy-start(bf16[1,7168,256]{2,1,0:T(8,128)(2,1)} %refs_9_.1) | copy-start | bytes 11010052
  10.7 7.3 %copy-start.1 = (bf16[1,7168,256]{2,1,0:T(8,128)(2,1)S(1)}, bf16[1,7168,256]{2,1,0:T(8,128)(2,1)}, u32[]{:S(2)}) copy-start(bf16[1,7168,256]{2,1,0:T(8,128)(2,1)} %refs_10_.1) | copy-start | bytes 11010052
  10.7 7.3 %copy-start.2 = (bf16[1,256,7168]{2,1,0:T(8,128)(2,1)S(1)}, bf16[1,256,7168]{2,1,0:T(8,128)(2,1)}, u32[]{:S(2)}) copy-start(bf16[1,256,7168]{2,1,0:T(8,128)(2,1)} %refs_11_.1) | copy-start | bytes 11010052
  10.8 5.2 %collective-permute-start.1 = (bf16[8,7296]{1,0:T(8,128)(2,1)S(1)}, bf16[8,7296]{1,0:T(8,128)(2,1)S(1)}, u32[]{:S(2)}, u32[]{:S(2)}) collective-permute-start(bf16[8,7296]{1,0:T(8,128)(2,1)S(1)} %join.1.after_ref.loaded_ref.refs_0_), channel_id=1, source_target_pairs={{0,2},{1,5},{2,0},{3,7},{4,6},{5,1},{6,4},{7,3},{8,10},{9,13},{10,... | collective-permute-start | bytes 350216 | tf_op jit(solution)/shard_map/ppermute | solution.py:30
  11.9 4.8 %collective-permute-start.2 = (bf16[8,7296]{1,0:T(8,128)(2,1)S(1)}, bf16[8,7296]{1,0:T(8,128)(2,1)S(1)}, u32[]{:S(2)}, u32[]{:S(2)}) collective-permute-start(bf16[8,7296]{1,0:T(8,128)(2,1)S(1)} %join.1.after_ref.loaded_ref.refs_0_), channel_id=1, source_target_pairs={{0,4},{1,3},{2,6},{3,1},{4,0},{5,7},{6,2},{7,5},{8,12},{9,11},{10,... | collective-permute-start | bytes 350216 | tf_op jit(solution)/shard_map/ppermute | solution.py:30
  15.9 1.4 %collective-permute-start.8 = (bf16[8,7296]{1,0:T(8,128)(2,1)S(1)}, bf16[8,7296]{1,0:T(8,128)(2,1)S(1)}, u32[]{:S(2)}, u32[]{:S(2)}) collective-permute-start(bf16[8,7296]{1,0:T(8,128)(2,1)S(1)} %pad_maximum_fusion.refs_3_), channel_id=1, source_target_pairs={{0,1},{1,0},{2,3},{3,2},{4,5},{5,4},{6,7},{7,6},{8,9},{9,8},{10,11... | collective-permute-start | bytes 350216 | tf_op jit(solution)/shard_map/ppermute | solution.py:30
  16.0 1.5 %collective-permute-start.5 = (bf16[8,7296]{1,0:T(8,128)(2,1)S(1)}, bf16[8,7296]{1,0:T(8,128)(2,1)S(1)}, u32[]{:S(2)}, u32[]{:S(2)}) collective-permute-start(bf16[8,7296]{1,0:T(8,128)(2,1)S(1)} %join.1.after_ref.loaded_ref.refs_0_), channel_id=1, source_target_pairs={{0,1},{1,0},{2,3},{3,2},{4,5},{5,4},{6,7},{7,6},{8,9},{9,8},{10,11... | collective-permute-start | bytes 350216 | tf_op jit(solution)/shard_map/ppermute | solution.py:30
  16.5 1.3 %collective-permute-start.6 = (bf16[8,7296]{1,0:T(8,128)(2,1)S(1)}, bf16[8,7296]{1,0:T(8,128)(2,1)S(1)}, u32[]{:S(2)}, u32[]{:S(2)}) collective-permute-start(bf16[8,7296]{1,0:T(8,128)(2,1)S(1)} %collective-permute-done.1.refs_1_), channel_id=1, source_target_pairs={{0,1},{1,0},{2,3},{3,2},{4,5},{5,4},{6,7},{7,6},{8,9},{9,8},{10,11... | collective-permute-start | bytes 350216 | tf_op jit(solution)/shard_map/ppermute | solution.py:30
  16.7 1.3 %collective-permute-start.7 = (bf16[8,7296]{1,0:T(8,128)(2,1)S(1)}, bf16[8,7296]{1,0:T(8,128)(2,1)S(1)}, u32[]{:S(2)}, u32[]{:S(2)}) collective-permute-start(bf16[8,7296]{1,0:T(8,128)(2,1)S(1)} %collective-permute-done.2.refs_2_), channel_id=1, source_target_pairs={{0,1},{1,0},{2,3},{3,2},{4,5},{5,4},{6,7},{7,6},{8,9},{9,8},{10,11... | collective-permute-start | bytes 350216 | tf_op jit(solution)/shard_map/ppermute | solution.py:30
  19.8 1.4 %collective-permute-start.10 = (bf16[8,7168]{1,0:T(8,128)(2,1)S(1)}, bf16[8,7168]{1,0:T(8,128)(2,1)S(1)}, u32[]{:S(2)}, u32[]{:S(2)}) collective-permute-start(bf16[8,7168]{1,0:T(8,128)(2,1)S(1)} %get-tuple-element.22), channel_id=1, source_target_pairs={{0,1},{1,0},{2,3},{3,2},{4,5},{5,4},{6,7},{7,6},{8,9},{9,8},{10,11... | collective-permute-start | bytes 344072 | tf_op jit(solution)/shard_map/ppermute | solution.py:30
  20.2 3.5 %collective-permute-start.14 = (bf16[8,7168]{1,0:T(8,128)(2,1)S(1)}, bf16[8,7168]{1,0:T(8,128)(2,1)S(1)}, u32[]{:S(2)}, u32[]{:S(2)}) collective-permute-start(bf16[8,7168]{1,0:T(8,128)(2,1)S(1)} %get-tuple-element.26), channel_id=1, source_target_pairs={{0,1},{1,0},{2,3},{3,2},{4,5},{5,4},{6,7},{7,6},{8,9},{9,8},{10,11... | collective-permute-start | bytes 344072 | tf_op jit(solution)/shard_map/ppermute | solution.py:30
  20.4 2.2 %collective-permute-start.12 = (bf16[8,7168]{1,0:T(8,128)(2,1)S(1)}, bf16[8,7168]{1,0:T(8,128)(2,1)S(1)}, u32[]{:S(2)}, u32[]{:S(2)}) collective-permute-start(bf16[8,7168]{1,0:T(8,128)(2,1)S(1)} %get-tuple-element.24), channel_id=1, source_target_pairs={{0,1},{1,0},{2,3},{3,2},{4,5},{5,4},{6,7},{7,6},{8,9},{9,8},{10,11... | collective-permute-start | bytes 344072 | tf_op jit(solution)/shard_map/ppermute | solution.py:30
  20.7 8.2 %collective-permute-start.9 = (bf16[8,7168]{1,0:T(8,128)(2,1)S(1)}, bf16[8,7168]{1,0:T(8,128)(2,1)S(1)}, u32[]{:S(2)}, u32[]{:S(2)}) collective-permute-start(bf16[8,7168]{1,0:T(8,128)(2,1)S(1)} %get-tuple-element.20), channel_id=1, source_target_pairs={{0,1},{1,0},{2,3},{3,2},{4,5},{5,4},{6,7},{7,6},{8,9},{9,8},{10,11... | collective-permute-start | bytes 344072 | tf_op jit(solution)/shard_map/ppermute | solution.py:30
  21.2 7.7 %collective-permute-start.11 = (bf16[8,7168]{1,0:T(8,128)(2,1)S(1)}, bf16[8,7168]{1,0:T(8,128)(2,1)S(1)}, u32[]{:S(2)}, u32[]{:S(2)}) collective-permute-start(bf16[8,7168]{1,0:T(8,128)(2,1)S(1)} %add_convert_fusion.2), channel_id=1, source_target_pairs={{0,2},{1,5},{2,0},{3,7},{4,6},{5,1},{6,4},{7,3},{8,10},{9,13},{10,... | collective-permute-start | bytes 344072 | tf_op jit(solution)/shard_map/ppermute | solution.py:30
  22.7 6.3 %collective-permute-start.13 = (bf16[8,7168]{1,0:T(8,128)(2,1)S(1)}, bf16[8,7168]{1,0:T(8,128)(2,1)S(1)}, u32[]{:S(2)}, u32[]{:S(2)}) collective-permute-start(bf16[8,7168]{1,0:T(8,128)(2,1)S(1)} %add_convert_fusion.1), channel_id=1, source_target_pairs={{0,4},{1,3},{2,6},{3,1},{4,0},{5,7},{6,2},{7,5},{8,12},{9,11},{10,... | collective-permute-start | bytes 344072 | tf_op jit(solution)/shard_map/ppermute | solution.py:30
  23.8 5.1 %collective-permute-start.16 = (bf16[4,7168]{1,0:T(4,128)(2,1)S(1)}, bf16[4,7168]{1,0:T(4,128)(2,1)S(1)}, u32[]{:S(2)}, u32[]{:S(2)}) collective-permute-start(bf16[4,7168]{1,0:T(4,128)(2,1)S(1)} %get-tuple-element.31), channel_id=1, source_target_pairs={{0,6},{1,7},{2,4},{3,5},{4,2},{5,3},{6,0},{7,1},{8,14},{9,15},{10,... | collective-permute-start | bytes 172040 | tf_op jit(solution)/shard_map/ppermute | solution.py:30
  26.0 5.9 %collective-permute-start.15 = (bf16[4,7168]{1,0:T(4,128)(2,1)S(1)}, bf16[4,7168]{1,0:T(4,128)(2,1)S(1)}, u32[]{:S(2)}, u32[]{:S(2)}) collective-permute-start(bf16[4,7168]{1,0:T(4,128)(2,1)S(1)} %get-tuple-element.30), channel_id=1, source_target_pairs={{0,6},{1,7},{2,4},{3,5},{4,2},{5,3},{6,0},{7,1},{8,14},{9,15},{10,... | collective-permute-start | bytes 172040 | tf_op jit(solution)/shard_map/ppermute | solution.py:30
  29.1 5.1 %collective-permute-start.17 = (bf16[4,7168]{1,0:T(4,128)(2,1)S(1)}, bf16[4,7168]{1,0:T(4,128)(2,1)S(1)}, u32[]{:S(2)}, u32[]{:S(2)}) collective-permute-start(bf16[4,7168]{1,0:T(4,128)(2,1)S(1)} %fusion), channel_id=1, source_target_pairs={{0,8},{1,9},{2,10},{3,11},{4,12},{5,13},{6,14},{7,15},{8,0},{9,1},... | collective-permute-start | bytes 172040 | tf_op jit(solution)/shard_map/ppermute | solution.py:30

commit v8 on v7

--- a/solution.py
+++ b/solution.py
@@ -100,15 +100,7 @@
     )(upper, lower)
 
 
-def attention_kernel(after_ref, lengths_ref, queries_hbm, cache_hbm, attended_ref, queries_ref, cache_ref, sem):
-    copies = [
-        pltpu.make_async_copy(queries_hbm, queries_ref, sem.at[0]),
-        pltpu.make_async_copy(cache_hbm, cache_ref, sem.at[1]),
-    ]
-    for copy in copies:
-        copy.start()
-    for copy in copies:
-        copy.wait()
+def attention_kernel(after_ref, lengths_ref, queries_ref, cache_ref, attended_ref):
     queries = queries_ref[0].T
     cached = cache_ref[0]
     scores = jnp.dot(queries, cached, preferred_element_type=jnp.float32) * softmax_scale
@@ -129,20 +121,15 @@
     heads = queries.shape[1]
     queries = jnp.swapaxes(queries, 1, 2)
     cache = jnp.swapaxes(cache, 1, 2)
-    hbm = pl.BlockSpec(memory_space=pltpu.HBM)
+    vmem = pl.BlockSpec(memory_space=pltpu.VMEM)
     return pl.pallas_call(
         attention_kernel,
         out_shape=jax.ShapeDtypeStruct((1, heads, VALUE_DIM), jnp.bfloat16),
-        in_specs=[pl.BlockSpec(memory_space=pl.ANY), pl.BlockSpec(memory_space=pltpu.SMEM), hbm, hbm],
-        scratch_shapes=[
-            pltpu.VMEM(queries.shape, queries.dtype),
-            pltpu.VMEM(cache.shape, cache.dtype),
-            pltpu.SemaphoreType.DMA((2,)),
-        ],
+        in_specs=[pl.BlockSpec(memory_space=pl.ANY), pl.BlockSpec(memory_space=pltpu.SMEM), vmem, vmem],
         compiler_params=pltpu.CompilerParams(vmem_limit_bytes=VMEM_LIMIT),
         cost_estimate=pl.CostEstimate(flops=360_000_000, bytes_accessed=1_700_000, transcendentals=164_000),
         name="attention",
-    )(after, lengths, *map(in_hbm, (queries, cache)))
+    )(after, lengths, queries, cache)
 
 
 def experts_kernel(picks, count, loaded_ref, *refs):
@@ -220,16 +207,17 @@
     for partners in far[:-1]:
         rows = jnp.concatenate([rows, trade(rows, partners)], axis=0)
     arrived = trade(rows, far[-1])
-    diagonal = trade(rows, near[2])
+    across = [far[-1][partner] for partner in near[2]]
+    beside = trade(rows, near[2])
+    beyond = trade(rows, across)
     rows = join(rows, arrived)
     attended = attention(rows, lengths, queries, cache)
     weights = (w_gate, w_up, w_down)
     pieces = [rows] + [trade(rows, partners) for partners in near[:2]]
-    pieces[1], attended = lax.optimization_barrier((pieces[1], attended))
-    pieces.append(jnp.concatenate([diagonal, trade(arrived, near[2])], axis=0))
+    beyond, attended = lax.optimization_barrier((beyond, attended))
+    pieces.append(jnp.concatenate([beside, beyond], axis=0))
     held, attended = lax.optimization_barrier((rows, attended))
     pieces += [trade(piece, core) for piece in [held] + pieces[1:]]
-
     outputs = experts(rows, pieces, routes.shape[1], gain, weights)
     own, other = outputs[:4], outputs[4:]
     sums = [mine + trade(theirs, core).astype(jnp.float32) for mine, theirs in zip(own[1:], other[1:])]

time: 35.1 us -> 35 us (level)
  Pallas kernels: 6.03 us -> 3.92 us
  waiting for transfers between devices: 5.1 us -> 6.15 us
  starting transfers between devices: 20.4 us -> 21.4 us
    pallas_call x1, Pallas kernels: 3.34 us -> 1.14 us  [attention(): pl.pallas_call(attention_kernel, out_shape=jax.ShapeDtypeStruct((1, heads...]
    ppermute x18, waiting for transfers between devices: 5.1 us -> 6.15 us  [trade(): return lax.ppermute(value, 'node', list(enumerate(partners)))]
    ppermute x18, starting transfers between devices: 20.4 us -> 21.4 us  [trade(): return lax.ppermute(value, 'node', list(enumerate(partners)))]
    unnamed x9 -> x13, local copies, waits for them, and re-layouts: 0.92 us -> 0.94 us
  transfers between devices with their start and end apart: 18 -> 18, of which waited for: 8 -> 7; matrix products, arithmetic and copies ran while one was open for 3% -> 3% of each run, Pallas kernels for 10% -> 3%
where the time goes in v8:
time: 35 us; the launch traced here: 34.8 us
  starting transfers between devices  21.4 us (61%)
  waiting for transfers between devices  6.15 us (18%)
  Pallas kernels  3.92 us (11%)
  between operations  1.45 us (4%)
  local copies, waits for them, and re-layouts  0.98 us (3%)
  other arithmetic  0.91 us (3%)
    ppermute x18, starting transfers between devices, trade(): return lax.ppermute(value, 'node', list(enumerate(partners)))  21.4 us
    ppermute x18, waiting for transfers between devices, trade(): return lax.ppermute(value, 'node', list(enumerate(partners)))  6.15 us
    pallas_call x1, Pallas kernels, experts(): pl.pallas_call(functools.partial(experts_kernel, picks, count), out_shape...  1.86 us
    pallas_call x1, Pallas kernels, attention(): pl.pallas_call(attention_kernel, out_shape=jax.ShapeDtypeStruct((1, heads...  1.14 us
    unnamed x13, local copies, waits for them, and re-layouts  0.94 us
    pallas_call x1, Pallas kernels, pack(): pl.pallas_call(pack_kernel, out_shape=jax.ShapeDtypeStruct((count, width...  0.88 us
  transfers between devices with their start and end apart: 18, of which 7 were waited for; matrix products, arithmetic and copies ran while one was open for 3% of the time, Pallas kernels for 3%

profile of v8, /device:TPU:0, one launch (start us, length us, event | category | flops | bytes accessed | tf_op | source)
XLA Modules:
  0.0 34.8 jit_solution(2015200484791245494)
XLA Ops:
  0.6 0.9 %pack.1.upper_ref = bf16[4,7296]{1,0:T(4,128)(2,1)S(1)} custom-call(bf16[4,7168]{1,0:T(4,128)(2,1)} %tokens_hbm.1, s32[2,4]{1,0:T(2,128)} %bitcast.12, f32[2,4]{1,0:T(2,128)} %bitcast.13), custom_call_target="tpu_custom_call" | custom-call | tf_op jit(solution)/shard_map/pack/pallas_call | solution.py:71
  1.5 4.1 %collective-permute-start = (bf16[4,7296]{1,0:T(4,128)(2,1)S(1)}, bf16[4,7296]{1,0:T(4,128)(2,1)S(1)}, u32[]{:S(2)}, u32[]{:S(2)}) collective-permute-start(bf16[4,7296]{1,0:T(4,128)(2,1)S(1)} %pack.1.upper_ref), channel_id=1, source_target_pairs={{0,8},{1,9},{2,10},{3,11},{4,12},{5,13},{6,14},{7,15},{8,0},{9,1},... | collective-permute-start | bytes 175112 | tf_op jit(solution)/shard_map/ppermute | solution.py:30
  5.6 2.3 %collective-permute-start.4 = (bf16[4,7296]{1,0:T(4,128)(2,1)S(1)}, bf16[4,7296]{1,0:T(4,128)(2,1)S(1)}, u32[]{:S(2)}, u32[]{:S(2)}) collective-permute-start(bf16[4,7296]{1,0:T(4,128)(2,1)S(1)} %pack.1.upper_ref), channel_id=1, source_target_pairs={{0,14},{1,15},{2,12},{3,13},{4,10},{5,11},{6,8},{7,9},{8,6},{9,7},... | collective-permute-start | bytes 175112 | tf_op jit(solution)/shard_map/ppermute | solution.py:30
  7.9 0.2 collective-permute-start.3
  8.8 0.0 copy-start.3
  8.9 1.9 %collective-permute-start.1 = (bf16[8,7296]{1,0:T(8,128)(2,1)S(1)}, bf16[8,7296]{1,0:T(8,128)(2,1)S(1)}, u32[]{:S(2)}, u32[]{:S(2)}) collective-permute-start(bf16[8,7296]{1,0:T(8,128)(2,1)S(1)} %join.1.after_ref.loaded_ref.refs_0_), channel_id=1, source_target_pairs={{0,2},{1,5},{2,0},{3,7},{4,6},{5,1},{6,4},{7,3},{8,10},{9,13},{10,... | collective-permute-start | bytes 350216 | tf_op jit(solution)/shard_map/ppermute | solution.py:30
  10.8 1.8 %collective-permute-start.2 = (bf16[8,7296]{1,0:T(8,128)(2,1)S(1)}, bf16[8,7296]{1,0:T(8,128)(2,1)S(1)}, u32[]{:S(2)}, u32[]{:S(2)}) collective-permute-start(bf16[8,7296]{1,0:T(8,128)(2,1)S(1)} %join.1.after_ref.loaded_ref.refs_0_), channel_id=1, source_target_pairs={{0,4},{1,3},{2,6},{3,1},{4,0},{5,7},{6,2},{7,5},{8,12},{9,11},{10,... | collective-permute-start | bytes 350216 | tf_op jit(solution)/shard_map/ppermute | solution.py:30
  12.7 1.1 %attention.1 = bf16[1,128,512]{2,1,0:T(8,128)(2,1)S(1)} custom-call(bf16[8,7296]{1,0:T(8,128)(2,1)S(1)} %join.1.after_ref.loaded_ref.refs_0_, s32[1]{0:T(128)S(6)} %copy.13.lengths_ref, bf16[1,576,128]{2,1,0:T(8,128)(2,1)S(1)} %bitcast.9, bf16[1,576,1280]{2,1,0:T(8,128)(2,1)S(1)} %bitcast.7), custom_call_target="tpu_custom_call" | custom-call | flops 360000000 | bytes 1700000 | tf_op jit(solution)/shard_map/attention/pallas_call | solution.py:125
  13.9 0.1 collective-permute-start.5
  13.9 0.1 collective-permute-done.3
  14.1 0.1 pad_maximum_fusion.refs_3_
  14.1 0.4 %collective-permute-start.8 = (bf16[8,7296]{1,0:T(8,128)(2,1)S(1)}, bf16[8,7296]{1,0:T(8,128)(2,1)S(1)}, u32[]{:S(2)}, u32[]{:S(2)}) collective-permute-start(bf16[8,7296]{1,0:T(8,128)(2,1)S(1)} %pad_maximum_fusion.refs_3_), channel_id=1, source_target_pairs={{0,1},{1,0},{2,3},{3,2},{4,5},{5,4},{6,7},{7,6},{8,9},{9,8},{10,11... | collective-permute-start | bytes 350216 | tf_op jit(solution)/shard_map/ppermute | solution.py:30
  14.6 1.2 %collective-permute-done.1.refs_1_ = bf16[8,7296]{1,0:T(8,128)(2,1)S(1)} collective-permute-done((bf16[8,7296]{1,0:T(8,128)(2,1)S(1)}, bf16[8,7296]{1,0:T(8,128)(2,1)S(1)}, u32[]{:S(2)}, u32[]{:S(2)}) %collective-permute-start.1) | collective-permute-done | bytes 116768 | tf_op jit(solution)/shard_map/ppermute | solution.py:30
  15.7 0.5 %collective-permute-start.7 = (bf16[8,7296]{1,0:T(8,128)(2,1)S(1)}, bf16[8,7296]{1,0:T(8,128)(2,1)S(1)}, u32[]{:S(2)}, u32[]{:S(2)}) collective-permute-start(bf16[8,7296]{1,0:T(8,128)(2,1)S(1)} %collective-permute-done.2.refs_2_), channel_id=1, source_target_pairs={{0,1},{1,0},{2,3},{3,2},{4,5},{5,4},{6,7},{7,6},{8,9},{9,8},{10,11... | collective-permute-start | bytes 350216 | tf_op jit(solution)/shard_map/ppermute | solution.py:30
  16.2 0.8 %collective-permute-done.6.refs_5_ = bf16[8,7296]{1,0:T(8,128)(2,1)S(1)} collective-permute-done((bf16[8,7296]{1,0:T(8,128)(2,1)S(1)}, bf16[8,7296]{1,0:T(8,128)(2,1)S(1)}, u32[]{:S(2)}, u32[]{:S(2)}) %collective-permute-start.6) | collective-permute-done | bytes 116768 | tf_op jit(solution)/shard_map/ppermute | solution.py:30
  17.1 0.2 collective-permute-done.7.refs_6_
  17.2 1.9 %experts.1 = (f32[8,7168]{1,0:T(8,128)S(1)}, f32[8,7168]{1,0:T(8,128)S(1)}, f32[8,7168]{1,0:T(8,128)S(1)}, f32[8,7168]{1,0:T(8,128)S(1)}, bf16[8,7168]{1,0:T(8,1...) custom-call(bf16[8,7296]{1,0:T(8,128)(2,1)S(1)} %join.1.after_ref.loaded_ref.ref, ...), custom_call_target="tpu_custom_call" | custom-call | flops 2000000000 | bytes 500000 | tf_op jit(solution)/shard_map/experts/pallas_call | solution.py:189
  19.1 0.4 %collective-permute-start.10 = (bf16[8,7168]{1,0:T(8,128)(2,1)S(1)}, bf16[8,7168]{1,0:T(8,128)(2,1)S(1)}, u32[]{:S(2)}, u32[]{:S(2)}) collective-permute-start(bf16[8,7168]{1,0:T(8,128)(2,1)S(1)} %get-tuple-element.22), channel_id=1, source_target_pairs={{0,1},{1,0},{2,3},{3,2},{4,5},{5,4},{6,7},{7,6},{8,9},{9,8},{10,11... | collective-permute-start | bytes 344072 | tf_op jit(solution)/shard_map/ppermute | solution.py:30
  19.5 0.2 collective-permute-start.14
  19.7 0.3 collective-permute-start.12
  20.0 0.2 collective-permute-start.9
  20.2 0.3 collective-permute-done.10
  20.5 1.3 %collective-permute-start.11 = (bf16[8,7168]{1,0:T(8,128)(2,1)S(1)}, bf16[8,7168]{1,0:T(8,128)(2,1)S(1)}, u32[]{:S(2)}, u32[]{:S(2)}) collective-permute-start(bf16[8,7168]{1,0:T(8,128)(2,1)S(1)} %add_convert_fusion.2), channel_id=1, source_target_pairs={{0,2},{1,5},{2,0},{3,7},{4,6},{5,1},{6,4},{7,3},{8,10},{9,13},{10,... | collective-permute-start | bytes 344072 | tf_op jit(solution)/shard_map/ppermute | solution.py:30
  21.8 1.4 %collective-permute-start.13 = (bf16[8,7168]{1,0:T(8,128)(2,1)S(1)}, bf16[8,7168]{1,0:T(8,128)(2,1)S(1)}, u32[]{:S(2)}, u32[]{:S(2)}) collective-permute-start(bf16[8,7168]{1,0:T(8,128)(2,1)S(1)} %add_convert_fusion.1), channel_id=1, source_target_pairs={{0,4},{1,3},{2,6},{3,1},{4,0},{5,7},{6,2},{7,5},{8,12},{9,11},{10,... | collective-permute-start | bytes 344072 | tf_op jit(solution)/shard_map/ppermute | solution.py:30
  23.3 1.1 %collective-permute-start.16 = (bf16[4,7168]{1,0:T(4,128)(2,1)S(1)}, bf16[4,7168]{1,0:T(4,128)(2,1)S(1)}, u32[]{:S(2)}, u32[]{:S(2)}) collective-permute-start(bf16[4,7168]{1,0:T(4,128)(2,1)S(1)} %get-tuple-element.31), channel_id=1, source_target_pairs={{0,6},{1,7},{2,4},{3,5},{4,2},{5,3},{6,0},{7,1},{8,14},{9,15},{10,... | collective-permute-start | bytes 172040 | tf_op jit(solution)/shard_map/ppermute | solution.py:30
  24.3 0.9 %copy.12 = bf16[1,1,128,512]{3,1,2,0:T(2,128)(2,1)} copy(bf16[1,1,128,512]{3,2,1,0:T(8,128)(2,1)S(1)} %bitcast.8) | data formatting | bytes 262144
  25.2 1.9 %collective-permute-start.15 = (bf16[4,7168]{1,0:T(4,128)(2,1)S(1)}, bf16[4,7168]{1,0:T(4,128)(2,1)S(1)}, u32[]{:S(2)}, u32[]{:S(2)}) collective-permute-start(bf16[4,7168]{1,0:T(4,128)(2,1)S(1)} %get-tuple-element.30), channel_id=1, source_target_pairs={{0,6},{1,7},{2,4},{3,5},{4,2},{5,3},{6,0},{7,1},{8,14},{9,15},{10,... | collective-permute-start | bytes 172040 | tf_op jit(solution)/shard_map/ppermute | solution.py:30
  27.2 1.4 %collective-permute-done.16 = bf16[4,7168]{1,0:T(4,128)(2,1)S(1)} collective-permute-done((bf16[4,7168]{1,0:T(4,128)(2,1)S(1)}, bf16[4,7168]{1,0:T(4,128)(2,1)S(1)}, u32[]{:S(2)}, u32[]{:S(2)}) %collective-permute-start.16) | collective-permute-done | bytes 57376 | tf_op jit(solution)/shard_map/ppermute | solution.py:30
  28.6 0.1 convert_add_fusion
  28.7 3.3 %collective-permute-start.17 = (bf16[4,7168]{1,0:T(4,128)(2,1)S(1)}, bf16[4,7168]{1,0:T(4,128)(2,1)S(1)}, u32[]{:S(2)}, u32[]{:S(2)}) collective-permute-start(bf16[4,7168]{1,0:T(4,128)(2,1)S(1)} %fusion), channel_id=1, source_target_pairs={{0,8},{1,9},{2,10},{3,11},{4,12},{5,13},{6,14},{7,15},{8,0},{9,1},... | collective-permute-start | bytes 172040 | tf_op jit(solution)/shard_map/ppermute | solution.py:30
  31.9 2.2 %collective-permute-done.17 = bf16[4,7168]{1,0:T(4,128)(2,1)S(1)} collective-permute-done((bf16[4,7168]{1,0:T(4,128)(2,1)S(1)}, bf16[4,7168]{1,0:T(4,128)(2,1)S(1)}, u32[]{:S(2)}, u32[]{:S(2)}) %collective-permute-start.17) | collective-permute-done | bytes 57376 | tf_op jit(solution)/shard_map/ppermute | solution.py:30
  34.1 0.7 %fusion.2 = bf16[4,7168]{1,0:T(4,128)(2,1)} fusion(f32[8,7168]{1,0:T(8,128)S(1)} %convert_add_fusion, bf16[4,7168]{1,0:T(4,128)(2,1)S(1)} %collective-permute-done.17, bf16[4,7168]{1,0:T(4,128)(2,1)S(1)} %collective-permute-done.15), kind=kLoop, calls=%fused_computation.9 | loop fusion | flops 143360 | bytes 286720 | tf_op jit(solution)/shard_map/convert_element_type | solution.py:242
  (29 shorter events, 0.3 us)
Async XLA Ops:
  1.5 7.3 %collective-permute-start = (bf16[4,7296]{1,0:T(4,128)(2,1)S(1)}, bf16[4,7296]{1,0:T(4,128)(2,1)S(1)}, u32[]{:S(2)}, u32[]{:S(2)}) collective-permute-start(bf16[4,7296]{1,0:T(4,128)(2,1)S(1)} %pack.1.upper_ref), channel_id=1, source_target_pairs={{0,8},{1,9},{2,10},{3,11},{4,12},{5,13},{6,14},{7,15},{8,0},{9,1},... | collective-permute-start | bytes 175112 | tf_op jit(solution)/shard_map/ppermute | solution.py:30
  5.6 8.2 %collective-permute-start.4 = (bf16[4,7296]{1,0:T(4,128)(2,1)S(1)}, bf16[4,7296]{1,0:T(4,128)(2,1)S(1)}, u32[]{:S(2)}, u32[]{:S(2)}) collective-permute-start(bf16[4,7296]{1,0:T(4,128)(2,1)S(1)} %pack.1.upper_ref), channel_id=1, source_target_pairs={{0,14},{1,15},{2,12},{3,13},{4,10},{5,11},{6,8},{7,9},{8,6},{9,7},... | collective-permute-start | bytes 175112 | tf_op jit(solution)/shard_map/ppermute | solution.py:30
  7.9 6.2 %collective-permute-start.3 = (bf16[4,7296]{1,0:T(4,128)(2,1)S(1)}, bf16[4,7296]{1,0:T(4,128)(2,1)S(1)}, u32[]{:S(2)}, u32[]{:S(2)}) collective-permute-start(bf16[4,7296]{1,0:T(4,128)(2,1)S(1)} %pack.1.upper_ref), channel_id=1, source_target_pairs={{0,6},{1,7},{2,4},{3,5},{4,2},{5,3},{6,0},{7,1},{8,14},{9,15},{10,... | collective-permute-start | bytes 175112 | tf_op jit(solution)/shard_map/ppermute | solution.py:30
  8.8 3.9 %copy-start.3 = (bf16[1,1280,576]{1,2,0:T(8,128)(2,1)S(1)}, bf16[1,1280,576]{1,2,0:T(8,128)(2,1)}, u32[]{:S(2)}) copy-start(bf16[1,1280,576]{1,2,0:T(8,128)(2,1)} %param.18) | copy-start | bytes 4423684
  8.8 3.9 %copy-start.4 = (bf16[1,128,576]{1,2,0:T(8,128)(2,1)S(1)}, bf16[1,128,576]{1,2,0:T(8,128)(2,1)}, u32[]{:S(2)}) copy-start(bf16[1,128,576]{1,2,0:T(8,128)(2,1)} %param.17) | copy-start | bytes 442372
  8.8 8.4 %copy-start.5 = (bf16[7168]{0:T(1024)(128)(2,1)S(1)}, bf16[7168]{0:T(1024)(128)(2,1)}, u32[]{:S(2)}) copy-start(bf16[7168]{0:T(1024)(128)(2,1)} %param.13) | copy-start | bytes 43012
  8.8 8.4 %copy-start = (bf16[1,7168,256]{2,1,0:T(8,128)(2,1)S(1)}, bf16[1,7168,256]{2,1,0:T(8,128)(2,1)}, u32[]{:S(2)}) copy-start(bf16[1,7168,256]{2,1,0:T(8,128)(2,1)} %refs_9_.1) | copy-start | bytes 11010052
  8.8 8.4 %copy-start.1 = (bf16[1,7168,256]{2,1,0:T(8,128)(2,1)S(1)}, bf16[1,7168,256]{2,1,0:T(8,128)(2,1)}, u32[]{:S(2)}) copy-start(bf16[1,7168,256]{2,1,0:T(8,128)(2,1)} %refs_10_.1) | copy-start | bytes 11010052
  8.9 8.4 %copy-start.2 = (bf16[1,256,7168]{2,1,0:T(8,128)(2,1)S(1)}, bf16[1,256,7168]{2,1,0:T(8,128)(2,1)}, u32[]{:S(2)}) copy-start(bf16[1,256,7168]{2,1,0:T(8,128)(2,1)} %refs_11_.1) | copy-start | bytes 11010052
  8.9 6.8 %collective-permute-start.1 = (bf16[8,7296]{1,0:T(8,128)(2,1)S(1)}, bf16[8,7296]{1,0:T(8,128)(2,1)S(1)}, u32[]{:S(2)}, u32[]{:S(2)}) collective-permute-start(bf16[8,7296]{1,0:T(8,128)(2,1)S(1)} %join.1.after_ref.loaded_ref.refs_0_), channel_id=1, source_target_pairs={{0,2},{1,5},{2,0},{3,7},{4,6},{5,1},{6,4},{7,3},{8,10},{9,13},{10,... | collective-permute-start | bytes 350216 | tf_op jit(solution)/shard_map/ppermute | solution.py:30
  10.8 4.9 %collective-permute-start.2 = (bf16[8,7296]{1,0:T(8,128)(2,1)S(1)}, bf16[8,7296]{1,0:T(8,128)(2,1)S(1)}, u32[]{:S(2)}, u32[]{:S(2)}) collective-permute-start(bf16[8,7296]{1,0:T(8,128)(2,1)S(1)} %join.1.after_ref.loaded_ref.refs_0_), channel_id=1, source_target_pairs={{0,4},{1,3},{2,6},{3,1},{4,0},{5,7},{6,2},{7,5},{8,12},{9,11},{10,... | collective-permute-start | bytes 350216 | tf_op jit(solution)/shard_map/ppermute | solution.py:30
  13.9 2.4 %collective-permute-start.5 = (bf16[8,7296]{1,0:T(8,128)(2,1)S(1)}, bf16[8,7296]{1,0:T(8,128)(2,1)S(1)}, u32[]{:S(2)}, u32[]{:S(2)}) collective-permute-start(bf16[8,7296]{1,0:T(8,128)(2,1)S(1)} %join.1.after_ref.loaded_ref.refs_0_), channel_id=1, source_target_pairs={{0,1},{1,0},{2,3},{3,2},{4,5},{5,4},{6,7},{7,6},{8,9},{9,8},{10,11... | collective-permute-start | bytes 350216 | tf_op jit(solution)/shard_map/ppermute | solution.py:30
  14.1 2.1 %collective-permute-start.8 = (bf16[8,7296]{1,0:T(8,128)(2,1)S(1)}, bf16[8,7296]{1,0:T(8,128)(2,1)S(1)}, u32[]{:S(2)}, u32[]{:S(2)}) collective-permute-start(bf16[8,7296]{1,0:T(8,128)(2,1)S(1)} %pad_maximum_fusion.refs_3_), channel_id=1, source_target_pairs={{0,1},{1,0},{2,3},{3,2},{4,5},{5,4},{6,7},{7,6},{8,9},{9,8},{10,11... | collective-permute-start | bytes 350216 | tf_op jit(solution)/shard_map/ppermute | solution.py:30
  15.7 1.3 %collective-permute-start.6 = (bf16[8,7296]{1,0:T(8,128)(2,1)S(1)}, bf16[8,7296]{1,0:T(8,128)(2,1)S(1)}, u32[]{:S(2)}, u32[]{:S(2)}) collective-permute-start(bf16[8,7296]{1,0:T(8,128)(2,1)S(1)} %collective-permute-done.1.refs_1_), channel_id=1, source_target_pairs={{0,1},{1,0},{2,3},{3,2},{4,5},{5,4},{6,7},{7,6},{8,9},{9,8},{10,11... | collective-permute-start | bytes 350216 | tf_op jit(solution)/shard_map/ppermute | solution.py:30
  15.7 1.5 %collective-permute-start.7 = (bf16[8,7296]{1,0:T(8,128)(2,1)S(1)}, bf16[8,7296]{1,0:T(8,128)(2,1)S(1)}, u32[]{:S(2)}, u32[]{:S(2)}) collective-permute-start(bf16[8,7296]{1,0:T(8,128)(2,1)S(1)} %collective-permute-done.2.refs_2_), channel_id=1, source_target_pairs={{0,1},{1,0},{2,3},{3,2},{4,5},{5,4},{6,7},{7,6},{8,9},{9,8},{10,11... | collective-permute-start | bytes 350216 | tf_op jit(solution)/shard_map/ppermute | solution.py:30
  19.1 1.4 %collective-permute-start.10 = (bf16[8,7168]{1,0:T(8,128)(2,1)S(1)}, bf16[8,7168]{1,0:T(8,128)(2,1)S(1)}, u32[]{:S(2)}, u32[]{:S(2)}) collective-permute-start(bf16[8,7168]{1,0:T(8,128)(2,1)S(1)} %get-tuple-element.22), channel_id=1, source_target_pairs={{0,1},{1,0},{2,3},{3,2},{4,5},{5,4},{6,7},{7,6},{8,9},{9,8},{10,11... | collective-permute-start | bytes 344072 | tf_op jit(solution)/shard_map/ppermute | solution.py:30
  19.5 3.7 %collective-permute-start.14 = (bf16[8,7168]{1,0:T(8,128)(2,1)S(1)}, bf16[8,7168]{1,0:T(8,128)(2,1)S(1)}, u32[]{:S(2)}, u32[]{:S(2)}) collective-permute-start(bf16[8,7168]{1,0:T(8,128)(2,1)S(1)} %get-tuple-element.26), channel_id=1, source_target_pairs={{0,1},{1,0},{2,3},{3,2},{4,5},{5,4},{6,7},{7,6},{8,9},{9,8},{10,11... | collective-permute-start | bytes 344072 | tf_op jit(solution)/shard_map/ppermute | solution.py:30
  19.7 2.1 %collective-permute-start.12 = (bf16[8,7168]{1,0:T(8,128)(2,1)S(1)}, bf16[8,7168]{1,0:T(8,128)(2,1)S(1)}, u32[]{:S(2)}, u32[]{:S(2)}) collective-permute-start(bf16[8,7168]{1,0:T(8,128)(2,1)S(1)} %get-tuple-element.24), channel_id=1, source_target_pairs={{0,1},{1,0},{2,3},{3,2},{4,5},{5,4},{6,7},{7,6},{8,9},{9,8},{10,11... | collective-permute-start | bytes 344072 | tf_op jit(solution)/shard_map/ppermute | solution.py:30
  20.0 8.5 %collective-permute-start.9 = (bf16[8,7168]{1,0:T(8,128)(2,1)S(1)}, bf16[8,7168]{1,0:T(8,128)(2,1)S(1)}, u32[]{:S(2)}, u32[]{:S(2)}) collective-permute-start(bf16[8,7168]{1,0:T(8,128)(2,1)S(1)} %get-tuple-element.20), channel_id=1, source_target_pairs={{0,1},{1,0},{2,3},{3,2},{4,5},{5,4},{6,7},{7,6},{8,9},{9,8},{10,11... | collective-permute-start | bytes 344072 | tf_op jit(solution)/shard_map/ppermute | solution.py:30
  20.5 8.0 %collective-permute-start.11 = (bf16[8,7168]{1,0:T(8,128)(2,1)S(1)}, bf16[8,7168]{1,0:T(8,128)(2,1)S(1)}, u32[]{:S(2)}, u32[]{:S(2)}) collective-permute-start(bf16[8,7168]{1,0:T(8,128)(2,1)S(1)} %add_convert_fusion.2), channel_id=1, source_target_pairs={{0,2},{1,5},{2,0},{3,7},{4,6},{5,1},{6,4},{7,3},{8,10},{9,13},{10,... | collective-permute-start | bytes 344072 | tf_op jit(solution)/shard_map/ppermute | solution.py:30
  21.8 6.7 %collective-permute-start.13 = (bf16[8,7168]{1,0:T(8,128)(2,1)S(1)}, bf16[8,7168]{1,0:T(8,128)(2,1)S(1)}, u32[]{:S(2)}, u32[]{:S(2)}) collective-permute-start(bf16[8,7168]{1,0:T(8,128)(2,1)S(1)} %add_convert_fusion.1), channel_id=1, source_target_pairs={{0,4},{1,3},{2,6},{3,1},{4,0},{5,7},{6,2},{7,5},{8,12},{9,11},{10,... | collective-permute-start | bytes 344072 | tf_op jit(solution)/shard_map/ppermute | solution.py:30
  23.3 5.3 %collective-permute-start.16 = (bf16[4,7168]{1,0:T(4,128)(2,1)S(1)}, bf16[4,7168]{1,0:T(4,128)(2,1)S(1)}, u32[]{:S(2)}, u32[]{:S(2)}) collective-permute-start(bf16[4,7168]{1,0:T(4,128)(2,1)S(1)} %get-tuple-element.31), channel_id=1, source_target_pairs={{0,6},{1,7},{2,4},{3,5},{4,2},{5,3},{6,0},{7,1},{8,14},{9,15},{10,... | collective-permute-start | bytes 172040 | tf_op jit(solution)/shard_map/ppermute | solution.py:30
  25.2 6.7 %collective-permute-start.15 = (bf16[4,7168]{1,0:T(4,128)(2,1)S(1)}, bf16[4,7168]{1,0:T(4,128)(2,1)S(1)}, u32[]{:S(2)}, u32[]{:S(2)}) collective-permute-start(bf16[4,7168]{1,0:T(4,128)(2,1)S(1)} %get-tuple-element.30), channel_id=1, source_target_pairs={{0,6},{1,7},{2,4},{3,5},{4,2},{5,3},{6,0},{7,1},{8,14},{9,15},{10,... | collective-permute-start | bytes 172040 | tf_op jit(solution)/shard_map/ppermute | solution.py:30
  28.7 5.4 %collective-permute-start.17 = (bf16[4,7168]{1,0:T(4,128)(2,1)S(1)}, bf16[4,7168]{1,0:T(4,128)(2,1)S(1)}, u32[]{:S(2)}, u32[]{:S(2)}) collective-permute-start(bf16[4,7168]{1,0:T(4,128)(2,1)S(1)} %fusion), channel_id=1, source_target_pairs={{0,8},{1,9},{2,10},{3,11},{4,12},{5,13},{6,14},{7,15},{8,0},{9,1},... | collective-permute-start | bytes 172040 | tf_op jit(solution)/shard_map/ppermute | solution.py:30

commit v9 on v8

--- a/solution.py
+++ b/solution.py
@@ -214,10 +214,9 @@
     attended = attention(rows, lengths, queries, cache)
     weights = (w_gate, w_up, w_down)
     pieces = [rows] + [trade(rows, partners) for partners in near[:2]]
-    beyond, attended = lax.optimization_barrier((beyond, attended))
+    beside, attended = lax.optimization_barrier((beside, attended))
     pieces.append(jnp.concatenate([beside, beyond], axis=0))
-    held, attended = lax.optimization_barrier((rows, attended))
-    pieces += [trade(piece, core) for piece in [held] + pieces[1:]]
+    pieces += [trade(piece, core) for piece in pieces]
     outputs = experts(rows, pieces, routes.shape[1], gain, weights)
     own, other = outputs[:4], outputs[4:]
     sums = [mine + trade(theirs, core).astype(jnp.float32) for mine, theirs in zip(own[1:], other[1:])]

time: 35 us -> 34.3 us (0.980)
  starting transfers between devices: 21.4 us -> 19.4 us
  waiting for transfers between devices: 6.15 us -> 7.52 us
    ppermute x18, starting transfers between devices: 21.4 us -> 19.4 us  [trade(): return lax.ppermute(value, 'node', list(enumerate(partners)))]
    ppermute x18, waiting for transfers between devices: 6.15 us -> 7.52 us  [trade(): return lax.ppermute(value, 'node', list(enumerate(partners)))]
where the time goes in v9:
time: 34.3 us; the launch traced here: 34.2 us
  starting transfers between devices  19.4 us (57%)
  waiting for transfers between devices  7.52 us (22%)
  Pallas kernels  3.92 us (11%)
  between operations  1.46 us (4%)
  local copies, waits for them, and re-layouts  0.98 us (3%)
  other arithmetic  0.91 us (3%)
    ppermute x18, starting transfers between devices, trade(): return lax.ppermute(value, 'node', list(enumerate(partners)))  19.4 us
    ppermute x18, waiting for transfers between devices, trade(): return lax.ppermute(value, 'node', list(enumerate(partners)))  7.52 us
    pallas_call x1, Pallas kernels, experts(): pl.pallas_call(functools.partial(experts_kernel, picks, count), out_shape...  1.86 us
    pallas_call x1, Pallas kernels, attention(): pl.pallas_call(attention_kernel, out_shape=jax.ShapeDtypeStruct((1, heads...  1.15 us
    unnamed x13, local copies, waits for them, and re-layouts  0.94 us
    pallas_call x1, Pallas kernels, pack(): pl.pallas_call(pack_kernel, out_shape=jax.ShapeDtypeStruct((count, width...  0.88 us
  transfers between devices with their start and end apart: 18, of which 7 were waited for; matrix products, arithmetic and copies ran while one was open for 3% of the time, Pallas kernels for 3%

profile of v9, /device:TPU:0, one launch (start us, length us, event | category | flops | bytes accessed | tf_op | source)
XLA Modules:
  0.0 34.2 jit_solution(16135904333382799669)
XLA Ops:
  0.6 0.9 %pack.1.upper_ref = bf16[4,7296]{1,0:T(4,128)(2,1)S(1)} custom-call(bf16[4,7168]{1,0:T(4,128)(2,1)} %tokens_hbm.1, s32[2,4]{1,0:T(2,128)} %bitcast.12, f32[2,4]{1,0:T(2,128)} %bitcast.13), custom_call_target="tpu_custom_call" | custom-call | tf_op jit(solution)/shard_map/pack/pallas_call | solution.py:71
  1.5 4.1 %collective-permute-start = (bf16[4,7296]{1,0:T(4,128)(2,1)S(1)}, bf16[4,7296]{1,0:T(4,128)(2,1)S(1)}, u32[]{:S(2)}, u32[]{:S(2)}) collective-permute-start(bf16[4,7296]{1,0:T(4,128)(2,1)S(1)} %pack.1.upper_ref), channel_id=1, source_target_pairs={{0,8},{1,9},{2,10},{3,11},{4,12},{5,13},{6,14},{7,15},{8,0},{9,1},... | collective-permute-start | bytes 175112 | tf_op jit(solution)/shard_map/ppermute | solution.py:30
  5.6 2.5 %collective-permute-start.3 = (bf16[4,7296]{1,0:T(4,128)(2,1)S(1)}, bf16[4,7296]{1,0:T(4,128)(2,1)S(1)}, u32[]{:S(2)}, u32[]{:S(2)}) collective-permute-start(bf16[4,7296]{1,0:T(4,128)(2,1)S(1)} %pack.1.upper_ref), channel_id=1, source_target_pairs={{0,6},{1,7},{2,4},{3,5},{4,2},{5,3},{6,0},{7,1},{8,14},{9,15},{10,... | collective-permute-start | bytes 175112 | tf_op jit(solution)/shard_map/ppermute | solution.py:30
  8.8 0.0 copy-start.3
  8.8 0.0 copy-start.4
  8.9 1.7 %collective-permute-start.1 = (bf16[8,7296]{1,0:T(8,128)(2,1)S(1)}, bf16[8,7296]{1,0:T(8,128)(2,1)S(1)}, u32[]{:S(2)}, u32[]{:S(2)}) collective-permute-start(bf16[8,7296]{1,0:T(8,128)(2,1)S(1)} %join.1.after_ref.loaded_ref.refs_0_), channel_id=1, source_target_pairs={{0,2},{1,5},{2,0},{3,7},{4,6},{5,1},{6,4},{7,3},{8,10},{9,13},{10,... | collective-permute-start | bytes 350216 | tf_op jit(solution)/shard_map/ppermute | solution.py:30
  10.7 1.6 %collective-permute-start.2 = (bf16[8,7296]{1,0:T(8,128)(2,1)S(1)}, bf16[8,7296]{1,0:T(8,128)(2,1)S(1)}, u32[]{:S(2)}, u32[]{:S(2)}) collective-permute-start(bf16[8,7296]{1,0:T(8,128)(2,1)S(1)} %join.1.after_ref.loaded_ref.refs_0_), channel_id=1, source_target_pairs={{0,4},{1,3},{2,6},{3,1},{4,0},{5,7},{6,2},{7,5},{8,12},{9,11},{10,... | collective-permute-start | bytes 350216 | tf_op jit(solution)/shard_map/ppermute | solution.py:30
  12.2 1.1 %attention.1 = bf16[1,128,512]{2,1,0:T(8,128)(2,1)S(1)} custom-call(bf16[8,7296]{1,0:T(8,128)(2,1)S(1)} %join.1.after_ref.loaded_ref.refs_0_, s32[1]{0:T(128)S(6)} %copy.13.lengths_ref, bf16[1,576,128]{2,1,0:T(8,128)(2,1)S(1)} %bitcast.9, bf16[1,576,1280]{2,1,0:T(8,128)(2,1)S(1)} %bitcast.7), custom_call_target="tpu_custom_call" | custom-call | flops 360000000 | bytes 1700000 | tf_op jit(solution)/shard_map/attention/pallas_call | solution.py:125
  13.4 2.0 %collective-permute-done.4 = bf16[4,7296]{1,0:T(4,128)(2,1)S(1)} collective-permute-done((bf16[4,7296]{1,0:T(4,128)(2,1)S(1)}, bf16[4,7296]{1,0:T(4,128)(2,1)S(1)}, u32[]{:S(2)}, u32[]{:S(2)}) %collective-permute-start.4) | collective-permute-done | bytes 58400 | tf_op jit(solution)/shard_map/ppermute | solution.py:30
  15.4 0.1 pad_maximum_fusion.refs_3_
  15.5 0.1 collective-permute-start.8
  15.6 0.5 %collective-permute-start.6 = (bf16[8,7296]{1,0:T(8,128)(2,1)S(1)}, bf16[8,7296]{1,0:T(8,128)(2,1)S(1)}, u32[]{:S(2)}, u32[]{:S(2)}) collective-permute-start(bf16[8,7296]{1,0:T(8,128)(2,1)S(1)} %collective-permute-done.1.refs_1_), channel_id=1, source_target_pairs={{0,1},{1,0},{2,3},{3,2},{4,5},{5,4},{6,7},{7,6},{8,9},{9,8},{10,11... | collective-permute-start | bytes 350216 | tf_op jit(solution)/shard_map/ppermute | solution.py:30
  16.1 0.1 collective-permute-start.7
  16.2 0.7 %collective-permute-done.8.refs_7_ = bf16[8,7296]{1,0:T(8,128)(2,1)S(1)} collective-permute-done((bf16[8,7296]{1,0:T(8,128)(2,1)S(1)}, bf16[8,7296]{1,0:T(8,128)(2,1)S(1)}, u32[]{:S(2)}, u32[]{:S(2)}) %collective-permute-start.8) | collective-permute-done | bytes 116768 | tf_op jit(solution)/shard_map/ppermute | solution.py:30
  16.9 0.2 collective-permute-done.6.refs_5_
  17.1 0.4 %collective-permute-done.7.refs_6_ = bf16[8,7296]{1,0:T(8,128)(2,1)S(1)} collective-permute-done((bf16[8,7296]{1,0:T(8,128)(2,1)S(1)}, bf16[8,7296]{1,0:T(8,128)(2,1)S(1)}, u32[]{:S(2)}, u32[]{:S(2)}) %collective-permute-start.7) | collective-permute-done | bytes 116768 | tf_op jit(solution)/shard_map/ppermute | solution.py:30
  17.4 1.9 %experts.1 = (f32[8,7168]{1,0:T(8,128)S(1)}, f32[8,7168]{1,0:T(8,128)S(1)}, f32[8,7168]{1,0:T(8,128)S(1)}, f32[8,7168]{1,0:T(8,128)S(1)}, bf16[8,7168]{1,0:T(8,1...) custom-call(bf16[8,7296]{1,0:T(8,128)(2,1)S(1)} %join.1.after_ref.loaded_ref.ref, ...), custom_call_target="tpu_custom_call" | custom-call | flops 2000000000 | bytes 500000 | tf_op jit(solution)/shard_map/experts/pallas_call | solution.py:189
  19.3 0.2 collective-permute-start.10
  19.5 0.4 %collective-permute-start.14 = (bf16[8,7168]{1,0:T(8,128)(2,1)S(1)}, bf16[8,7168]{1,0:T(8,128)(2,1)S(1)}, u32[]{:S(2)}, u32[]{:S(2)}) collective-permute-start(bf16[8,7168]{1,0:T(8,128)(2,1)S(1)} %get-tuple-element.22), channel_id=1, source_target_pairs={{0,1},{1,0},{2,3},{3,2},{4,5},{5,4},{6,7},{7,6},{8,9},{9,8},{10,11... | collective-permute-start | bytes 344072 | tf_op jit(solution)/shard_map/ppermute | solution.py:30
  19.9 0.2 collective-permute-start.12
  20.0 0.4 %collective-permute-start.9 = (bf16[8,7168]{1,0:T(8,128)(2,1)S(1)}, bf16[8,7168]{1,0:T(8,128)(2,1)S(1)}, u32[]{:S(2)}, u32[]{:S(2)}) collective-permute-start(bf16[8,7168]{1,0:T(8,128)(2,1)S(1)} %get-tuple-element.16), channel_id=1, source_target_pairs={{0,1},{1,0},{2,3},{3,2},{4,5},{5,4},{6,7},{7,6},{8,9},{9,8},{10,11... | collective-permute-start | bytes 344072 | tf_op jit(solution)/shard_map/ppermute | solution.py:30
  20.4 0.3 collective-permute-done.10
  20.7 0.7 %collective-permute-start.11 = (bf16[8,7168]{1,0:T(8,128)(2,1)S(1)}, bf16[8,7168]{1,0:T(8,128)(2,1)S(1)}, u32[]{:S(2)}, u32[]{:S(2)}) collective-permute-start(bf16[8,7168]{1,0:T(8,128)(2,1)S(1)} %add_convert_fusion.2), channel_id=1, source_target_pairs={{0,2},{1,5},{2,0},{3,7},{4,6},{5,1},{6,4},{7,3},{8,10},{9,13},{10,... | collective-permute-start | bytes 344072 | tf_op jit(solution)/shard_map/ppermute | solution.py:30
  21.5 0.8 %collective-permute-start.13 = (bf16[8,7168]{1,0:T(8,128)(2,1)S(1)}, bf16[8,7168]{1,0:T(8,128)(2,1)S(1)}, u32[]{:S(2)}, u32[]{:S(2)}) collective-permute-start(bf16[8,7168]{1,0:T(8,128)(2,1)S(1)} %add_convert_fusion.1), channel_id=1, source_target_pairs={{0,4},{1,3},{2,6},{3,1},{4,0},{5,7},{6,2},{7,5},{8,12},{9,11},{10,... | collective-permute-start | bytes 344072 | tf_op jit(solution)/shard_map/ppermute | solution.py:30
  22.3 2.2 %collective-permute-start.16 = (bf16[4,7168]{1,0:T(4,128)(2,1)S(1)}, bf16[4,7168]{1,0:T(4,128)(2,1)S(1)}, u32[]{:S(2)}, u32[]{:S(2)}) collective-permute-start(bf16[4,7168]{1,0:T(4,128)(2,1)S(1)} %get-tuple-element.27), channel_id=1, source_target_pairs={{0,6},{1,7},{2,4},{3,5},{4,2},{5,3},{6,0},{7,1},{8,14},{9,15},{10,... | collective-permute-start | bytes 172040 | tf_op jit(solution)/shard_map/ppermute | solution.py:30
  24.5 0.9 %copy.12 = bf16[1,1,128,512]{3,1,2,0:T(2,128)(2,1)} copy(bf16[1,1,128,512]{3,2,1,0:T(8,128)(2,1)S(1)} %bitcast.8) | data formatting | bytes 262144
  25.4 0.8 %collective-permute-start.15 = (bf16[4,7168]{1,0:T(4,128)(2,1)S(1)}, bf16[4,7168]{1,0:T(4,128)(2,1)S(1)}, u32[]{:S(2)}, u32[]{:S(2)}) collective-permute-start(bf16[4,7168]{1,0:T(4,128)(2,1)S(1)} %get-tuple-element.26), channel_id=1, source_target_pairs={{0,6},{1,7},{2,4},{3,5},{4,2},{5,3},{6,0},{7,1},{8,14},{9,15},{10,... | collective-permute-start | bytes 172040 | tf_op jit(solution)/shard_map/ppermute | solution.py:30
  26.2 1.8 %collective-permute-done.16 = bf16[4,7168]{1,0:T(4,128)(2,1)S(1)} collective-permute-done((bf16[4,7168]{1,0:T(4,128)(2,1)S(1)}, bf16[4,7168]{1,0:T(4,128)(2,1)S(1)}, u32[]{:S(2)}, u32[]{:S(2)}) %collective-permute-start.16) | collective-permute-done | bytes 57376 | tf_op jit(solution)/shard_map/ppermute | solution.py:30
  28.0 0.1 convert_add_fusion
  28.1 3.2 %collective-permute-start.17 = (bf16[4,7168]{1,0:T(4,128)(2,1)S(1)}, bf16[4,7168]{1,0:T(4,128)(2,1)S(1)}, u32[]{:S(2)}, u32[]{:S(2)}) collective-permute-start(bf16[4,7168]{1,0:T(4,128)(2,1)S(1)} %fusion), channel_id=1, source_target_pairs={{0,8},{1,9},{2,10},{3,11},{4,12},{5,13},{6,14},{7,15},{8,0},{9,1},... | collective-permute-start | bytes 172040 | tf_op jit(solution)/shard_map/ppermute | solution.py:30
  31.3 2.2 %collective-permute-done.17 = bf16[4,7168]{1,0:T(4,128)(2,1)S(1)} collective-permute-done((bf16[4,7168]{1,0:T(4,128)(2,1)S(1)}, bf16[4,7168]{1,0:T(4,128)(2,1)S(1)}, u32[]{:S(2)}, u32[]{:S(2)}) %collective-permute-start.17) | collective-permute-done | bytes 57376 | tf_op jit(solution)/shard_map/ppermute | solution.py:30
  33.5 0.7 %fusion.2 = bf16[4,7168]{1,0:T(4,128)(2,1)} fusion(f32[8,7168]{1,0:T(8,128)S(1)} %convert_add_fusion, bf16[4,7168]{1,0:T(4,128)(2,1)S(1)} %collective-permute-done.17, bf16[4,7168]{1,0:T(4,128)(2,1)S(1)} %collective-permute-done.15), kind=kLoop, calls=%fused_computation.9 | loop fusion | flops 143360 | bytes 286720 | tf_op jit(solution)/shard_map/convert_element_type | solution.py:241
  (29 shorter events, 0.3 us)
Async XLA Ops:
  1.5 7.3 %collective-permute-start = (bf16[4,7296]{1,0:T(4,128)(2,1)S(1)}, bf16[4,7296]{1,0:T(4,128)(2,1)S(1)}, u32[]{:S(2)}, u32[]{:S(2)}) collective-permute-start(bf16[4,7296]{1,0:T(4,128)(2,1)S(1)} %pack.1.upper_ref), channel_id=1, source_target_pairs={{0,8},{1,9},{2,10},{3,11},{4,12},{5,13},{6,14},{7,15},{8,0},{9,1},... | collective-permute-start | bytes 175112 | tf_op jit(solution)/shard_map/ppermute | solution.py:30
  5.6 7.8 %collective-permute-start.3 = (bf16[4,7296]{1,0:T(4,128)(2,1)S(1)}, bf16[4,7296]{1,0:T(4,128)(2,1)S(1)}, u32[]{:S(2)}, u32[]{:S(2)}) collective-permute-start(bf16[4,7296]{1,0:T(4,128)(2,1)S(1)} %pack.1.upper_ref), channel_id=1, source_target_pairs={{0,6},{1,7},{2,4},{3,5},{4,2},{5,3},{6,0},{7,1},{8,14},{9,15},{10,... | collective-permute-start | bytes 175112 | tf_op jit(solution)/shard_map/ppermute | solution.py:30
  8.1 7.3 %collective-permute-start.4 = (bf16[4,7296]{1,0:T(4,128)(2,1)S(1)}, bf16[4,7296]{1,0:T(4,128)(2,1)S(1)}, u32[]{:S(2)}, u32[]{:S(2)}) collective-permute-start(bf16[4,7296]{1,0:T(4,128)(2,1)S(1)} %pack.1.upper_ref), channel_id=1, source_target_pairs={{0,14},{1,15},{2,12},{3,13},{4,10},{5,11},{6,8},{7,9},{8,6},{9,7},... | collective-permute-start | bytes 175112 | tf_op jit(solution)/shard_map/ppermute | solution.py:30
  8.8 3.5 %copy-start.3 = (bf16[1,1280,576]{1,2,0:T(8,128)(2,1)S(1)}, bf16[1,1280,576]{1,2,0:T(8,128)(2,1)}, u32[]{:S(2)}) copy-start(bf16[1,1280,576]{1,2,0:T(8,128)(2,1)} %param.18) | copy-start | bytes 4423684
  8.8 3.4 %copy-start.4 = (bf16[1,128,576]{1,2,0:T(8,128)(2,1)S(1)}, bf16[1,128,576]{1,2,0:T(8,128)(2,1)}, u32[]{:S(2)}) copy-start(bf16[1,128,576]{1,2,0:T(8,128)(2,1)} %param.17) | copy-start | bytes 442372
  8.8 8.6 %copy-start.5 = (bf16[7168]{0:T(1024)(128)(2,1)S(1)}, bf16[7168]{0:T(1024)(128)(2,1)}, u32[]{:S(2)}) copy-start(bf16[7168]{0:T(1024)(128)(2,1)} %param.13) | copy-start | bytes 43012
  8.8 8.6 %copy-start = (bf16[1,7168,256]{2,1,0:T(8,128)(2,1)S(1)}, bf16[1,7168,256]{2,1,0:T(8,128)(2,1)}, u32[]{:S(2)}) copy-start(bf16[1,7168,256]{2,1,0:T(8,128)(2,1)} %refs_9_.1) | copy-start | bytes 11010052
  8.8 8.6 %copy-start.1 = (bf16[1,7168,256]{2,1,0:T(8,128)(2,1)S(1)}, bf16[1,7168,256]{2,1,0:T(8,128)(2,1)}, u32[]{:S(2)}) copy-start(bf16[1,7168,256]{2,1,0:T(8,128)(2,1)} %refs_10_.1) | copy-start | bytes 11010052
  8.9 8.6 %copy-start.2 = (bf16[1,256,7168]{2,1,0:T(8,128)(2,1)S(1)}, bf16[1,256,7168]{2,1,0:T(8,128)(2,1)}, u32[]{:S(2)}) copy-start(bf16[1,256,7168]{2,1,0:T(8,128)(2,1)} %refs_11_.1) | copy-start | bytes 11010052
  8.9 6.7 %collective-permute-start.1 = (bf16[8,7296]{1,0:T(8,128)(2,1)S(1)}, bf16[8,7296]{1,0:T(8,128)(2,1)S(1)}, u32[]{:S(2)}, u32[]{:S(2)}) collective-permute-start(bf16[8,7296]{1,0:T(8,128)(2,1)S(1)} %join.1.after_ref.loaded_ref.refs_0_), channel_id=1, source_target_pairs={{0,2},{1,5},{2,0},{3,7},{4,6},{5,1},{6,4},{7,3},{8,10},{9,13},{10,... | collective-permute-start | bytes 350216 | tf_op jit(solution)/shard_map/ppermute | solution.py:30
  10.7 5.4 %collective-permute-start.2 = (bf16[8,7296]{1,0:T(8,128)(2,1)S(1)}, bf16[8,7296]{1,0:T(8,128)(2,1)S(1)}, u32[]{:S(2)}, u32[]{:S(2)}) collective-permute-start(bf16[8,7296]{1,0:T(8,128)(2,1)S(1)} %join.1.after_ref.loaded_ref.refs_0_), channel_id=1, source_target_pairs={{0,4},{1,3},{2,6},{3,1},{4,0},{5,7},{6,2},{7,5},{8,12},{9,11},{10,... | collective-permute-start | bytes 350216 | tf_op jit(solution)/shard_map/ppermute | solution.py:30
  12.2 4.7 %collective-permute-start.5 = (bf16[8,7296]{1,0:T(8,128)(2,1)S(1)}, bf16[8,7296]{1,0:T(8,128)(2,1)S(1)}, u32[]{:S(2)}, u32[]{:S(2)}) collective-permute-start(bf16[8,7296]{1,0:T(8,128)(2,1)S(1)} %join.1.after_ref.loaded_ref.refs_0_), channel_id=1, source_target_pairs={{0,1},{1,0},{2,3},{3,2},{4,5},{5,4},{6,7},{7,6},{8,9},{9,8},{10,11... | collective-permute-start | bytes 350216 | tf_op jit(solution)/shard_map/ppermute | solution.py:30
  15.5 1.4 %collective-permute-start.8 = (bf16[8,7296]{1,0:T(8,128)(2,1)S(1)}, bf16[8,7296]{1,0:T(8,128)(2,1)S(1)}, u32[]{:S(2)}, u32[]{:S(2)}) collective-permute-start(bf16[8,7296]{1,0:T(8,128)(2,1)S(1)} %pad_maximum_fusion.refs_3_), channel_id=1, source_target_pairs={{0,1},{1,0},{2,3},{3,2},{4,5},{5,4},{6,7},{7,6},{8,9},{9,8},{10,11... | collective-permute-start | bytes 350216 | tf_op jit(solution)/shard_map/ppermute | solution.py:30
  15.6 1.5 %collective-permute-start.6 = (bf16[8,7296]{1,0:T(8,128)(2,1)S(1)}, bf16[8,7296]{1,0:T(8,128)(2,1)S(1)}, u32[]{:S(2)}, u32[]{:S(2)}) collective-permute-start(bf16[8,7296]{1,0:T(8,128)(2,1)S(1)} %collective-permute-done.1.refs_1_), channel_id=1, source_target_pairs={{0,1},{1,0},{2,3},{3,2},{4,5},{5,4},{6,7},{7,6},{8,9},{9,8},{10,11... | collective-permute-start | bytes 350216 | tf_op jit(solution)/shard_map/ppermute | solution.py:30
  16.1 1.3 %collective-permute-start.7 = (bf16[8,7296]{1,0:T(8,128)(2,1)S(1)}, bf16[8,7296]{1,0:T(8,128)(2,1)S(1)}, u32[]{:S(2)}, u32[]{:S(2)}) collective-permute-start(bf16[8,7296]{1,0:T(8,128)(2,1)S(1)} %collective-permute-done.2.refs_2_), channel_id=1, source_target_pairs={{0,1},{1,0},{2,3},{3,2},{4,5},{5,4},{6,7},{7,6},{8,9},{9,8},{10,11... | collective-permute-start | bytes 350216 | tf_op jit(solution)/shard_map/ppermute | solution.py:30
  19.3 1.4 %collective-permute-start.10 = (bf16[8,7168]{1,0:T(8,128)(2,1)S(1)}, bf16[8,7168]{1,0:T(8,128)(2,1)S(1)}, u32[]{:S(2)}, u32[]{:S(2)}) collective-permute-start(bf16[8,7168]{1,0:T(8,128)(2,1)S(1)} %get-tuple-element.18), channel_id=1, source_target_pairs={{0,1},{1,0},{2,3},{3,2},{4,5},{5,4},{6,7},{7,6},{8,9},{9,8},{10,11... | collective-permute-start | bytes 344072 | tf_op jit(solution)/shard_map/ppermute | solution.py:30
  19.5 2.7 %collective-permute-start.14 = (bf16[8,7168]{1,0:T(8,128)(2,1)S(1)}, bf16[8,7168]{1,0:T(8,128)(2,1)S(1)}, u32[]{:S(2)}, u32[]{:S(2)}) collective-permute-start(bf16[8,7168]{1,0:T(8,128)(2,1)S(1)} %get-tuple-element.22), channel_id=1, source_target_pairs={{0,1},{1,0},{2,3},{3,2},{4,5},{5,4},{6,7},{7,6},{8,9},{9,8},{10,11... | collective-permute-start | bytes 344072 | tf_op jit(solution)/shard_map/ppermute | solution.py:30
  19.9 1.6 %collective-permute-start.12 = (bf16[8,7168]{1,0:T(8,128)(2,1)S(1)}, bf16[8,7168]{1,0:T(8,128)(2,1)S(1)}, u32[]{:S(2)}, u32[]{:S(2)}) collective-permute-start(bf16[8,7168]{1,0:T(8,128)(2,1)S(1)} %get-tuple-element.20), channel_id=1, source_target_pairs={{0,1},{1,0},{2,3},{3,2},{4,5},{5,4},{6,7},{7,6},{8,9},{9,8},{10,11... | collective-permute-start | bytes 344072 | tf_op jit(solution)/shard_map/ppermute | solution.py:30
  20.0 8.0 %collective-permute-start.9 = (bf16[8,7168]{1,0:T(8,128)(2,1)S(1)}, bf16[8,7168]{1,0:T(8,128)(2,1)S(1)}, u32[]{:S(2)}, u32[]{:S(2)}) collective-permute-start(bf16[8,7168]{1,0:T(8,128)(2,1)S(1)} %get-tuple-element.16), channel_id=1, source_target_pairs={{0,1},{1,0},{2,3},{3,2},{4,5},{5,4},{6,7},{7,6},{8,9},{9,8},{10,11... | collective-permute-start | bytes 344072 | tf_op jit(solution)/shard_map/ppermute | solution.py:30
  20.7 7.3 %collective-permute-start.11 = (bf16[8,7168]{1,0:T(8,128)(2,1)S(1)}, bf16[8,7168]{1,0:T(8,128)(2,1)S(1)}, u32[]{:S(2)}, u32[]{:S(2)}) collective-permute-start(bf16[8,7168]{1,0:T(8,128)(2,1)S(1)} %add_convert_fusion.2), channel_id=1, source_target_pairs={{0,2},{1,5},{2,0},{3,7},{4,6},{5,1},{6,4},{7,3},{8,10},{9,13},{10,... | collective-permute-start | bytes 344072 | tf_op jit(solution)/shard_map/ppermute | solution.py:30
  21.5 6.5 %collective-permute-start.13 = (bf16[8,7168]{1,0:T(8,128)(2,1)S(1)}, bf16[8,7168]{1,0:T(8,128)(2,1)S(1)}, u32[]{:S(2)}, u32[]{:S(2)}) collective-permute-start(bf16[8,7168]{1,0:T(8,128)(2,1)S(1)} %add_convert_fusion.1), channel_id=1, source_target_pairs={{0,4},{1,3},{2,6},{3,1},{4,0},{5,7},{6,2},{7,5},{8,12},{9,11},{10,... | collective-permute-start | bytes 344072 | tf_op jit(solution)/shard_map/ppermute | solution.py:30
  22.3 5.6 %collective-permute-start.16 = (bf16[4,7168]{1,0:T(4,128)(2,1)S(1)}, bf16[4,7168]{1,0:T(4,128)(2,1)S(1)}, u32[]{:S(2)}, u32[]{:S(2)}) collective-permute-start(bf16[4,7168]{1,0:T(4,128)(2,1)S(1)} %get-tuple-element.27), channel_id=1, source_target_pairs={{0,6},{1,7},{2,4},{3,5},{4,2},{5,3},{6,0},{7,1},{8,14},{9,15},{10,... | collective-permute-start | bytes 172040 | tf_op jit(solution)/shard_map/ppermute | solution.py:30
  25.4 5.9 %collective-permute-start.15 = (bf16[4,7168]{1,0:T(4,128)(2,1)S(1)}, bf16[4,7168]{1,0:T(4,128)(2,1)S(1)}, u32[]{:S(2)}, u32[]{:S(2)}) collective-permute-start(bf16[4,7168]{1,0:T(4,128)(2,1)S(1)} %get-tuple-element.26), channel_id=1, source_target_pairs={{0,6},{1,7},{2,4},{3,5},{4,2},{5,3},{6,0},{7,1},{8,14},{9,15},{10,... | collective-permute-start | bytes 172040 | tf_op jit(solution)/shard_map/ppermute | solution.py:30
  28.1 5.4 %collective-permute-start.17 = (bf16[4,7168]{1,0:T(4,128)(2,1)S(1)}, bf16[4,7168]{1,0:T(4,128)(2,1)S(1)}, u32[]{:S(2)}, u32[]{:S(2)}) collective-permute-start(bf16[4,7168]{1,0:T(4,128)(2,1)S(1)} %fusion), channel_id=1, source_target_pairs={{0,8},{1,9},{2,10},{3,11},{4,12},{5,13},{6,14},{7,15},{8,0},{9,1},... | collective-permute-start | bytes 172040 | tf_op jit(solution)/shard_map/ppermute | solution.py:30
